TPU v7x, 512 devices: a whole 4x8x8 slice. The times are simulated.
512 devices in a mesh: fsdp: 32 (over z_hi, y, core), rep: 16 (over z_lo, x).
Axes of the slice: x: 4, y: 8, z: 8 (z_hi: 2, z_lo: 4; z = z_hi * 4 + z_lo), core: 2. Of those that a mesh axis runs over, the one named last changes fastest.
Arguments:
- student_global: bfloat16 [512, 257, 768], P(('fsdp', 'rep')), may hold values from -24 to 24
- student_local: bfloat16 [1024, 37, 768], P(('fsdp', 'rep')), may hold values from -6 to 6
- teacher_global: bfloat16 [512, 257, 768], P(('fsdp', 'rep')), may hold values from -6 to 6
- grad_global: bfloat16 [512, 257, 768], P(('fsdp', 'rep')), may hold values from -6 to 6
- grad_local: bfloat16 [1024, 37, 768], P(('fsdp', 'rep')), may hold values from -6 to 6
- student_qkv: float32 [768, 2304], P('fsdp'), may hold values from -0.21875 to 0.21875
- teacher_qkv: float32 [768, 2304], P('fsdp'), may hold values from -0.21875 to 0.21875
- first_moment: float32 [768, 2304], P('fsdp'), may hold values from -1 to 1
- second_moment: float32 [768, 2304], P('fsdp'), may hold values from 1e-05 to 0.002
Outputs:
- student_out_global: bfloat16 [512, 257, 768], P(('fsdp', 'rep'))
- student_out_local: bfloat16 [1024, 37, 768], P(('fsdp', 'rep'))
- teacher_out: bfloat16 [512, 257, 768], P(('fsdp', 'rep'))
- back_global: bfloat16 [512, 257, 768], P(('fsdp', 'rep'))
- back_local: bfloat16 [1024, 37, 768], P(('fsdp', 'rep'))
- new_student: float32 [768, 2304], P('fsdp')
- new_teacher: float32 [768, 2304], P('fsdp')
- new_first: float32 [768, 2304], P('fsdp')
- new_second: float32 [768, 2304], P('fsdp')
All inputs are finite; a program needn't handle non-finite values.
Results may differ from a plain program's by a relative error of at most 0.017.
Values may be sent and summed in bfloat16 or wider, within the bound.
No kernel may reach another device: no remote copies, remote signals or barrier semaphores. Data moves between devices by JAX's collectives and lax.ppermute only.
A program may use at most 64 MiB of HBM per device.

v0:
```python
import jax
import jax.numpy as jnp
from jax import lax
from jax.sharding import PartitionSpec as P

HEADS = 12
HEAD_DIM = 64


norm_eps = 1e-06
beta_one = 0.9
beta_two = 0.999
corr_one = 1.0 - 0.9**10
corr_two = 1.0 - 0.999**10
learn_rate = 0.002
decay_rate = 0.04
momentum = 0.994
adam_eps = 1e-08


def attend(crops, weight):
    crop_count, length, feature = crops.shape
    inputs = crops.astype(jnp.float32)
    average = jnp.mean(inputs, axis=-1, keepdims=True)
    centred = inputs - average
    variance = jnp.mean(centred * centred, axis=-1, keepdims=True)
    normed = (centred * lax.rsqrt(variance + norm_eps)).astype(jnp.bfloat16)
    projected = jnp.dot(
        normed.reshape(crop_count * length, feature), weight, preferred_element_type=jnp.float32
    )
    projected = projected.astype(jnp.bfloat16).reshape(crop_count, length, 3, HEADS, HEAD_DIM)
    queries = projected[:, :, 0]
    key_rows = projected[:, :, 1]
    value_rows = projected[:, :, 2]
    scores = jnp.einsum(
        "nqhe,nkhe->nhqk", queries, key_rows, preferred_element_type=jnp.float32
    ) * HEAD_DIM ** (-0.5)
    exponent = jnp.exp(scores)
    probability = (exponent / jnp.sum(exponent, axis=-1, keepdims=True)).astype(jnp.bfloat16)
    heads_out = jnp.einsum(
        "nhqk,nkhe->nqhe", probability, value_rows, preferred_element_type=jnp.float32
    )
    return heads_out.reshape(crop_count, length, HEADS * HEAD_DIM)


def adam_update(weight, teacher, first, second, gradient):
    first = beta_one * first + (1.0 - beta_one) * gradient
    second = beta_two * second + (1.0 - beta_two) * gradient * gradient
    update = first / corr_one / (jnp.sqrt(second / corr_two) + adam_eps)
    weight_new = weight - learn_rate * (update + decay_rate * weight)
    teacher_new = momentum * teacher + (1.0 - momentum) * weight_new
    return (weight_new, teacher_new, first, second)


def on_device(
    student_global,
    student_local,
    teacher_global,
    grad_global,
    grad_local,
    student_qkv,
    teacher_qkv,
    first_moment,
    second_moment,
):
    student_half = student_qkv.astype(jnp.bfloat16)
    teacher_half = teacher_qkv.astype(jnp.bfloat16)
    student_full = lax.all_gather(student_half, "fsdp", axis=0, tiled=True)
    teacher_full = lax.all_gather(teacher_half, "fsdp", axis=0, tiled=True)

    def forward(global_in, local_in, weight_in):
        return (attend(global_in, weight_in), attend(local_in, weight_in))

    results, pullback = jax.vjp(forward, student_global, student_local, student_full)
    back_g, back_l, weight_term = pullback(
        (grad_global.astype(jnp.float32), grad_local.astype(jnp.float32))
    )
    teacher_rows = attend(teacher_global, teacher_full).astype(jnp.bfloat16)
    token_total = (
        (
            student_global.shape[0] * student_global.shape[1]
            + student_local.shape[0] * student_local.shape[1]
        )
        * lax.axis_size("fsdp")
        * lax.axis_size("rep")
    )
    grad_scale = 1.0 / jnp.sqrt(jnp.float32(token_total))
    row_share = lax.psum_scatter(weight_term, "fsdp", scatter_dimension=0, tiled=True).astype(
        jnp.float32
    )
    gradient = lax.psum(row_share.astype(jnp.bfloat16), "rep").astype(jnp.float32) * grad_scale
    new_student, new_teacher, new_first, new_second = adam_update(
        student_qkv, teacher_qkv, first_moment, second_moment, gradient
    )
    return (
        results[0].astype(jnp.bfloat16),
        results[1].astype(jnp.bfloat16),
        teacher_rows,
        back_g,
        back_l,
        new_student,
        new_teacher,
        new_first,
        new_second,
    )


def solution(mesh):
    return jax.shard_map(
        on_device,
        mesh=mesh,
        in_specs=(
            P(("fsdp", "rep"), None, None),
            P(("fsdp", "rep"), None, None),
            P(("fsdp", "rep"), None, None),
            P(("fsdp", "rep"), None, None),
            P(("fsdp", "rep"), None, None),
            P("fsdp", None),
            P("fsdp", None),
            P("fsdp", None),
            P("fsdp", None),
        ),
        out_specs=(
            P(("fsdp", "rep"), None, None),
            P(("fsdp", "rep"), None, None),
            P(("fsdp", "rep"), None, None),
            P(("fsdp", "rep"), None, None),
            P(("fsdp", "rep"), None, None),
            P("fsdp", None),
            P("fsdp", None),
            P("fsdp", None),
            P("fsdp", None),
        ),
        check_vma=False,
    )
```

profile of v0, /device:TPU:1, one launch (start us, length us, event | category | flops | bytes accessed | tf_op | source)
XLA Modules:
  0.0 574.4 jit_solution(15887253723977354695)
XLA Ops:
  7.2 0.0 all-gather.3.cloned.1.call-start
  7.2 1.6 convert_element_type.200
  8.8 0.0 reduce-scatter.2.cloned.1.call-start
  8.9 1.0 convert_reduce_fusion.2
  9.9 1.1 fusion.47
  11.0 0.5 copy-done.28
  11.5 0.6 copy-done.26
  12.1 1.0 fusion.48
  13.1 1.2 reshape.310
  14.4 2.2 copy.50
  16.6 1.2 convert_reduce_fusion.1
  17.8 1.3 fusion.31
  19.1 0.6 fusion.56
  19.7 101.4 %all-gather.3.cloned.1.call-done = bf16[768,2304]{1,0:T(8,128)(2,1)} async-done(((bf16[24,2304]{1,0:T(8,128)(2,1)}), bf16[768,2304]{1,0:T(8,128)(2,1)}) %all-gather.3.cloned.1.call-update) | async-done | bytes 3538960 | tf_op jit(solution)/shard_map/all_gather | solution.py:68
  121.1 2.7 convolution_convert_fusion.4
  123.8 0.5 reshape.301
  124.4 0.2 fusion.68
  124.6 0.3 fusion.69
  124.9 1.0 fusion.19
  125.9 1.4 fusion.37
  127.4 1.1 fusion.21
  128.4 1.0 fusion.20
  129.5 2.2 convolution_convert_fusion.3
  131.7 2.6 copy.40
  134.3 2.5 fusion.9
  136.8 3.0 fusion.6
  139.8 2.4 fusion.14
  142.3 2.4 fusion.13
  144.7 0.2 pad_add_fusion.1
  144.9 1.1 copy.57
  146.0 2.5 reshape.311
  148.5 2.9 fusion.15
  151.4 0.4 pad_add_fusion
  151.9 2.2 convolution_convert_fusion.1
  154.1 2.9 fusion.7
  157.0 0.0 reduce-scatter.2.cloned.1.call-update
  157.0 0.0 all-reduce.8.cloned.1.call-start
  157.1 134.7 %reduce-scatter.2.cloned.1.call-done = bf16[24,2304]{1,0:T(8,128)(2,1)} async-done(((bf16[768,2304]{1,0:T(8,128)(2,1)}), bf16[24,2304]{1,0:T(8,128)(2,1)}) %reduce-scatter.2.cloned.1.call-update) | async-done | bytes 110608 | tf_op jit(solution)/shard_map/reduce_scatter | solution.py:88
  291.8 0.3 all-gather.5.cloned.1.call-start
  292.0 152.6 %all-reduce.8.cloned.1.call-done = bf16[24,2304]{1,0:T(8,128)(2,1)} async-done(((bf16[24,2304]{1,0:T(8,128)(2,1)}), bf16[24,2304]{1,0:T(8,128)(2,1)}) %all-reduce.8.cloned.1.call-update) | async-done | bytes 110608 | tf_op jit(solution)/shard_map/psum | solution.py:91
  444.6 2.4 multiply_add_fusion
  447.0 1.2 convert_reduce_fusion
  448.2 1.3 fusion.29
  449.5 0.6 add_rsqrt_fusion
  450.1 1.5 fusion.18
  451.6 0.8 copy.47
  452.4 1.9 convert_element_type.213
  454.2 2.9 fusion.22
  457.1 1.7 reshape.312
  458.8 1.2 fusion.49
  460.0 1.2 fusion.55
  461.2 1.2 add_convert_fusion.1
  462.4 0.7 copy.60
  463.2 3.4 convolution_convert_fusion.9
  466.5 2.0 copy.58
  468.6 3.3 fusion.33
  471.9 0.4 fusion.67
  472.3 0.9 add_convert_fusion
  473.2 87.2 %all-gather.5.cloned.1.call-done = bf16[768,2304]{1,0:T(8,128)(2,1)} async-done(((bf16[24,2304]{1,0:T(8,128)(2,1)}), bf16[768,2304]{1,0:T(8,128)(2,1)}) %all-gather.5.cloned.1.call-update) | async-done | bytes 3538960 | tf_op jit(solution)/shard_map/all_gather | solution.py:69
  560.4 3.3 convolution_convert_fusion.2
  563.7 1.0 copy.48
  564.7 1.1 fusion.8
  565.8 1.1 fusion.11
  566.8 1.0 copy.59
  (86 shorter events, 0.3 us)
Async XLA Ops:
  7.2 113.9 %all-gather.3.cloned.1.call-start = ((), (), s32[]{:S(2)}) async-start(), calls=%async_computation.1 | async-start | bytes 3649536 | tf_op jit(solution)/shard_map/all_gather | solution.py:68
  8.8 282.9 %reduce-scatter.2.cloned.1.call-start = ((), (), s32[]{:S(2)}) async-start(), calls=%async_computation.3 | async-start | bytes 3649536 | tf_op jit(solution)/shard_map/reduce_scatter | solution.py:88
  9.9 1.1 copy-start.18
  11.0 0.5 copy-start.28
  11.5 0.6 copy-start.26
  13.1 108.0 %copy-start.9 = (bf16[74,768]{1,0:T(8,128)(2,1)}, bf16[74,768]{1,0:T(8,128)(2,1)S(1)}, u32[]{:S(2)}) copy-start(bf16[74,768]{1,0:T(8,128)(2,1)S(1)} %reshape.300) | copy-start | bytes 340996
  14.4 110.5 %copy-start.12 = (bf16[2,37,12,64]{3,2,0,1:T(8,128)(2,1)}, bf16[2,37,12,64]{3,2,0,1:T(8,128)(2,1)S(1)}, u32[]{:S(2)}) copy-start(bf16[2,37,12,64]{3,2,0,1:T(8,128)(2,1)S(1)} %reshape.310) | copy-start | bytes 340996
  17.8 103.3 %copy-start.22 = (f32[257]{0:T(512)}, f32[257]{0:T(512)S(1)}, u32[]{:S(2)}) copy-start(f32[257]{0:T(512)S(1)} %broadcast_multiply_fusion.1) | copy-start | bytes 3088
  19.0 102.0 %copy-start.20 = (f32[257]{0:T(512)}, f32[257]{0:T(512)S(1)}, u32[]{:S(2)}) copy-start(f32[257]{0:T(512)S(1)} %fusion.31) | copy-start | bytes 3088
  124.5 1.4 copy-start.11
  124.9 3.6 copy-start.7
  125.9 3.5 copy-start
  125.9 3.5 copy-start.2
  125.9 3.5 copy-start.23
  125.9 3.5 copy-start.32
  134.3 2.5 copy-start.1
  134.3 2.5 copy-start.6
  142.3 2.4 copy-start.15
  142.3 2.4 copy-start.16
  142.3 2.4 copy-start.17
  148.4 2.9 copy-start.13
  148.5 2.9 copy-start.14
  148.5 3.4 copy-start.3
  148.5 3.4 copy-start.24
  148.5 3.4 copy-start.33
  151.8 2.3 copy-start.8
  151.9 2.3 copy-start.5
  151.9 2.3 copy-start.10
  157.0 287.6 %all-reduce.8.cloned.1.call-start = ((), (), s32[]{:S(2)}) async-start(), calls=%async_computation.4 | async-start | bytes 221184 | tf_op jit(solution)/shard_map/psum | solution.py:91
  291.8 268.6 %all-gather.5.cloned.1.call-start = ((), (), s32[]{:S(2)}) async-start(), calls=%async_computation.2 | async-start | bytes 3649536 | tf_op jit(solution)/shard_map/all_gather | solution.py:69
  448.2 1.3 copy-start.30
  451.6 7.2 %copy-start.19 = (f32[2,37]{1,0:T(2,128)S(1)}, f32[2,37]{1,0:T(2,128)}, u32[]{:S(2)}) copy-start(f32[2,37]{1,0:T(2,128)} %copy-done.18) | copy-start | bytes 892
  451.6 8.4 %copy-start.29 = (f32[2,37]{1,0:T(2,128)S(1)}, f32[2,37]{1,0:T(2,128)}, u32[]{:S(2)}) copy-start(f32[2,37]{1,0:T(2,128)} %copy-done.28) | copy-start | bytes 892
  451.6 8.4 %copy-start.27 = (f32[2,37]{1,0:T(2,128)S(1)}, f32[2,37]{1,0:T(2,128)}, u32[]{:S(2)}) copy-start(f32[2,37]{1,0:T(2,128)} %copy-done.26) | copy-start | bytes 892
  457.1 11.4 %copy-start.25 = (f32[257]{0:T(512)S(1)}, f32[257]{0:T(512)}, u32[]{:S(2)}) copy-start(f32[257]{0:T(512)} %copy-done.22) | copy-start | bytes 3088
  468.5 3.3 copy-start.21
  468.6 3.4 copy-start.4
  468.6 3.4 copy-start.34
  468.6 91.8 %copy-start.31 = (f32[257]{0:T(512)S(1)}, f32[257]{0:T(512)}, u32[]{:S(2)}) copy-start(f32[257]{0:T(512)} %copy-done.30) | copy-start | bytes 3088
  468.6 91.8 %copy-start.35 = (f32[257]{0:T(512)S(1)}, f32[257]{0:T(512)}, u32[]{:S(2)}) copy-start(f32[257]{0:T(512)} %add_rsqrt_fusion) | copy-start | bytes 3088
Sparse Core Ops, SparseCore 0:
  11.8 109.2 all-gather.2
  157.1 134.5 reduce-scatter.1
  294.9 149.6 all-reduce.7
  447.7 112.6 all-gather.4
where the time goes:
time: 575 us; the launch traced here: 574 us
  waiting for transfers between devices  476 us (83%)
  matrix products  44.6 us (8%)
  local copies, waits for them, and re-layouts  20.6 us (4%)
  other arithmetic  18.6 us (3%)
  between operations  14.3 us (2%)
    psum x1, waiting for transfers between devices, on_device(): lax.psum(row_share.astype(jnp.bfloat16), 'rep').astype(jnp.float32)  153 us
    reduce_scatter x1, waiting for transfers between devices, on_device(): lax.psum_scatter(weight_term, 'fsdp', scatter_dimension=0, tiled=True)  135 us
    all_gather x1, waiting for transfers between devices, on_device(): student_full = lax.all_gather(student_half, 'fsdp', axis=0, tiled=True)  101 us
    all_gather x1, waiting for transfers between devices, on_device(): teacher_full = lax.all_gather(teacher_half, 'fsdp', axis=0, tiled=True)  87.2 us
    dot_general x7, matrix products, attend(): jnp.dot(normed.reshape(crop_count * length, feature), weight, preferred_e...  19.6 us
    dot_general x7, matrix products, attend(): jnp.einsum('nhqk,nkhe->nqhe', probability, value_rows, preferred_element_...  14.3 us
  transfers between devices with their start and end apart: 4, of which 4 were waited for; matrix products, arithmetic and copies ran while one was open for 6% of the time, Pallas kernels for 0%

commit v1 on v0

--- a/solution.py
+++ b/solution.py
@@ -1,7 +1,7 @@
 import jax
 import jax.numpy as jnp
 from jax import lax
-from jax.sharding import PartitionSpec as P
+from jax.sharding import Mesh, PartitionSpec as P
 
 HEADS = 12
 HEAD_DIM = 64
@@ -52,6 +52,63 @@
     return (weight_new, teacher_new, first, second)
 
 
+ROWS = 24
+MAIN = 512
+TAIL = 64
+QUARTER = MAIN + TAIL
+AXES = ("zh", "yh", "yl", "c", "zl", "x")
+FSDP = ("zh", "yh", "yl", "c")
+SWAP = [(0, 1), (1, 0)]
+
+
+def own_quarter(half):
+    place = lax.axis_index("x")
+    main = lax.dynamic_slice_in_dim(half, place * MAIN, MAIN, axis=1)
+    tail = lax.dynamic_slice_in_dim(half, 4 * MAIN + place * TAIL, TAIL, axis=1)
+    return jnp.concatenate([main, tail], axis=1)
+
+
+def join_quarters(parts):
+    rows = parts.shape[1]
+    main = parts[:, :, :MAIN].transpose(1, 0, 2).reshape(rows, 4 * MAIN)
+    tail = parts[:, :, MAIN:].transpose(1, 0, 2).reshape(rows, 4 * TAIL)
+    return jnp.concatenate([main, tail], axis=1)
+
+
+def split_quarters(whole):
+    rows = whole.shape[0]
+    main = whole[:, : 4 * MAIN].reshape(rows, 4, MAIN).transpose(1, 0, 2)
+    tail = whole[:, 4 * MAIN :].reshape(rows, 4, TAIL).transpose(1, 0, 2)
+    return jnp.concatenate([main, tail], axis=2)
+
+
+def gather_rows(half):
+    part = own_quarter(half)
+    column = lax.all_to_all(
+        jnp.broadcast_to(part[None], (8, ROWS, QUARTER)), ("zh", "yh"), 0, 0, tiled=True
+    )
+    block = column.reshape(8 * ROWS, QUARTER)
+    own = lax.all_to_all(
+        jnp.broadcast_to(block[None], (8, 8 * ROWS, QUARTER)), ("x", "yl"), 0, 0, tiled=True
+    ).reshape(4, 16 * ROWS, QUARTER)
+    other = lax.ppermute(own, "c", SWAP)
+    return own, other
+
+
+def add_up(own, other):
+    total = own.astype(jnp.float32) + lax.ppermute(other, "c", SWAP).astype(jnp.float32)
+    total = total.astype(jnp.bfloat16).reshape(8, 8 * ROWS, QUARTER)
+    shares = lax.all_to_all(total, ("x", "yl"), 0, 0, tiled=True)
+    total = jnp.sum(shares.astype(jnp.float32), axis=0).astype(jnp.bfloat16)
+    shares = lax.all_to_all(total.reshape(8, ROWS, QUARTER), ("zh", "yh"), 0, 0, tiled=True)
+    total = jnp.sum(shares.astype(jnp.float32), axis=0).astype(jnp.bfloat16)
+    shares = lax.all_to_all(
+        jnp.broadcast_to(total[None], (16, ROWS, QUARTER)), ("zl", "x"), 0, 0, tiled=True
+    )
+    total = jnp.sum(shares.astype(jnp.float32).reshape(4, 4, ROWS, QUARTER), axis=0)
+    return join_quarters(total)
+
+
 def on_device(
     student_global,
     student_local,
@@ -65,8 +122,12 @@
 ):
     student_half = student_qkv.astype(jnp.bfloat16)
     teacher_half = teacher_qkv.astype(jnp.bfloat16)
-    student_full = lax.all_gather(student_half, "fsdp", axis=0, tiled=True)
-    teacher_full = lax.all_gather(teacher_half, "fsdp", axis=0, tiled=True)
+    teacher_full = lax.all_gather(teacher_half, FSDP, axis=0, tiled=True)
+    own, other = gather_rows(student_half)
+    core = lax.axis_index("c")
+    both = jnp.where(core == 0, jnp.stack([own, other]), jnp.stack([other, own]))
+    both = both.reshape(2, 4, 2, 8, ROWS, QUARTER).transpose(1, 3, 2, 0, 4, 5)
+    student_full = join_quarters(both.reshape(4, 32 * ROWS, QUARTER))
 
     def forward(global_in, local_in, weight_in):
         return (attend(global_in, weight_in), attend(local_in, weight_in))
@@ -81,14 +142,12 @@
             student_global.shape[0] * student_global.shape[1]
             + student_local.shape[0] * student_local.shape[1]
         )
-        * lax.axis_size("fsdp")
-        * lax.axis_size("rep")
+        * lax.axis_size(AXES)
     )
     grad_scale = 1.0 / jnp.sqrt(jnp.float32(token_total))
-    row_share = lax.psum_scatter(weight_term, "fsdp", scatter_dimension=0, tiled=True).astype(
-        jnp.float32
-    )
-    gradient = lax.psum(row_share.astype(jnp.bfloat16), "rep").astype(jnp.float32) * grad_scale
+    parts = split_quarters(weight_term).reshape(4, 8, 2, 2, ROWS, QUARTER)
+    parts = parts.transpose(3, 0, 2, 1, 4, 5).reshape(2, 4, 16 * ROWS, QUARTER)
+    gradient = add_up(parts[core], parts[1 - core]) * grad_scale
     new_student, new_teacher, new_first, new_second = adam_update(
         student_qkv, teacher_qkv, first_moment, second_moment, gradient
     )
@@ -106,30 +165,31 @@
 
 
 def solution(mesh):
+    mesh = Mesh(mesh.devices.reshape(2, 4, 2, 2, 4, 4), AXES)
     return jax.shard_map(
         on_device,
         mesh=mesh,
         in_specs=(
-            P(("fsdp", "rep"), None, None),
-            P(("fsdp", "rep"), None, None),
-            P(("fsdp", "rep"), None, None),
-            P(("fsdp", "rep"), None, None),
-            P(("fsdp", "rep"), None, None),
-            P("fsdp", None),
-            P("fsdp", None),
-            P("fsdp", None),
-            P("fsdp", None),
+            P(AXES, None, None),
+            P(AXES, None, None),
+            P(AXES, None, None),
+            P(AXES, None, None),
+            P(AXES, None, None),
+            P(FSDP, None),
+            P(FSDP, None),
+            P(FSDP, None),
+            P(FSDP, None),
         ),
         out_specs=(
-            P(("fsdp", "rep"), None, None),
-            P(("fsdp", "rep"), None, None),
-            P(("fsdp", "rep"), None, None),
-            P(("fsdp", "rep"), None, None),
-            P(("fsdp", "rep"), None, None),
-            P("fsdp", None),
-            P("fsdp", None),
-            P("fsdp", None),
-            P("fsdp", None),
+            P(AXES, None, None),
+            P(AXES, None, None),
+            P(AXES, None, None),
+            P(AXES, None, None),
+            P(AXES, None, None),
+            P(FSDP, None),
+            P(FSDP, None),
+            P(FSDP, None),
+            P(FSDP, None),
         ),
         check_vma=False,
     )

time: 575 us -> 326 us (0.57)
  waiting for transfers between devices: 476 us -> 87 us
  blocking collectives: 0 us -> 117 us
  local copies, waits for them, and re-layouts: 20.6 us -> 41.8 us
  matrix products: 44.6 us -> 37.4 us
  starting transfers between devices: 0.38 us -> 7.56 us
    psum x1 -> x0, waiting for transfers between devices: 153 us -> none  [on_device(): lax.psum(row_share.astype(jnp.bfloat16), 'rep').astype(jnp.float32)]
    reduce_scatter x1 -> x0, waiting for transfers between devices: 135 us -> none  [on_device(): lax.psum_scatter(weight_term, 'fsdp', scatter_dimension=0, tiled=True)]
    all_to_all x0 -> x5, blocking collectives: none -> 117 us  [the longest x1 29.6 us: gather_rows(): lax.all_to_all(jnp.broadcast_to(part[None], (8, ROWS, QUARTER)), ('zh', '...]
    all_gather x2 -> x1, waiting for transfers between devices: 189 us -> 83 us  [on_device(): teacher_full = lax.all_gather(teacher_half, FSDP, axis=0, tiled=True)]
    transpose x0 -> x9, local copies, waits for them, and re-layouts: none -> 9.43 us  [the longest x4 3.17 us: join_quarters(): tail = parts[:, :, MAIN:].transpose(1, 0, 2).reshape(rows, 4 * TAIL)]
    ppermute x0 -> x2, starting transfers between devices: none -> 7.52 us  [the longest x1 5.61 us: gather_rows(): other = lax.ppermute(own, 'c', SWAP)]
    ppermute x0 -> x2, local copies, waits for them, and re-layouts: none -> 6.6 us  [the longest x1 3.87 us: gather_rows(): other = lax.ppermute(own, 'c', SWAP)]
  transfers between devices with their start and end apart: 4 -> 3, of which waited for: 4 -> 2; matrix products, arithmetic and copies ran while one was open for 6% -> 7% of each run, Pallas kernels for 0% -> 0%
where the time goes in v1:
time: 326 us; the launch traced here: 325 us
  blocking collectives  117 us (36%)
  waiting for transfers between devices  87 us (27%)
  local copies, waits for them, and re-layouts  41.8 us (13%)
  matrix products  37.4 us (11%)
  other arithmetic  18.9 us (6%)
  between operations  14.8 us (5%)
  starting transfers between devices  7.56 us (2%)
    all_gather x1, waiting for transfers between devices, on_device(): teacher_full = lax.all_gather(teacher_half, FSDP, axis=0, tiled=True)  83 us
    all_to_all x1, blocking collectives, gather_rows(): lax.all_to_all(jnp.broadcast_to(part[None], (8, ROWS, QUARTER)), ('zh', '...  29.6 us
    all_to_all x1, blocking collectives, add_up(): shares = lax.all_to_all(total, ('x', 'yl'), 0, 0, tiled=True)  27.7 us
    all_to_all x1, blocking collectives, gather_rows(): lax.all_to_all(jnp.broadcast_to(block[None], (8, 8 * ROWS, QUARTER)), ('x...  26.8 us
    dot_general x7, matrix products, attend(): jnp.dot(normed.reshape(crop_count * length, feature), weight, preferred_e...  17.6 us
    all_to_all x1, blocking collectives, add_up(): lax.all_to_all(total.reshape(8, ROWS, QUARTER), ('zh', 'yh'), 0, 0, tiled...  17.4 us
    all_to_all x1, blocking collectives, add_up(): lax.all_to_all(jnp.broadcast_to(total[None], (16, ROWS, QUARTER)), ('zl',...  15.8 us
    dot_general x7, matrix products, attend(): jnp.einsum('nhqk,nkhe->nqhe', probability, value_rows, preferred_element_...  10.4 us
  transfers between devices with their start and end apart: 3, of which 2 were waited for; matrix products, arithmetic and copies ran while one was open for 7% of the time, Pallas kernels for 0%

profile of v1, /device:TPU:1, one launch (start us, length us, event | category | flops | bytes accessed | tf_op | source)
XLA Modules:
  0.0 324.9 jit_solution(6840570980324879663)
XLA Ops:
  7.2 1.0 convert_element_type.212
  8.3 29.6 %all_to_all.25 = bf16[8,24,576]{2,1,0:T(8,128)(2,1)S(1)} all-to-all(bf16[8,24,576]{2,1,0:T(8,128)(2,1)S(1)} %broadcast_in_dim.36), channel_id=1, replica_groups=mesh['zh'=2,'yh'=4,'yl'=2,'c'=2,'zl'=4,'x'=4] {'zh','yh'}, dimensions={0} | all-to-all | bytes 442368 | tf_op jit(solution)/shard_map/all_to_all | solution.py:87
  38.1 26.8 %all_to_all.26 = bf16[8,192,576]{2,1,0:T(8,128)(2,1)S(1)} all-to-all(bf16[8,192,576]{2,1,0:T(8,128)(2,1)S(1)} %broadcast_in_dim.75), channel_id=1, replica_groups=mesh['zh'=2,'yh'=4,'yl'=2,'c'=2,'zl'=4,'x'=4] {'x','yl'}, dimensions={0} | all-to-all | bytes 3538944 | tf_op jit(solution)/shard_map/all_to_all | solution.py:91
  65.0 2.3 copy.188
  67.3 5.6 %collective-permute-start = (bf16[4,384,576]{1,2,0:T(8,128)(2,1)}, bf16[4,384,576]{1,2,0:T(8,128)(2,1)}, u32[]{:S(2)}, u32[]{:S(2)}) collective-permute-start(bf16[4,384,576]{1,2,0:T(8,128)(2,1)} %copy.188), channel_id=1, source_target_pairs={{0,16},{16,0},{1,17},{17,1},{2,18},{18,2},{3,19},{19,3},{4,20},{20... | collective-permute-start | bytes 5308424 | tf_op jit(solution)/shard_map/ppermute | solution.py:94
  73.9 0.7 reshape.360
  74.6 1.0 reshape.370
  75.6 1.1 copy.203
  77.1 0.6 fusion.55
  77.7 3.9 %copy.189 = bf16[4,384,576]{2,1,0:T(8,128)(2,1)} copy(bf16[4,384,576]{1,2,0:T(8,128)(2,1)} %collective-permute-done) | data formatting | bytes 3538944 | tf_op jit(solution)/shard_map/ppermute | solution.py:94
  81.6 3.1 fusion.9
  85.2 1.0 slice_bitcast_fusion.1
  86.5 2.1 copy.192
  88.6 2.8 copy.191
  91.4 3.3 %convolution_convert_fusion.4 = bf16[74,2304]{1,0:T(8,128)(2,1)S(1)} fusion(bf16[74,768]{1,0:T(8,128)(2,1)} %reshape.360, bf16[768,256]{0,1:T(8,128)(2,1)} %bitcast.230, bf16[768,2048]{0,1:T(8,128)(2,1)} %bitcast.212), kind=kOutput, calls=%fused_computation.25 | convolution fusion | flops 269130240 | bytes 3993600 | tf_op jit(solution)/shard_map/jvp()/dot_general | solution.py:28
  95.8 1.0 fusion.21
  97.1 1.1 fusion.23
  98.2 1.0 fusion.22
  99.2 1.2 convolution_convert_fusion.3
  100.4 1.2 copy.193
  101.6 1.1 fusion.11
  103.1 3.1 fusion.6
  106.2 2.4 fusion.16
  108.7 2.4 fusion.15
  111.3 1.1 copy.210
  112.4 2.5 reshape.371
  114.8 2.1 fusion.17
  116.9 1.6 pad_add_fusion
  118.6 2.2 convolution_convert_fusion.1
  120.8 1.1 fusion.7
  122.4 1.3 copy-done.1
  124.0 0.7 slice-done
  124.7 0.9 copy.212
  125.6 2.2 copy.213
  127.7 1.5 pad_maximum_fusion
  129.3 0.6 copy.214
  129.9 1.9 copy-done
  131.9 2.4 copy.215
  134.3 1.9 collective-permute-start.1
  136.2 4.0 %collective-permute-done.1 = bf16[4,384,576]{1,2,0:T(8,128)(2,1)} collective-permute-done((bf16[4,384,576]{1,2,0:T(8,128)(2,1)}, bf16[4,384,576]{1,2,0:T(8,128)(2,1)}, u32[]{:S(2)}, u32[]{:S(2)}) %collective-permute-start.1) | collective-permute-done | bytes 1769504 | tf_op jit(solution)/shard_map/ppermute | solution.py:99
  140.2 2.7 copy.216
  142.9 2.0 fusion.10
  145.0 27.7 %all_to_all.27 = bf16[8,192,576]{2,1,0:T(8,128)(2,1)S(1)} all-to-all(bf16[8,192,576]{2,1,0:T(8,128)(2,1)S(1)} %bitcast.203), channel_id=1, replica_groups=mesh['zh'=2,'yh'=4,'yl'=2,'c'=2,'zl'=4,'x'=4] {'x','yl'}, dimensions={0} | all-to-all | bytes 3538944 | tf_op jit(solution)/shard_map/all_to_all | solution.py:101
  173.0 17.4 %all_to_all.28 = bf16[8,24,576]{2,1,0:T(8,128)(2,1)S(1)} all-to-all(bf16[8,24,576]{2,1,0:T(8,128)(2,1)S(1)} %bitcast.227), channel_id=1, replica_groups=mesh['zh'=2,'yh'=4,'yl'=2,'c'=2,'zl'=4,'x'=4] {'zh','yh'}, dimensions={0} | all-to-all | bytes 442368 | tf_op jit(solution)/shard_map/all_to_all | solution.py:103
  190.6 15.8 %all_to_all.29 = bf16[16,24,576]{2,1,0:T(8,128)(2,1)S(1)} all-to-all(bf16[16,24,576]{2,1,0:T(8,128)(2,1)S(1)} %broadcast_in_dim.90), channel_id=1, replica_groups=mesh['zh'=2,'yh'=4,'yl'=2,'c'=2,'zl'=4,'x'=4] {'zl','x'}, dimensions={0} | all-to-all | bytes 884736 | tf_op jit(solution)/shard_map/all_to_all | solution.py:105
  206.8 2.0 multiply_add_fusion
  209.2 0.6 add_rsqrt_fusion
  210.3 0.9 convert_element_type.225
  211.2 2.8 fusion.24
  214.1 0.9 fusion.51
  214.9 0.6 multiply_multiply_fusion.1
  215.6 0.9 fusion.54
  216.5 0.8 add_convert_fusion.1
  217.3 0.7 copy.221
  218.0 2.6 convolution_convert_fusion.9
  220.6 2.0 copy.219
  222.6 3.9 %fusion.35 = (f32[257]{0:T(512)S(1)}, f32[257,768]{1,0:T(8,128)S(1)}) fusion(bf16[1,257,768]{2,1,0:T(8,128)(2,1)S(1)} %copy-done.9, f32[257]{0:T(512)S(1)} %copy-done.39, bf16[257,2304]{0,1:T(8,128)(2,1)} %bitcast.222, bf16[768,256]{0,1:T(8,128)(2,1)} %bitcast.231, bf16[768,2048]{0,1:T(8,128)(2,1)} %bitcast.214), kind=kOutput, calls=%fused_computation.72 | convolution fusion | flops 917770496 | bytes 5909512 | tf_op jit(solution)/shard_map/transpose(jvp())/dot_general | solution.py:28
  226.9 0.9 add_convert_fusion
  227.8 83.0 %all-gather.2.cloned.1.call-done = bf16[768,2304]{1,0:T(8,128)(2,1)} async-done(((bf16[24,2304]{1,0:T(8,128)(2,1)}), bf16[768,2304]{1,0:T(8,128)(2,1)}) %all-gather.2.cloned.1.call-update) | async-done | bytes 3538960 | tf_op jit(solution)/shard_map/all_gather | solution.py:125
  310.8 3.2 convolution_convert_fusion.2
  314.0 1.0 copy.201
  314.9 1.1 fusion.8
  316.0 1.1 fusion.13
  317.1 1.0 copy.220
  (144 shorter events, 7.3 us)
Async XLA Ops:
  7.2 303.6 %all-gather.2.cloned.1.call-start = ((), (), s32[]{:S(2)}) async-start(), calls=%async_computation.5 | async-start | bytes 3649536 | tf_op jit(solution)/shard_map/all_gather | solution.py:125
  38.1 34.8 %copy-start.6 = (bf16[2,37,768]{2,0,1:T(2,128)(2,1)S(1)}, bf16[2,37,768]{2,0,1:T(2,128)(2,1)}, u32[]{:S(2)}) copy-start(bf16[2,37,768]{2,0,1:T(2,128)(2,1)} %param.10) | copy-start | bytes 340996
  38.1 36.5 %copy-start.32 = (bf16[2,37,768]{2,0,1:T(2,128)(2,1)S(1)}, bf16[2,37,768]{2,0,1:T(2,128)(2,1)}, u32[]{:S(2)}) copy-start(bf16[2,37,768]{2,0,1:T(2,128)(2,1)} %param.13) | copy-start | bytes 340996
  38.1 37.5 %copy-start.24 = (bf16[1,257,768]{2,1,0:T(8,128)(2,1)S(1)}, bf16[1,257,768]{2,1,0:T(8,128)(2,1)}, u32[]{:S(2)}) copy-start(bf16[1,257,768]{2,1,0:T(8,128)(2,1)} %param.12) | copy-start | bytes 1184260
  65.0 11.7 %copy-start.8 = (bf16[1,257,768]{2,1,0:T(8,128)(2,1)S(1)}, bf16[1,257,768]{2,1,0:T(8,128)(2,1)}, u32[]{:S(2)}) copy-start(bf16[1,257,768]{2,1,0:T(8,128)(2,1)} %param.9) | copy-start | bytes 1184260
  67.3 10.4 %collective-permute-start = (bf16[4,384,576]{1,2,0:T(8,128)(2,1)}, bf16[4,384,576]{1,2,0:T(8,128)(2,1)}, u32[]{:S(2)}, u32[]{:S(2)}) collective-permute-start(bf16[4,384,576]{1,2,0:T(8,128)(2,1)} %copy.188), channel_id=1, source_target_pairs={{0,16},{16,0},{1,17},{17,1},{2,18},{18,2},{3,19},{19,3},{4,20},{20... | collective-permute-start | bytes 5308424 | tf_op jit(solution)/shard_map/ppermute | solution.py:94
  73.0 11.7 %copy-start.35 = (f32[2,37]{1,0:T(2,128)}, f32[2,37]{1,0:T(2,128)S(1)}, u32[]{:S(2)}) copy-start(f32[2,37]{1,0:T(2,128)S(1)} %broadcast_multiply_fusion.2) | copy-start | bytes 892
  73.2 0.5 copy-start.41
  73.8 3.0 copy-start.40
  76.8 41.7 %copy-start.38 = (f32[257]{0:T(512)}, f32[257]{0:T(512)S(1)}, u32[]{:S(2)}) copy-start(f32[257]{0:T(512)S(1)} %broadcast_multiply_fusion.1) | copy-start | bytes 3088
  77.1 7.6 %copy-start.36 = (f32[257]{0:T(512)}, f32[257]{0:T(512)S(1)}, u32[]{:S(2)}) copy-start(f32[257]{0:T(512)S(1)} %fusion.33) | copy-start | bytes 3088
  94.7 1.1 copy-start.21
  95.4 3.8 %copy-start.19 = (bf16[2,37,1,12,64]{4,3,2,1,0:T(8,128)(2,1)}, bf16[2,37,1,12,64]{4,3,2,1,0:T(8,128)(2,1)S(1)}, u32[]{:S(2)}) copy-start(bf16[2,37,1,12,64]{4,3,2,1,0:T(8,128)(2,1)S(1)} %get-tuple-element.82) | copy-start | bytes 340996
  95.7 2.4 copy-start.12
  95.8 2.4 copy-start.33
  96.8 2.4 copy-start.10
  96.8 2.4 copy-start.25
  96.8 2.4 copy-start.44
  101.6 1.2 copy-start.4
  101.6 1.5 copy-start.11
  103.1 3.2 copy-start.5
  106.2 8.6 %copy-start.2 = (bf16[12,257,257]{1,2,0:T(8,128)(2,1)}, bf16[12,257,257]{1,2,0:T(8,128)(2,1)S(1)}, u32[]{:S(2)}) copy-start(bf16[12,257,257]{1,2,0:T(8,128)(2,1)S(1)} %get-tuple-element.79) | copy-start | bytes 4755532
  108.7 2.4 copy-start.27
  108.7 2.4 copy-start.28
  108.7 2.4 copy-start.29
  118.5 2.2 copy-start.14
  118.5 2.2 copy-start.17
  118.6 2.2 copy-start.23
  121.9 1.7 copy-start.1
  123.7 1.0 slice-start
  129.9 1.9 copy-start
  134.3 5.9 %collective-permute-start.1 = (bf16[4,384,576]{1,2,0:T(8,128)(2,1)}, bf16[4,384,576]{1,2,0:T(8,128)(2,1)}, u32[]{:S(2)}, u32[]{:S(2)}) collective-permute-start(bf16[4,384,576]{1,2,0:T(8,128)(2,1)} %bitcast.220), channel_id=1, source_target_pairs={{0,16},{16,0},{1,17},{17,1},{2,18},{18,2},{3,19},{19,3},{4,20},{20... | collective-permute-start | bytes 5308424 | tf_op jit(solution)/shard_map/ppermute | solution.py:99
  172.6 34.1 %copy-start.22 = (f32[24,2304]{1,0:T(8,128)S(1)}, f32[24,2304]{1,0:T(8,128)}, u32[]{:S(2)}) copy-start(f32[24,2304]{1,0:T(8,128)} %param.14) | copy-start | bytes 663556
  172.6 34.1 %copy-start.30 = (f32[24,2304]{1,0:T(8,128)S(1)}, f32[24,2304]{1,0:T(8,128)}, u32[]{:S(2)}) copy-start(f32[24,2304]{1,0:T(8,128)} %param.15) | copy-start | bytes 663556
  173.0 33.7 %copy-start.31 = (f32[24,2304]{1,0:T(8,128)S(1)}, f32[24,2304]{1,0:T(8,128)}, u32[]{:S(2)}) copy-start(f32[24,2304]{1,0:T(8,128)} %param.16) | copy-start | bytes 663556
  173.0 35.8 %copy-start.15 = (bf16[1,257,768]{2,1,0:T(8,128)(2,1)S(1)}, bf16[1,257,768]{2,1,0:T(8,128)(2,1)}, u32[]{:S(2)}) copy-start(bf16[1,257,768]{2,1,0:T(8,128)(2,1)} %param.11) | copy-start | bytes 1184260
  190.5 19.4 %copy-start.13 = (f32[2,12,37,37]{2,3,1,0:T(8,128)S(1)}, f32[2,12,37,37]{2,3,1,0:T(8,128)}, u32[]{:S(2)}) copy-start(f32[2,12,37,37]{2,3,1,0:T(8,128)} %copy-done.12) | copy-start | bytes 394276
  190.5 19.4 %copy-start.20 = (bf16[2,37,1,12,64]{4,3,2,1,0:T(8,128)(2,1)S(1)}, bf16[2,37,1,12,64]{4,3,2,1,0:T(8,128)(2,1)}, u32[]{:S(2)}) copy-start(bf16[2,37,1,12,64]{4,3,2,1,0:T(8,128)(2,1)} %copy-done.19) | copy-start | bytes 340996
  190.5 19.4 %copy-start.34 = (f32[2,12,37]{2,1,0:T(8,128)S(1)}, f32[2,12,37]{2,1,0:T(8,128)}, u32[]{:S(2)}) copy-start(f32[2,12,37]{2,1,0:T(8,128)} %copy-done.33) | copy-start | bytes 10660
  206.5 4.7 %copy-start.18 = (bf16[74,2304]{1,0:T(8,128)(2,1)S(1)}, bf16[74,2304]{1,0:T(8,128)(2,1)}, u32[]{:S(2)}) copy-start(bf16[74,2304]{1,0:T(8,128)(2,1)} %reshape.371) | copy-start | bytes 1022980
  206.5 4.7 %copy-start.26 = (bf16[768,4,64]{0,2,1:T(8,128)(2,1)S(1)}, bf16[768,4,64]{0,2,1:T(8,128)(2,1)}, u32[]{:S(2)}) copy-start(bf16[768,4,64]{0,2,1:T(8,128)(2,1)} %copy.192) | copy-start | bytes 1179652
  209.0 1.3 copy-start.42
  210.3 3.8 %copy-start.7 = (bf16[2,37,768]{2,0,1:T(2,128)(2,1)S(1)}, bf16[2,37,768]{2,0,1:T(2,128)(2,1)}, u32[]{:S(2)}) copy-start(bf16[2,37,768]{2,0,1:T(2,128)(2,1)} %param.10) | copy-start | bytes 340996
  211.2 6.8 %copy-start.3 = (bf16[12,257,257]{1,2,0:T(8,128)(2,1)S(1)}, bf16[12,257,257]{1,2,0:T(8,128)(2,1)}, u32[]{:S(2)}) copy-start(bf16[12,257,257]{1,2,0:T(8,128)(2,1)} %copy-done.2) | copy-start | bytes 4755532
  214.0 8.6 %copy-start.9 = (bf16[1,257,768]{2,1,0:T(8,128)(2,1)S(1)}, bf16[1,257,768]{2,1,0:T(8,128)(2,1)}, u32[]{:S(2)}) copy-start(bf16[1,257,768]{2,1,0:T(8,128)(2,1)} %param.9) | copy-start | bytes 1184260
  214.0 8.6 %copy-start.39 = (f32[257]{0:T(512)S(1)}, f32[257]{0:T(512)}, u32[]{:S(2)}) copy-start(f32[257]{0:T(512)} %copy-done.38) | copy-start | bytes 3088
  222.6 3.9 %copy-start.37 = (f32[257]{0:T(512)S(1)}, f32[257]{0:T(512)}, u32[]{:S(2)}) copy-start(f32[257]{0:T(512)} %copy-done.36) | copy-start | bytes 3088
  222.6 3.9 %copy-start.45 = (f32[257]{0:T(512)S(1)}, f32[257]{0:T(512)}, u32[]{:S(2)}) copy-start(f32[257]{0:T(512)} %fusion.55) | copy-start | bytes 3088
  222.6 88.2 %copy-start.16 = (bf16[1,257,768]{2,1,0:T(8,128)(2,1)S(1)}, bf16[1,257,768]{2,1,0:T(8,128)(2,1)}, u32[]{:S(2)}) copy-start(bf16[1,257,768]{2,1,0:T(8,128)(2,1)} %param.11) | copy-start | bytes 1184260
  222.6 88.2 %copy-start.43 = (f32[257]{0:T(512)S(1)}, f32[257]{0:T(512)}, u32[]{:S(2)}) copy-start(f32[257]{0:T(512)} %copy-done.42) | copy-start | bytes 3088
  222.6 88.2 %copy-start.46 = (f32[257]{0:T(512)S(1)}, f32[257]{0:T(512)}, u32[]{:S(2)}) copy-start(f32[257]{0:T(512)} %add_rsqrt_fusion) | copy-start | bytes 3088
Sparse Core Ops, SparseCore 0:
  208.9 101.8 all-gather.1

commit v2 on v0

v2 whole, which is shorter than its diff:
```python
import jax
import jax.numpy as jnp
from jax import lax
from jax.experimental import pallas as pl
from jax.experimental.pallas import tpu as pltpu
from jax.sharding import Mesh, PartitionSpec as P

HEADS = 12
D = 768
G_TOK = 257
LOCAL_AT = 272
L_ALL = 74
ROWS_S = 352
ROWS_T = 272
KEYS = 384
PAIRS = 6
MAIN = 512
TAIL = 64
QUARTER = MAIN + 2 * TAIL
HALF = 384
NT = (((1,), (1,)), ((), ()))
NN = (((1,), (0,)), ((), ()))
TN = (((0,), (0,)), ((), ()))
norm_eps = 1e-06


def dot(a, b, dims):
    return lax.dot_general(a, b, dims, preferred_element_type=jnp.float32)


def normalize(x):
    x = x.astype(jnp.float32)
    centred = x - jnp.mean(x, axis=-1, keepdims=True)
    scale = lax.rsqrt(jnp.mean(centred * centred, axis=-1, keepdims=True) + norm_eps)
    return centred * scale, scale


def one_hot(order_ref):
    row = lax.broadcasted_iota(jnp.int32, (D, D), 0)
    return jnp.where(row == order_ref[...], 1.0, 0.0).astype(jnp.bfloat16)


def project(n_ref, wo_ref, wx_ref, tail_ref, p_ref):
    own = n_ref[:, :HALF]
    other = n_ref[:, HALF:]
    for g in range(4):
        part = dot(own, wo_ref[g, :, :MAIN], NN) + dot(other, wx_ref[g, :, :MAIN], NN)
        p_ref[:, g * MAIN : (g + 1) * MAIN] = part.astype(jnp.bfloat16)
        tail_ref[:HALF, g * TAIL : (g + 1) * TAIL] = wo_ref[g, :, MAIN : MAIN + TAIL]
        tail_ref[HALF:, g * TAIL : (g + 1) * TAIL] = wx_ref[g, :, MAIN : MAIN + TAIL]
    part = dot(n_ref[...], tail_ref[...], NN)
    p_ref[:, 4 * MAIN :] = part.astype(jnp.bfloat16)


def doubled(x, first):
    rows = x.shape[0]
    zero = jnp.zeros_like(x)
    pad = jnp.zeros((KEYS - rows, 128), x.dtype)
    return jnp.concatenate([jnp.where(first, x, zero), pad, jnp.where(first, zero, x), pad], axis=0)


def bias_of(rows):
    q = lax.broadcasted_iota(jnp.int32, (rows, KEYS), 0)
    k = lax.broadcasted_iota(jnp.int32, (rows, KEYS), 1)
    in_global = (q < LOCAL_AT) & (k < G_TOK)
    in_local = (q >= LOCAL_AT) & (k >= LOCAL_AT) & (k < LOCAL_AT + L_ALL) & (q % 2 == k % 2)
    return jnp.where(in_global | in_local, 0.0, -1e30)


def softmax(scores, bias):
    e = jnp.exp(scores + bias)
    return e * (1.0 / jnp.sum(e, axis=-1, keepdims=True))


def pre_kernel(xg_ref, xl_ref, order_ref, n_ref, nt_ref, scr):
    scr[...] = jnp.zeros_like(scr)
    scr[:G_TOK, :] = normalize(xg_ref[...])[0].astype(jnp.bfloat16)
    scr[LOCAL_AT : LOCAL_AT + L_ALL, :] = normalize(xl_ref[...])[0].astype(jnp.bfloat16)
    n = dot(scr[...], one_hot(order_ref), NN)
    n_ref[...] = n.astype(jnp.bfloat16)
    nt_ref[...] = n.T.astype(jnp.bfloat16)


def student_kernel(
    n_ref, nt_ref, wo_ref, wx_ref, gg_ref, gl_ref,
    og_ref, ol_ref, dwo_ref, dwx_ref, dp_ref,
    p_scr, do_scr, tail_scr, bias_scr,
):
    do_scr[...] = jnp.zeros_like(do_scr)
    do_scr[:G_TOK, :] = gg_ref[...]
    do_scr[LOCAL_AT : LOCAL_AT + L_ALL, :] = gl_ref[...]
    bias_scr[...] = bias_of(ROWS_S)
    project(n_ref, wo_ref, wx_ref, tail_scr, p_scr)
    first = lax.broadcasted_iota(jnp.int32, (ROWS_S, 128), 1) < 64

    @pl.loop(0, PAIRS)
    def _(i):
        at = [pl.ds(pl.multiple_of(part * D + i * 128, 128), 128) for part in range(3)]
        q, k, v = (p_scr[:, a] for a in at)
        do = do_scr[:, at[0]]
        kd = doubled(k * jnp.bfloat16(0.125), first)
        vd = doubled(v, first)
        scores = dot(q, kd, NT)
        bias = bias_scr[...]
        p = [softmax(scores[:, h * KEYS : (h + 1) * KEYS], bias) for h in range(2)]
        pb = jnp.concatenate([x.astype(jnp.bfloat16) for x in p], axis=1)
        o = dot(pb, vd, NN)
        dv = dot(pb, do, TN)
        dprob = dot(do, vd, NT)
        od = o * do.astype(jnp.float32)
        delta = [
            jnp.sum(jnp.where(first if h == 0 else ~first, od, 0.0), axis=-1, keepdims=True)
            for h in range(2)
        ]
        ds = jnp.concatenate(
            [
                (p[h] * (dprob[:, h * KEYS : (h + 1) * KEYS] - delta[h])).astype(jnp.bfloat16)
                for h in range(2)
            ],
            axis=1,
        )
        dq = dot(ds, kd, NN)
        dk = dot(ds, q * jnp.bfloat16(0.125), TN)
        o = o.astype(jnp.bfloat16)
        og_ref[:, at[0]] = o[:G_TOK]
        ol_ref[:, at[0]] = o[LOCAL_AT : LOCAL_AT + L_ALL]
        dp_ref[:, at[0]] = dq.astype(jnp.bfloat16)
        dp_ref[:, at[1]] = jnp.where(first, dk[:ROWS_S], dk[KEYS : KEYS + ROWS_S]).astype(jnp.bfloat16)
        dp_ref[:, at[2]] = jnp.where(first, dv[:ROWS_S], dv[KEYS : KEYS + ROWS_S]).astype(jnp.bfloat16)

    for out_ref, rows in ((dwx_ref, slice(HALF, D)), (dwo_ref, slice(0, HALF))):
        nt = nt_ref[rows, :]
        for g in range(4):
            out_ref[g, :, :MAIN] = dot(nt, dp_ref[:, g * MAIN : (g + 1) * MAIN], NN).astype(jnp.bfloat16)
        tail = dot(nt, dp_ref[:, 4 * MAIN :], NN).astype(jnp.bfloat16)
        for g in range(4):
            out_ref[g, :, MAIN : MAIN + TAIL] = tail[:, g * TAIL : (g + 1) * TAIL]
            out_ref[g, :, MAIN + TAIL :] = jnp.zeros((HALF, TAIL), jnp.bfloat16)


def post_kernel(dp_ref, wo_ref, wx_ref, xg_ref, xl_ref, order_ref, bg_ref, bl_ref, tail_scr):
    halves = []
    for w_ref, at in ((wo_ref, 0), (wx_ref, HALF)):
        for g in range(4):
            tail_scr[at : at + HALF, g * TAIL : (g + 1) * TAIL] = w_ref[g, :, MAIN : MAIN + TAIL]
        total = dot(dp_ref[:, 4 * MAIN :], tail_scr[at : at + HALF, :], NT)
        for g in range(4):
            total += dot(dp_ref[:, g * MAIN : (g + 1) * MAIN], w_ref[g, :, :MAIN], NT)
        halves.append(total.astype(jnp.bfloat16))
    dn = dot(jnp.concatenate(halves, axis=1), one_hot(order_ref), NT)
    for x_ref, out_ref, at, count in ((xg_ref, bg_ref, 0, G_TOK), (xl_ref, bl_ref, LOCAL_AT, L_ALL)):
        hat, scale = normalize(x_ref[...])
        d = dn[at : at + count]
        mean = jnp.mean(d, axis=-1, keepdims=True)
        along = jnp.mean(d * hat, axis=-1, keepdims=True)
        out_ref[...] = (scale * (d - mean - hat * along)).astype(jnp.bfloat16)


def teacher_kernel(x_ref, order_ref, wo_ref, wx_ref, o_ref, n_scr, scr, p_scr, tail_scr, bias_scr):
    scr[...] = jnp.zeros_like(scr)
    scr[:G_TOK, :] = normalize(x_ref[...])[0].astype(jnp.bfloat16)
    n_scr[...] = dot(scr[...], one_hot(order_ref), NN).astype(jnp.bfloat16)
    bias_scr[...] = bias_of(ROWS_T)
    project(n_scr, wo_ref, wx_ref, tail_scr, p_scr)
    first = lax.broadcasted_iota(jnp.int32, (ROWS_T, 128), 1) < 64

    @pl.loop(0, PAIRS)
    def _(i):
        at = [pl.ds(pl.multiple_of(part * D + i * 128, 128), 128) for part in range(3)]
        q, k, v = (p_scr[:, a] for a in at)
        scores = dot(q, doubled(k * jnp.bfloat16(0.125), first), NT)
        bias = bias_scr[...]
        p = [softmax(scores[:, h * KEYS : (h + 1) * KEYS], bias).astype(jnp.bfloat16) for h in range(2)]
        o = dot(jnp.concatenate(p, axis=1), doubled(v, first), NN)
        o_ref[:, at[0]] = o[:G_TOK].astype(jnp.bfloat16)


BF = jnp.bfloat16
VMEM = pltpu.CompilerParams(vmem_limit_bytes=40 * 2**20)


def call(kernel, outs, scratch, flops, nbytes, *args):
    return pl.pallas_call(
        kernel,
        out_shape=[jax.ShapeDtypeStruct(s, BF) for s in outs],
        scratch_shapes=[pltpu.VMEM(s, t) for s, t in scratch],
        compiler_params=VMEM,
        cost_estimate=pl.CostEstimate(flops=flops, bytes_accessed=nbytes, transcendentals=0),
    )(*args)


def pre(xg, xl, order):
    return call(pre_kernel, [(ROWS_S, D), (D, ROWS_S)], [((ROWS_S, D), BF)], 10**9, 10**6, xg, xl, order)


def student(n, nt, wo, wx, gg, gl):
    return call(
        student_kernel,
        [(G_TOK, D), (L_ALL, D), (4, HALF, QUARTER), (4, HALF, QUARTER), (ROWS_S, 3 * D)],
        [((ROWS_S, 3 * D), BF), ((ROWS_S, D), BF), ((D, 256), BF), ((ROWS_S, KEYS), jnp.float32)],
        8 * 10**9, 10**7, n, nt, wo, wx, gg, gl,
    )


def post(dp, wo, wx, xg, xl, order):
    return call(post_kernel, [(G_TOK, D), (L_ALL, D)], [((D, 256), BF)], 3 * 10**9, 6 * 10**6, dp, wo, wx, xg, xl, order)


def teacher(x, order, wo, wx):
    return call(
        teacher_kernel,
        [(G_TOK, D)],
        [((ROWS_T, D), BF), ((ROWS_T, D), BF), ((ROWS_T, 3 * D), BF), ((D, 256), BF), ((ROWS_T, KEYS), jnp.float32)],
        3 * 10**9, 5 * 10**6, x, order, wo, wx,
    )[0]


ROWS = 24
AXES = ("zh", "yh", "yl", "c", "zl", "x")
FSDP = ("zh", "yh", "yl", "c")
SWAP = [(0, 1), (1, 0)]
TOKENS = 169472

beta_one = 0.9
beta_two = 0.999
corr_one = 1.0 - 0.9**10
corr_two = 1.0 - 0.999**10
learn_rate = 0.002
decay_rate = 0.04
momentum = 0.994
adam_eps = 1e-08


def adam_update(weight, teacher_weight, first, second, gradient):
    first = beta_one * first + (1.0 - beta_one) * gradient
    second = beta_two * second + (1.0 - beta_two) * gradient * gradient
    update = first / corr_one / (jnp.sqrt(second / corr_two) + adam_eps)
    weight_new = weight - learn_rate * (update + decay_rate * weight)
    teacher_new = momentum * teacher_weight + (1.0 - momentum) * weight_new
    return (weight_new, teacher_new, first, second)


def exchange(x, axes):
    return lax.all_to_all(x, axes, 0, 0, tiled=True)


def spread(x, count):
    return jnp.broadcast_to(x[None], (count,) + x.shape)


def swap(x):
    return lax.ppermute(x, "c", SWAP)


def own_quarter(half):
    place = lax.axis_index("x")
    main = lax.dynamic_slice_in_dim(half, place * MAIN, MAIN, axis=1)
    tail = lax.dynamic_slice_in_dim(half, 4 * MAIN + place * TAIL, TAIL, axis=1)
    return jnp.concatenate([main, tail, jnp.zeros_like(tail)], axis=1)


def join_quarters(parts):
    main = parts[:, :, :MAIN].transpose(1, 0, 2).reshape(ROWS, 4 * MAIN)
    tail = parts[:, :, MAIN : MAIN + TAIL].transpose(1, 0, 2).reshape(ROWS, 4 * TAIL)
    return jnp.concatenate([main, tail], axis=1)


def row_order():
    place = jnp.arange(D, dtype=jnp.int32)
    core = lax.axis_index("c").astype(jnp.int32)
    core = jnp.where(place < HALF, core, 1 - core)
    inner = place % HALF
    low, high, row = inner // 192, (inner % 192) // ROWS, inner % ROWS
    return (((high * 2 + low) * 2 + core) * ROWS + row)[None]


def add_up(own, other):
    total = own.astype(jnp.float32) + swap(other).astype(jnp.float32)
    total = total.astype(BF).reshape(8, 8 * ROWS, QUARTER)
    shares = exchange(total, ("x", "yl"))
    total = jnp.sum(shares.astype(jnp.float32), axis=0).astype(BF)
    shares = exchange(total.reshape(8, ROWS, QUARTER), ("zh", "yh"))
    total = jnp.sum(shares.astype(jnp.float32), axis=0).astype(BF)
    shares = exchange(spread(total, 16), ("zl", "x"))
    total = jnp.sum(shares.astype(jnp.float32).reshape(4, 4, ROWS, QUARTER), axis=0)
    return join_quarters(total)


def tokens(x):
    return x.transpose(1, 0, 2).reshape(L_ALL, D)


def crops(x):
    return x.reshape(L_ALL // 2, 2, D).transpose(1, 0, 2)


def on_device(
    student_global,
    student_local,
    teacher_global,
    grad_global,
    grad_local,
    student_qkv,
    teacher_qkv,
    first_moment,
    second_moment,
):
    order = row_order()
    parts = jnp.stack([own_quarter(student_qkv.astype(BF)), own_quarter(teacher_qkv.astype(BF))])
    columns = exchange(spread(parts, 8), ("zh", "yh"))
    columns = columns.transpose(1, 0, 2, 3).reshape(2, 8 * ROWS, QUARTER)
    student_own = exchange(spread(columns[0], 8), ("x", "yl")).reshape(4, HALF, QUARTER)
    student_other = swap(student_own)

    local = tokens(student_local)
    normed, normed_t = pre(student_global[0], local, order)
    out_g, out_l, own_term, other_term, d_projected = student(
        normed, normed_t, student_own, student_other, grad_global[0], tokens(grad_local)
    )
    teacher_own = exchange(spread(columns[1], 8), ("x", "yl")).reshape(4, HALF, QUARTER)
    teacher_other = swap(teacher_own)
    teacher_rows = teacher(teacher_global[0], order, teacher_own, teacher_other)
    back_g, back_l = post(d_projected, student_own, student_other, student_global[0], local, order)

    gradient = add_up(own_term, other_term) * (1.0 / jnp.sqrt(jnp.float32(TOKENS)))
    new_student, new_teacher, new_first, new_second = adam_update(
        student_qkv, teacher_qkv, first_moment, second_moment, gradient
    )
    return (
        out_g[None],
        crops(out_l),
        teacher_rows[None],
        back_g[None],
        crops(back_l),
        new_student,
        new_teacher,
        new_first,
        new_second,
    )


def solution(mesh):
    mesh = Mesh(mesh.devices.reshape(2, 4, 2, 2, 4, 4), AXES)
    crop, rows = P(AXES, None, None), P(FSDP, None)
    return jax.shard_map(
        on_device,
        mesh=mesh,
        in_specs=(crop,) * 5 + (rows,) * 4,
        out_specs=(crop,) * 5 + (rows,) * 4,
        check_vma=False,
    )
```

time: 575 us -> 179 us (0.31)
  the two profiles are of different devices: /device:TPU:1 before, /device:TPU:10 now
where the time goes in v2:
time: 179 us
  blocking collectives  83.8 us (47%)
  Pallas kernels  30 us (17%)
  waiting for transfers between devices  25.8 us (14%)
  starting transfers between devices  23.1 us (13%)
  local copies, waits for them, and re-layouts  8.3 us (5%)
  other arithmetic  6.77 us (4%)
    all_to_all x3, blocking collectives, exchange(): return lax.all_to_all(x, axes, 0, 0, tiled=True)  83.8 us
    pallas_call x4, Pallas kernels, call(): pl.pallas_call(kernel, out_shape=[jax.ShapeDtypeStruct(s, BF) for s in ou...  30 us
    all_to_all x3, waiting for transfers between devices, exchange(): return lax.all_to_all(x, axes, 0, 0, tiled=True)  22 us
    all_to_all x3, starting transfers between devices, exchange(): return lax.all_to_all(x, axes, 0, 0, tiled=True)  17.2 us
    ppermute x3, starting transfers between devices, swap(): return lax.ppermute(x, 'c', SWAP)  5.94 us
    ppermute x3, waiting for transfers between devices, swap(): return lax.ppermute(x, 'c', SWAP)  3.73 us
    unnamed x24, local copies, waits for them, and re-layouts  3.6 us
  transfers between devices with their start and end apart: 6, of which 2 were waited for; matrix products, arithmetic and copies ran while one was open for 4% of the time, Pallas kernels for 17%

profile of v2, /device:TPU:10, one launch (start us, length us, event | category | flops | bytes accessed | tf_op | source)
XLA Modules:
  0.0 178.6 jit_solution(9725161976072426445)
XLA Ops:
  0.6 1.0 convert_element_type.20
  1.6 1.0 convert_element_type.21
  2.6 0.1 constant_dynamic-slice_fusion
  2.7 0.1 pad.7.clone
  2.8 34.8 %all_to_all.30 = bf16[8,2,24,640]{3,2,1,0:T(8,128)(2,1)S(1)} all-to-all(bf16[8,2,24,640]{3,2,1,0:T(8,128)(2,1)S(1)} %broadcast_in_dim.46), channel_id=1, replica_groups=mesh['zh'=2,'yh'=4,'yl'=2,'c'=2,'zl'=4,'x'=4] {'zh','yh'}, dimensions={0} | all-to-all | bytes 983040 | tf_op jit(solution)/shard_map/all_to_all | solution.py:244
  37.7 0.2 broadcast_in_dim.48
  37.9 28.5 %all_to_all.31 = bf16[8,192,640]{2,1,0:T(8,128)(2,1)} all-to-all(bf16[8,192,640]{2,1,0:T(8,128)(2,1)S(1)} %broadcast_in_dim.48), channel_id=1, replica_groups=mesh['zh'=2,'yh'=4,'yl'=2,'c'=2,'zl'=4,'x'=4] {'x','yl'}, dimensions={0} | all-to-all | bytes 3932160 | tf_op jit(solution)/shard_map/all_to_all | solution.py:244
  66.4 1.9 %collective-permute-start = (bf16[4,384,640]{2,1,0:T(8,128)(2,1)}, bf16[4,384,640]{2,1,0:T(8,128)(2,1)}, u32[]{:S(2)}, u32[]{:S(2)}) collective-permute-start(bf16[4,384,640]{2,1,0:T(8,128)(2,1)} %bitcast.6.wo_ref), channel_id=1, source_target_pairs={{0,16},{16,0},{1,17},{17,1},{2,18},{18,2},{3,19},{19,3},{4,20},{20... | collective-permute-start | bytes 5898248 | tf_op jit(solution)/shard_map/ppermute | solution.py:252
  68.3 1.5 broadcast_in_dim.51
  69.8 0.0 copy-start.9
  69.8 0.0 copy-start.10
  69.8 0.0 copy-start.1
  69.8 5.9 %all-to-all-start.2 = ((bf16[8,192,640]{2,1,0:T(8,128)(2,1)}), bf16[8,192,640]{2,1,0:T(8,128)(2,1)S(1)}, u32[]{:S(2)}, u32[]{:S(2)}) async-start(bf16[8,192,640]{2,1,0:T(8,128)(2,1)} %broadcast_in_dim.51), calls=%async_computation.2 | async-start | bytes 3932160 | tf_op jit(solution)/shard_map/all_to_all | solution.py:244
  75.7 0.0 copy-done.9
  75.7 0.2 reshape.188.xl_ref
  75.9 0.0 copy-done.10
  75.9 0.0 copy-start
  75.9 0.2 reshape.190.gl_ref
  76.1 0.1 fusion.order_ref
  76.1 0.0 copy-done.1
  76.1 1.0 shard_map.160
  77.1 0.0 collective-permute-done.wx_ref
  77.1 0.0 copy-done
  77.1 15.0 %shard_map.161 = (bf16[257,768]{1,0:T(8,128)(2,1)}, bf16[74,768]{1,0:T(8,128)(2,1)S(1)}, bf16[4,384,640]{2,1,0:T(8,128)(2,1)S(1)}, bf16[4,384,640]{2,1,0:T(8,128)(2,1)S(1)}, bf16[352,2304]{1,0:T(8,128)(2,1)S(1)}) custom-call(bf16[352,768]{1,0:T(8,128)(2,1)S(1)} %get-tuple-element.18.n_ref, bf16[768,352]{1,0:T(8,128)(2,1)S(1)} %get-tuple-element.19.nt_ref, ...), custom_call_target="tpu_custom_call" | custom-call | flops 8000000000 | bytes 10000000 | tf_op jit(solution)/shard_map/pallas_call | solution.py:183
  92.1 0.0 copy-start.3
  92.1 1.2 copy-done.3
  93.3 2.1 %collective-permute-start.2 = (bf16[4,384,640]{2,1,0:T(8,128)(2,1)S(1)}, bf16[4,384,640]{2,1,0:T(8,128)(2,1)S(1)}, u32[]{:S(2)}, u32[]{:S(2)}) collective-permute-start(bf16[4,384,640]{2,1,0:T(8,128)(2,1)S(1)} %get-tuple-element.26), channel_id=1, source_target_pairs={{0,16},{16,0},{1,17},{17,1},{2,18},{18,2},{3,19},{19,3},{4,20},{20... | collective-permute-start | bytes 5898248 | tf_op jit(solution)/shard_map/ppermute | solution.py:252
  95.4 3.7 %collective-permute-done.2 = bf16[4,384,640]{2,1,0:T(8,128)(2,1)S(1)} collective-permute-done((bf16[4,384,640]{2,1,0:T(8,128)(2,1)S(1)}, bf16[4,384,640]{2,1,0:T(8,128)(2,1)S(1)}, u32[]{:S(2)}, u32[]{:S(2)}) %collective-permute-start.2) | collective-permute-done | bytes 1966112 | tf_op jit(solution)/shard_map/ppermute | solution.py:252
  99.1 1.7 add_convert_fusion
  100.9 0.0 all-to-all-done.2
  100.9 5.7 %all-to-all-start.3 = ((bf16[8,192,640]{2,1,0:T(8,128)(2,1)}), bf16[8,192,640]{2,1,0:T(8,128)(2,1)}, u32[]{:S(2)}, u32[]{:S(2)}) async-start(bf16[8,192,640]{2,1,0:T(8,128)(2,1)} %bitcast.35), calls=%async_computation.3 | async-start | bytes 3932160 | tf_op jit(solution)/shard_map/all_to_all | solution.py:244
  106.6 1.9 %collective-permute-start.1 = (bf16[4,384,640]{2,1,0:T(8,128)(2,1)S(1)}, bf16[4,384,640]{2,1,0:T(8,128)(2,1)}, u32[]{:S(2)}, u32[]{:S(2)}) collective-permute-start(bf16[4,384,640]{2,1,0:T(8,128)(2,1)S(1)} %bitcast.29), channel_id=1, source_target_pairs={{0,16},{16,0},{1,17},{17,1},{2,18},{18,2},{3,19},{19,3},{4,20},{20... | collective-permute-start | bytes 5898248 | tf_op jit(solution)/shard_map/ppermute | solution.py:252
  108.5 22.0 %all-to-all-done.3 = bf16[8,192,640]{2,1,0:T(8,128)(2,1)} async-done(((bf16[8,192,640]{2,1,0:T(8,128)(2,1)}), bf16[8,192,640]{2,1,0:T(8,128)(2,1)}, u32[]{:S(2)}, u32[]{:S(2)}) %all-to-all-start.3) | async-done | bytes 1966112 | tf_op jit(solution)/shard_map/all_to_all | solution.py:244
  130.5 1.9 %reduce_sum.33 = bf16[192,640]{1,0:T(8,128)(2,1)S(1)} reduce(bf16[8,192,640]{2,1,0:T(8,128)(2,1)} %all-to-all-done.3, bf16[]{:T(256)} %constant.86.clone.1), dimensions={0}, to_apply=%region_0.1 | reduce | flops 860160 | bytes 2211842 | tf_op jit(solution)/shard_map/reduce_sum | solution.py:281
  132.4 20.4 %all_to_all.32 = bf16[8,24,640]{2,1,0:T(8,128)(2,1)S(1)} all-to-all(bf16[8,24,640]{2,1,0:T(8,128)(2,1)S(1)} %bitcast.38), channel_id=1, replica_groups=mesh['zh'=2,'yh'=4,'yl'=2,'c'=2,'zl'=4,'x'=4] {'zh','yh'}, dimensions={0} | all-to-all | bytes 491520 | tf_op jit(solution)/shard_map/all_to_all | solution.py:244
  152.8 0.8 broadcast_in_dim.54
  153.7 5.6 %all-to-all-start.5 = ((bf16[16,24,640]{2,1,0:T(8,128)(2,1)}), bf16[16,24,640]{2,1,0:T(8,128)(2,1)S(1)}, u32[]{:S(2)}, u32[]{:S(2)}) async-start(bf16[16,24,640]{2,1,0:T(8,128)(2,1)} %broadcast_in_dim.54), calls=%async_computation.5 | async-start | bytes 983040 | tf_op jit(solution)/shard_map/all_to_all | solution.py:244
  159.2 0.8 reshape.191
  160.0 0.0 copy-start.4
  160.0 1.4 copy-done.4
  161.4 0.0 copy-start.2
  161.4 5.5 %shard_map.163 = (bf16[257,768]{1,0:T(8,128)(2,1)}, bf16[74,768]{1,0:T(8,128)(2,1)S(1)}) custom-call(bf16[352,2304]{1,0:T(8,128)(2,1)S(1)} %copy-done.4, bf16[4,384,640]{2,1,0:T(8,128)(2,1)} %bitcast.6.wo_ref, bf16[4,384,640]{2,1,0:T(8,128)(2,1)} %collective-permute-done.wx_ref, bf16[257,768]{1,0:T(8,128)(2,1)S(1)} %bitcast.33, ...), custom_call_target="tpu_custom_call" | custom-call | flops 3000000000 | bytes 6000000 | tf_op jit(solution)/shard_map/pallas_call | solution.py:183
  166.9 0.8 reshape.193
  167.7 0.0 collective-permute-done.1.wx_ref
  167.7 0.0 copy-done.2
  167.7 8.6 %shard_map.162 = bf16[257,768]{1,0:T(8,128)(2,1)} custom-call(bf16[257,768]{1,0:T(8,128)(2,1)S(1)} %bitcast.34, s32[1,768]{1,0:T(1,128)S(1)} %fusion.order_ref, bf16[4,384,640]{2,1,0:T(8,128)(2,1)S(1)} %bitcast.30, bf16[4,384,640]{2,1,0:T(8,128)(2,1)} %collective-permute-done.1.wx_ref), custom_call_target="tpu_custom_call" | custom-call | flops 3000000000 | bytes 5000000 | tf_op jit(solution)/shard_map/pallas_call | solution.py:183
  176.3 0.0 copy-start.5
  176.3 0.0 copy-start.6
  176.3 0.0 copy-start.7
  176.3 0.0 copy-start.8
  176.3 0.0 all-to-all-done.5
  176.3 0.1 convert_reduce_fusion
  176.4 0.1 reshape.199
  176.6 0.6 copy-done.5
  177.2 0.1 copy-done.6
  177.3 0.1 copy-done.7
  177.4 0.1 copy-done.8
  177.5 1.0 multiply_add_fusion
  (13 shorter events, 0.2 us)
Async XLA Ops:
  66.4 10.7 %collective-permute-start = (bf16[4,384,640]{2,1,0:T(8,128)(2,1)}, bf16[4,384,640]{2,1,0:T(8,128)(2,1)}, u32[]{:S(2)}, u32[]{:S(2)}) collective-permute-start(bf16[4,384,640]{2,1,0:T(8,128)(2,1)} %bitcast.6.wo_ref), channel_id=1, source_target_pairs={{0,16},{16,0},{1,17},{17,1},{2,18},{18,2},{3,19},{19,3},{4,20},{20... | collective-permute-start | bytes 5898248 | tf_op jit(solution)/shard_map/ppermute | solution.py:252
  69.8 5.9 %copy-start.9 = (bf16[2,37,768]{2,0,1:T(2,128)(2,1)S(1)}, bf16[2,37,768]{2,0,1:T(2,128)(2,1)}, u32[]{:S(2)}) copy-start(bf16[2,37,768]{2,0,1:T(2,128)(2,1)} %param.10) | copy-start | bytes 340996
  69.8 6.1 %copy-start.10 = (bf16[2,37,768]{2,0,1:T(2,128)(2,1)S(1)}, bf16[2,37,768]{2,0,1:T(2,128)(2,1)}, u32[]{:S(2)}) copy-start(bf16[2,37,768]{2,0,1:T(2,128)(2,1)} %param.13) | copy-start | bytes 340996
  69.8 6.4 %copy-start.1 = (bf16[1,257,768]{2,1,0:T(8,128)(2,1)S(1)}, bf16[1,257,768]{2,1,0:T(8,128)(2,1)}, u32[]{:S(2)}) copy-start(bf16[1,257,768]{2,1,0:T(8,128)(2,1)} %param.9) | copy-start | bytes 1184260
  69.8 31.1 %all-to-all-start.2 = ((bf16[8,192,640]{2,1,0:T(8,128)(2,1)}), bf16[8,192,640]{2,1,0:T(8,128)(2,1)S(1)}, u32[]{:S(2)}, u32[]{:S(2)}) async-start(bf16[8,192,640]{2,1,0:T(8,128)(2,1)} %broadcast_in_dim.51), calls=%async_computation.2 | async-start | bytes 3932160 | tf_op jit(solution)/shard_map/all_to_all | solution.py:244
  75.9 1.3 copy-start
  92.1 1.2 copy-start.3
  93.3 5.9 %collective-permute-start.2 = (bf16[4,384,640]{2,1,0:T(8,128)(2,1)S(1)}, bf16[4,384,640]{2,1,0:T(8,128)(2,1)S(1)}, u32[]{:S(2)}, u32[]{:S(2)}) collective-permute-start(bf16[4,384,640]{2,1,0:T(8,128)(2,1)S(1)} %get-tuple-element.26), channel_id=1, source_target_pairs={{0,16},{16,0},{1,17},{17,1},{2,18},{18,2},{3,19},{19,3},{4,20},{20... | collective-permute-start | bytes 5898248 | tf_op jit(solution)/shard_map/ppermute | solution.py:252
  100.9 29.7 %all-to-all-start.3 = ((bf16[8,192,640]{2,1,0:T(8,128)(2,1)}), bf16[8,192,640]{2,1,0:T(8,128)(2,1)}, u32[]{:S(2)}, u32[]{:S(2)}) async-start(bf16[8,192,640]{2,1,0:T(8,128)(2,1)} %bitcast.35), calls=%async_computation.3 | async-start | bytes 3932160 | tf_op jit(solution)/shard_map/all_to_all | solution.py:244
  106.6 61.1 %collective-permute-start.1 = (bf16[4,384,640]{2,1,0:T(8,128)(2,1)S(1)}, bf16[4,384,640]{2,1,0:T(8,128)(2,1)}, u32[]{:S(2)}, u32[]{:S(2)}) collective-permute-start(bf16[4,384,640]{2,1,0:T(8,128)(2,1)S(1)} %bitcast.29), channel_id=1, source_target_pairs={{0,16},{16,0},{1,17},{17,1},{2,18},{18,2},{3,19},{19,3},{4,20},{20... | collective-permute-start | bytes 5898248 | tf_op jit(solution)/shard_map/ppermute | solution.py:252
  153.7 22.6 %all-to-all-start.5 = ((bf16[16,24,640]{2,1,0:T(8,128)(2,1)}), bf16[16,24,640]{2,1,0:T(8,128)(2,1)S(1)}, u32[]{:S(2)}, u32[]{:S(2)}) async-start(bf16[16,24,640]{2,1,0:T(8,128)(2,1)} %broadcast_in_dim.54), calls=%async_computation.5 | async-start | bytes 983040 | tf_op jit(solution)/shard_map/all_to_all | solution.py:244
  160.0 1.4 copy-start.4
  161.4 6.3 %copy-start.2 = (bf16[1,257,768]{2,1,0:T(8,128)(2,1)S(1)}, bf16[1,257,768]{2,1,0:T(8,128)(2,1)}, u32[]{:S(2)}) copy-start(bf16[1,257,768]{2,1,0:T(8,128)(2,1)} %param.11) | copy-start | bytes 1184260
  176.3 0.9 copy-start.5
  176.3 1.0 copy-start.6
  176.3 1.1 copy-start.7
  176.3 1.3 copy-start.8

commit v3 on v2

v3 whole, which is shorter than its diff:
```python
import jax
import jax.numpy as jnp
from jax import lax
from jax.experimental import pallas as pl
from jax.experimental.pallas import tpu as pltpu
from jax.sharding import Mesh, PartitionSpec as P

HEADS = 12
D = 768
G_TOK = 257
LOCAL_AT = 272
L_ALL = 74
ROWS_S = 352
ROWS_T = 272
KEYS = 384
PAIRS = 6
MAIN = 512
SPAN = 192
BLOCK = 4 * SPAN + SPAN // 2
HALF = 384
NT = (((1,), (1,)), ((), ()))
NN = (((1,), (0,)), ((), ()))
TN = (((0,), (0,)), ((), ()))
norm_eps = 1e-06


def dot(a, b, dims):
    return lax.dot_general(a, b, dims, preferred_element_type=jnp.float32)


def normalize(x):
    x = x.astype(jnp.float32)
    centred = x - jnp.mean(x, axis=-1, keepdims=True)
    scale = lax.rsqrt(jnp.mean(centred * centred, axis=-1, keepdims=True) + norm_eps)
    return centred * scale, scale


def one_hot(order_ref):
    row = lax.broadcasted_iota(jnp.int32, (D, D), 0)
    return jnp.where(row == order_ref[...], 1.0, 0.0).astype(jnp.bfloat16)


def assemble(src, at, w_ref):
    for g in range(4):
        for low in range(2):
            block, top = 4 * low + g, at + low * SPAN
            for u in range(4):
                w_ref[top : top + SPAN, g * MAIN + u * 128 : g * MAIN + (u + 1) * 128] = src[
                    block, u * SPAN : (u + 1) * SPAN, :
                ]
            top, left = top + (g % 2) * (SPAN // 2), 4 * MAIN + (g // 2) * 128
            w_ref[top : top + SPAN // 2, left : left + 128] = src[block, 4 * SPAN :, :]


def project(n_ref, w_ref, p_ref):
    for part in range(3):
        at = slice(part * D, (part + 1) * D)
        p_ref[:, at] = dot(n_ref[...], w_ref[:, at], NN).astype(jnp.bfloat16)


def doubled(x, first):
    rows = x.shape[0]
    zero = jnp.zeros_like(x)
    pad = jnp.zeros((KEYS - rows, 128), x.dtype)
    return jnp.concatenate([jnp.where(first, x, zero), pad, jnp.where(first, zero, x), pad], axis=0)


def bias_of(rows):
    q = lax.broadcasted_iota(jnp.int32, (rows, KEYS), 0)
    k = lax.broadcasted_iota(jnp.int32, (rows, KEYS), 1)
    in_global = (q < LOCAL_AT) & (k < G_TOK)
    in_local = (q >= LOCAL_AT) & (k >= LOCAL_AT) & (k < LOCAL_AT + L_ALL) & (q % 2 == k % 2)
    return jnp.where(in_global | in_local, 0.0, -1e30)


def softmax(scores, bias):
    e = jnp.exp(scores + bias)
    return e * (1.0 / jnp.sum(e, axis=-1, keepdims=True))


def copies(pairs, sem):
    return [pltpu.make_async_copy(a, b, sem.at[i]) for i, (a, b) in enumerate(pairs)]


def start(moves):
    for move in moves:
        move.start()


def wait(moves):
    for move in moves:
        move.wait()


def cut_kernel(place_ref, sw_ref, tw_ref, out_ref):
    place = place_ref[0]
    main = pl.ds(pl.multiple_of(place * MAIN, MAIN), MAIN)
    tail = pl.ds(pl.multiple_of(4 * MAIN + place // 2 * 128, 128), 128)
    for i, ref in enumerate((sw_ref, tw_ref)):
        units = ref[:, main].astype(jnp.bfloat16)
        last = ref[:, tail].astype(jnp.bfloat16)
        for copy in range(8):
            for u in range(4):
                out_ref[copy, i, u] = units[:, u * 128 : (u + 1) * 128]
            out_ref[copy, i, 4] = last


def pre_kernel(xg_ref, xl_ref, order_ref, n_ref, nt_ref, scr):
    scr[...] = jnp.zeros_like(scr)
    scr[:G_TOK, :] = normalize(xg_ref[...])[0].astype(jnp.bfloat16)
    scr[LOCAL_AT : LOCAL_AT + L_ALL, :] = normalize(xl_ref[...])[0].astype(jnp.bfloat16)
    n = dot(scr[...], one_hot(order_ref), NN)
    n_ref[...] = n.astype(jnp.bfloat16)
    nt_ref[...] = n.T.astype(jnp.bfloat16)


def student_kernel(
    n_hbm, nt_hbm, gg_hbm, gl_hbm, wo_hbm, wx_hbm,
    og_hbm, ol_hbm, dwo_hbm, dwx_hbm, dp_hbm,
    n_ref, nt_ref, gg_ref, gl_ref, wo_ref, wx_ref, og_ref, ol_ref, dwo_ref, dwx_ref, dp_ref,
    p_scr, do_scr, w_scr, bias_scr, sem,
):
    pairs = [(wo_hbm, wo_ref), (wx_hbm, wx_ref), (n_hbm, n_ref)]
    pairs += [(gg_hbm, gg_ref), (gl_hbm, gl_ref), (nt_hbm, nt_ref)]
    loads = copies(pairs, sem)
    start(loads)
    bias_scr[...] = bias_of(ROWS_S)
    do_scr[...] = jnp.zeros_like(do_scr)
    loads[0].wait()
    assemble(wo_ref, 0, w_scr)
    loads[1].wait()
    assemble(wx_ref, HALF, w_scr)
    wait(loads[2:])
    do_scr[:G_TOK, :] = gg_ref[...]
    do_scr[LOCAL_AT : LOCAL_AT + L_ALL, :] = gl_ref[...]
    project(n_ref, w_scr, p_scr)
    first = lax.broadcasted_iota(jnp.int32, (ROWS_S, 128), 1) < 64

    @pl.loop(0, PAIRS)
    def _(i):
        at = [pl.ds(pl.multiple_of(part * D + i * 128, 128), 128) for part in range(3)]
        q, k, v = (p_scr[:, a] for a in at)
        do = do_scr[:, at[0]]
        kd = doubled(k * jnp.bfloat16(0.125), first)
        vd = doubled(v, first)
        scores = dot(q, kd, NT)
        bias = bias_scr[...]
        p = [softmax(scores[:, h * KEYS : (h + 1) * KEYS], bias) for h in range(2)]
        pb = jnp.concatenate([x.astype(jnp.bfloat16) for x in p], axis=1)
        o = dot(pb, vd, NN)
        dv = dot(pb, do, TN)
        dprob = dot(do, vd, NT)
        od = o * do.astype(jnp.float32)
        delta = [
            jnp.sum(jnp.where(first if h == 0 else ~first, od, 0.0), axis=-1, keepdims=True)
            for h in range(2)
        ]
        ds = jnp.concatenate(
            [
                (p[h] * (dprob[:, h * KEYS : (h + 1) * KEYS] - delta[h])).astype(jnp.bfloat16)
                for h in range(2)
            ],
            axis=1,
        )
        dq = dot(ds, kd, NN)
        dk = dot(ds, q * jnp.bfloat16(0.125), TN)
        o = o.astype(jnp.bfloat16)
        og_ref[:, at[0]] = o[:G_TOK]
        ol_ref[:, at[0]] = o[LOCAL_AT : LOCAL_AT + L_ALL]
        dp_ref[:, at[0]] = dq.astype(jnp.bfloat16)
        dp_ref[:, at[1]] = jnp.where(first, dk[:ROWS_S], dk[KEYS : KEYS + ROWS_S]).astype(jnp.bfloat16)
        dp_ref[:, at[2]] = jnp.where(first, dv[:ROWS_S], dv[KEYS : KEYS + ROWS_S]).astype(jnp.bfloat16)

    pairs = [(og_ref, og_hbm), (ol_ref, ol_hbm), (dp_ref, dp_hbm), (dwx_ref, dwx_hbm), (dwo_ref, dwo_hbm)]
    stores = copies(pairs, sem)
    start(stores[:3])
    for out_ref, rows, move in ((dwx_ref, slice(HALF, D), stores[3]), (dwo_ref, slice(0, HALF), stores[4])):
        nt = nt_ref[rows, :]
        for g in range(4):
            term = dot(nt, dp_ref[:, g * MAIN : (g + 1) * MAIN], NN).astype(jnp.bfloat16)
            for low in range(2):
                for u in range(4):
                    out_ref[4 * low + g, u * SPAN : (u + 1) * SPAN, :] = term[
                        low * SPAN : (low + 1) * SPAN, u * 128 : (u + 1) * 128
                    ]
        term = dot(nt, dp_ref[:, 4 * MAIN :], NN).astype(jnp.bfloat16)
        for g in range(4):
            for low in range(2):
                top, left = low * SPAN + (g % 2) * (SPAN // 2), (g // 2) * 128
                out_ref[4 * low + g, 4 * SPAN :, :] = term[top : top + SPAN // 2, left : left + 128]
        move.start()
    wait(stores)


def post_kernel(
    dp_hbm, xg_hbm, xl_hbm, wo_ref, wx_ref, order_ref, bg_hbm, bl_hbm,
    dp_ref, xg_ref, xl_ref, bg_ref, bl_ref, w_scr, sem,
):
    loads = copies([(dp_hbm, dp_ref), (xg_hbm, xg_ref), (xl_hbm, xl_ref)], sem)
    start(loads)
    assemble(wo_ref, 0, w_scr)
    assemble(wx_ref, HALF, w_scr)
    wait(loads)
    dn = dot(dp_ref[...], w_scr[...], NT).astype(jnp.bfloat16)
    dn = dot(dn, one_hot(order_ref), NT)
    for x_ref, out_ref, at, count in ((xg_ref, bg_ref, 0, G_TOK), (xl_ref, bl_ref, LOCAL_AT, L_ALL)):
        hat, scale = normalize(x_ref[...])
        d = dn[at : at + count]
        mean = jnp.mean(d, axis=-1, keepdims=True)
        along = jnp.mean(d * hat, axis=-1, keepdims=True)
        out_ref[...] = (scale * (d - mean - hat * along)).astype(jnp.bfloat16)
    stores = copies([(bg_ref, bg_hbm), (bl_ref, bl_hbm)], sem)
    start(stores)
    wait(stores)


def teacher_kernel(x_hbm, order_ref, wo_ref, wx_ref, o_ref, x_ref, n_scr, scr, p_scr, w_scr, bias_scr, sem):
    loads = copies([(x_hbm, x_ref)], sem)
    start(loads)
    assemble(wo_ref, 0, w_scr)
    assemble(wx_ref, HALF, w_scr)
    bias_scr[...] = bias_of(ROWS_T)
    scr[...] = jnp.zeros_like(scr)
    wait(loads)
    scr[:G_TOK, :] = normalize(x_ref[...])[0].astype(jnp.bfloat16)
    n_scr[...] = dot(scr[...], one_hot(order_ref), NN).astype(jnp.bfloat16)
    project(n_scr, w_scr, p_scr)
    first = lax.broadcasted_iota(jnp.int32, (ROWS_T, 128), 1) < 64

    @pl.loop(0, PAIRS)
    def _(i):
        at = [pl.ds(pl.multiple_of(part * D + i * 128, 128), 128) for part in range(3)]
        q, k, v = (p_scr[:, a] for a in at)
        scores = dot(q, doubled(k * jnp.bfloat16(0.125), first), NT)
        bias = bias_scr[...]
        p = [softmax(scores[:, h * KEYS : (h + 1) * KEYS], bias).astype(jnp.bfloat16) for h in range(2)]
        o = dot(jnp.concatenate(p, axis=1), doubled(v, first), NN)
        o_ref[:, at[0]] = o[:G_TOK].astype(jnp.bfloat16)


BF = jnp.bfloat16


HBM = pl.BlockSpec(memory_space=pltpu.HBM)
HERE = pl.BlockSpec(memory_space=pltpu.VMEM)
F32 = jnp.float32


def call(kernel, mib, ins, outs, scratch, sems, flops, nbytes, *args):
    scratch = [pltpu.VMEM(s, t) for s, t in scratch]
    return pl.pallas_call(
        kernel,
        in_specs=ins,
        out_specs=[spec for _, spec in outs],
        out_shape=[jax.ShapeDtypeStruct(s, BF) for s, _ in outs],
        scratch_shapes=scratch + [pltpu.SemaphoreType.DMA((n,)) for n in sems],
        compiler_params=pltpu.CompilerParams(vmem_limit_bytes=mib * 2**20),
        cost_estimate=pl.CostEstimate(flops=flops, bytes_accessed=nbytes, transcendentals=0),
    )(*args)


def cut(place, sw, tw):
    ins = [pl.BlockSpec(memory_space=pltpu.SMEM), HERE, HERE]
    return call(cut_kernel, 12, ins, [((8, 2, 5, 24, 128), HERE)], [], [], 10**6, 10**6, place, sw, tw)[0]


def pre(xg, xl, order):
    outs = [((ROWS_S, D), HERE), ((D, ROWS_S), HERE)]
    return call(pre_kernel, 12, [HERE] * 3, outs, [((ROWS_S, D), BF)], [], 10**9, 10**6, xg, xl, order)


def student(n, nt, wo, wx, gg, gl):
    block = (8, BLOCK, 128)
    outs = [(G_TOK, D), (L_ALL, D), block, block, (ROWS_S, 3 * D)]
    here = [(ROWS_S, D), (D, ROWS_S), (G_TOK, D), (L_ALL, D), block, block] + outs
    here += [(ROWS_S, 3 * D), (ROWS_S, D), (D, 3 * D)]
    return call(
        student_kernel, 56, [HBM] * 6, [(s, HBM) for s in outs],
        [(s, BF) for s in here] + [((ROWS_S, KEYS), F32)], [6],
        8 * 10**9, 10**7, n, nt, gg, gl, wo, wx,
    )


def add_kernel(a_ref, b_ref, out_ref):
    out_ref[...] = (a_ref[...].astype(F32) + b_ref[...].astype(F32)).astype(BF)


def add(a, b):
    spec = pl.BlockSpec((2, BLOCK, 128), lambda i: (i, 0, 0))
    return pl.pallas_call(
        add_kernel,
        grid=(4,),
        in_specs=[spec, spec],
        out_specs=spec,
        out_shape=jax.ShapeDtypeStruct((8, BLOCK, 128), BF),
        compiler_params=pltpu.CompilerParams(vmem_limit_bytes=56 * 2**20),
        cost_estimate=pl.CostEstimate(flops=10**6, bytes_accessed=5 * 10**6, transcendentals=0),
    )(a, b)


def post(dp, wo, wx, xg, xl, order):
    outs = [((G_TOK, D), HBM), ((L_ALL, D), HBM)]
    here = [((ROWS_S, 3 * D), BF)] + [((G_TOK, D), BF), ((L_ALL, D), BF)] * 2 + [((D, 3 * D), BF)]
    return call(
        post_kernel, 20, [HBM] * 3 + [HERE] * 3, outs, here, [3],
        3 * 10**9, 6 * 10**6, dp, xg, xl, wo, wx, order,
    )


def teacher(x, order, wo, wx):
    here = [((G_TOK, D), BF), ((ROWS_T, D), BF), ((ROWS_T, D), BF), ((ROWS_T, 3 * D), BF)]
    here += [((D, 3 * D), BF), ((ROWS_T, KEYS), F32)]
    return call(
        teacher_kernel, 20, [HBM] + [HERE] * 3, [((G_TOK, D), HERE)], here, [1],
        3 * 10**9, 5 * 10**6, x, order, wo, wx,
    )[0]


ROWS = 24
AXES = ("zh", "yh", "yl", "c", "zl", "x")
FSDP = ("zh", "yh", "yl", "c")
SWAP = [(0, 1), (1, 0)]
TOKENS = 169472

beta_one = 0.9
beta_two = 0.999
corr_one = 1.0 - 0.9**10
corr_two = 1.0 - 0.999**10
learn_rate = 0.002
decay_rate = 0.04
momentum = 0.994
adam_eps = 1e-08


def adam_update(weight, teacher_weight, first, second, gradient):
    first = beta_one * first + (1.0 - beta_one) * gradient
    second = beta_two * second + (1.0 - beta_two) * gradient * gradient
    update = first / corr_one / (jnp.sqrt(second / corr_two) + adam_eps)
    weight_new = weight - learn_rate * (update + decay_rate * weight)
    teacher_new = momentum * teacher_weight + (1.0 - momentum) * weight_new
    return (weight_new, teacher_new, first, second)


def exchange(x, axes):
    return lax.all_to_all(x, axes, 0, 0, tiled=True)


def spread(x, count):
    return jnp.broadcast_to(x[None], (count,) + x.shape)


def swap(x):
    return lax.ppermute(x, "c", SWAP)


def gather_block(column):
    main = column[:, :4].transpose(1, 0, 2, 3).reshape(4 * SPAN, 128)
    tail = lax.dynamic_slice_in_dim(column[:, 4], lax.axis_index("x") % 2 * 4, 4, axis=0)
    return jnp.concatenate([main, tail.reshape(SPAN // 2, 128)], axis=0)


def by_row(block):
    main = block[: 4 * SPAN].reshape(4, 8, ROWS, 128).transpose(1, 0, 2, 3)
    tail = block[4 * SPAN :].reshape(4, 1, ROWS, 128)
    zero = jnp.zeros_like(tail)
    low = lax.axis_index("x") % 2 == 0
    tail = jnp.concatenate([jnp.where(low, tail, zero), jnp.where(low, zero, tail)], axis=0)
    return jnp.concatenate([main, tail], axis=1)


def join_units(units):
    main = units[:, :4].reshape(16, ROWS, 128)
    tail = units[:, 4].reshape(2, 2, ROWS, 128).sum(axis=1)
    whole = jnp.concatenate([main, tail], axis=0)
    return whole.transpose(1, 0, 2).reshape(ROWS, 3 * D)


def row_order():
    place = jnp.arange(D, dtype=jnp.int32)
    core = lax.axis_index("c").astype(jnp.int32)
    core = jnp.where(place < HALF, core, 1 - core)
    inner = place % HALF
    low, y_high, z_high, row = inner // SPAN, inner % SPAN // 48, inner % 48 // ROWS, inner % ROWS
    return ((((z_high * 4 + y_high) * 2 + low) * 2 + core) * ROWS + row)[None]


def add_up(own, other, beside):
    shares = exchange(add(own, swap(other)), ("yl", "x"))
    shares, beside = lax.optimization_barrier((shares, beside))
    total = jnp.sum(shares.astype(jnp.float32), axis=0).astype(BF)
    shares = exchange(by_row(total), ("yh", "zh"))
    total = jnp.sum(shares.astype(jnp.float32), axis=0).astype(BF)
    shares = exchange(spread(total, 16), ("x", "zl"))
    total = jnp.sum(shares.astype(jnp.float32).reshape(4, 4, 5, ROWS, 128), axis=1)
    return join_units(total), beside


def tokens(x):
    return x.transpose(1, 0, 2).reshape(L_ALL, D)


def crops(x):
    return x.reshape(L_ALL // 2, 2, D).transpose(1, 0, 2)


def on_device(
    student_global,
    student_local,
    teacher_global,
    grad_global,
    grad_local,
    student_qkv,
    teacher_qkv,
    first_moment,
    second_moment,
):
    order = row_order()
    place = lax.axis_index("x").astype(jnp.int32)[None]
    columns = exchange(cut(place, student_qkv, teacher_qkv), ("yh", "zh"))
    local, grad_rows = tokens(student_local), tokens(grad_local)
    normed, normed_t = pre(student_global[0], local, order)
    columns, normed, normed_t, local, grad_rows = lax.optimization_barrier(
        (columns, normed, normed_t, local, grad_rows)
    )
    student_own = exchange(spread(gather_block(columns[:, 0]), 8), ("yl", "x"))
    student_other = swap(student_own)
    out_g, out_l, own_term, other_term, d_projected = student(
        normed, normed_t, student_own, student_other, grad_global[0], grad_rows
    )
    teacher_own = exchange(spread(gather_block(columns[:, 1]), 8), ("yl", "x"))
    teacher_other = swap(teacher_own)
    teacher_rows = teacher(teacher_global[0], order, teacher_own, teacher_other)
    back_g, back_l = post(d_projected, student_own, student_other, student_global[0], local, order)

    gradient, (back_g, back_l) = add_up(own_term, other_term, (back_g, back_l))
    gradient = gradient * (1.0 / jnp.sqrt(jnp.float32(TOKENS)))
    new_student, new_teacher, new_first, new_second = adam_update(
        student_qkv, teacher_qkv, first_moment, second_moment, gradient
    )
    return (
        out_g[None],
        crops(out_l),
        teacher_rows[None],
        back_g[None],
        crops(back_l),
        new_student,
        new_teacher,
        new_first,
        new_second,
    )


def solution(mesh):
    mesh = Mesh(mesh.devices.reshape(2, 4, 2, 2, 4, 4), AXES)
    crop, rows = P(AXES, None, None), P(FSDP, None)
    return jax.shard_map(
        on_device,
        mesh=mesh,
        in_specs=(crop,) * 5 + (rows,) * 4,
        out_specs=(crop,) * 5 + (rows,) * 4,
        check_vma=False,
    )
```

time: 179 us -> 173 us (0.966)
  the two profiles are of different devices: /device:TPU:10 before, /device:TPU:8 now
where the time goes in v3:
time: 173 us; the launch traced here: 172 us
  blocking collectives  49.2 us (28%)
  Pallas kernels  36.3 us (21%)
  starting transfers between devices  35.2 us (20%)
  waiting for transfers between devices  34.7 us (20%)
  local copies, waits for them, and re-layouts  12.5 us (7%)
  other arithmetic  3.17 us (2%)
    all_to_all x2, blocking collectives, exchange(): return lax.all_to_all(x, axes, 0, 0, tiled=True)  49.2 us
    pallas_call x5, Pallas kernels, call(): pl.pallas_call(kernel, in_specs=ins, out_specs=[spec for _, spec in outs]...  32.2 us
    all_to_all x4, waiting for transfers between devices, exchange(): return lax.all_to_all(x, axes, 0, 0, tiled=True)  31.1 us
    all_to_all x4, starting transfers between devices, exchange(): return lax.all_to_all(x, axes, 0, 0, tiled=True)  29.2 us
    unnamed x45, local copies, waits for them, and re-layouts  7.17 us
    ppermute x3, starting transfers between devices, swap(): return lax.ppermute(x, 'c', SWAP)  5.94 us
    pallas_call x1, Pallas kernels, add(): pl.pallas_call(add_kernel, grid=(4,), in_specs=[spec, spec], out_specs=sp...  4.11 us
    ppermute x3, waiting for transfers between devices, swap(): return lax.ppermute(x, 'c', SWAP)  3.67 us
  transfers between devices with their start and end apart: 7, of which 4 were waited for; matrix products, arithmetic and copies ran while one was open for 4% of the time, Pallas kernels for 21%

profile of v3, /device:TPU:8, one launch (start us, length us, event | category | flops | bytes accessed | tf_op | source)
XLA Modules:
  0.0 172.1 jit_solution(5428573494809892796)
XLA Ops:
  0.6 0.0 copy-start.2
  0.7 0.9 copy-done.2
  1.6 0.9 copy-done.4
  2.5 0.8 shard_map.160
  3.4 14.6 %all-to-all-start = ((bf16[8,2,5,24,128]{4,3,2,1,0:T(8,128)(2,1)}), bf16[8,2,5,24,128]{4,3,2,1,0:T(8,128)(2,1)S(1)}, u32[]{:S(2)}, u32[]{:S(2)}) async-start(bf16[8,2,5,24,128]{4,3,2,1,0:T(8,128)(2,1)} %shard_map.160), calls=%async_computation | async-start | bytes 983040 | tf_op jit(solution)/shard_map/all_to_all | solution.py:345
  18.0 0.0 copy-done.20
  18.0 0.2 reshape.275.xl_ref.xl_hbm
  18.2 0.0 copy-start.6
  18.2 0.0 copy-done.21
  18.2 0.8 reshape.276.gl_hbm
  19.0 0.1 fusion.order_ref
  19.1 0.0 copy-done.10
  19.1 1.0 shard_map.161
  20.1 0.0 copy-done.6
  20.1 0.0 copy-start.13
  20.1 0.0 copy-start.15
  20.1 15.3 %all-to-all-done = bf16[8,2,5,24,128]{4,3,2,1,0:T(8,128)(2,1)S(1)} async-done(((bf16[8,2,5,24,128]{4,3,2,1,0:T(8,128)(2,1)}), bf16[8,2,5,24,128]{4,3,2,1,0:T(8,128)(2,1)S(1)}, u32[]{:S(2)}, u32[]{:S(2)}) %all-to-all-start) | async-done | bytes 491552 | tf_op jit(solution)/shard_map/all_to_all | solution.py:345
  35.4 0.1 slice_bitcast_fusion
  35.6 0.2 broadcast_in_dim.45
  35.8 0.0 copy-done.13
  35.8 0.0 copy-done.15
  35.9 28.9 %all_to_all.30.wo_hbm.wo_ref = bf16[8,864,128]{2,1,0:T(8,128)(2,1)S(1)} all-to-all(bf16[8,864,128]{2,1,0:T(8,128)(2,1)S(1)} %broadcast_in_dim.45), channel_id=1, replica_groups=mesh['zh'=2,'yh'=4,'yl'=2,'c'=2,'zl'=4,'x'=4] {'yl','x'}, dimensions={0} | all-to-all | bytes 3538944 | tf_op jit(solution)/shard_map/all_to_all | solution.py:345
  64.8 1.9 %collective-permute-start = (bf16[8,864,128]{2,1,0:T(8,128)(2,1)S(1)}, bf16[8,864,128]{2,1,0:T(8,128)(2,1)}, u32[]{:S(2)}, u32[]{:S(2)}) collective-permute-start(bf16[8,864,128]{2,1,0:T(8,128)(2,1)S(1)} %all_to_all.30.wo_hbm.wo_ref), channel_id=1, source_target_pairs={{0,16},{16,0},{1,17},{17,1},{2,18},{18,2},{3,19},{19,3},{4,20},{20... | collective-permute-start | bytes 5308424 | tf_op jit(solution)/shard_map/ppermute | solution.py:353
  66.8 1.5 broadcast_in_dim.47
  68.3 0.0 copy-done
  68.3 4.9 %all-to-all-start.2 = ((bf16[8,864,128]{2,1,0:T(8,128)(2,1)}), bf16[8,864,128]{2,1,0:T(8,128)(2,1)S(1)}, u32[]{:S(2)}, u32[]{:S(2)}) async-start(bf16[8,864,128]{2,1,0:T(8,128)(2,1)} %broadcast_in_dim.47), calls=%async_computation.2 | async-start | bytes 3538944 | tf_op jit(solution)/shard_map/all_to_all | solution.py:345
  73.2 0.0 collective-permute-done.wx_hbm.wx_ref
  73.2 15.5 %shard_map.162 = (bf16[257,768]{1,0:T(8,128)(2,1)}, bf16[74,768]{1,0:T(8,128)(2,1)}, bf16[8,864,128]{2,1,0:T(8,128)(2,1)}, bf16[8,864,128]{2,1,0:T(8,128)(2,1)}, bf16[352,2304]{1,0:T(8,128)(2,1)}) custom-call(bf16[352,768]{1,0:T(8,128)(2,1)} %copy-done.15, bf16[768,352]{1,0:T(8,128)(2,1)} %copy-done.13, bf16[257,768]{1,0:T(8,128)(2,1)} %bitcast.63, ...), custom_call_target="tpu_custom_call" | custom-call | flops 8000000000 | bytes 10000000 | tf_op jit(solution)/shard_map/pallas_call | solution.py:251
  88.7 2.1 %collective-permute-start.2 = (bf16[8,864,128]{2,1,0:T(8,128)(2,1)}, bf16[8,864,128]{2,1,0:T(8,128)(2,1)S(1)}, u32[]{:S(2)}, u32[]{:S(2)}) collective-permute-start(bf16[8,864,128]{2,1,0:T(8,128)(2,1)} %get-tuple-element.35), channel_id=1, source_target_pairs={{0,16},{16,0},{1,17},{17,1},{2,18},{18,2},{3,19},{19,3},{4,20},{20... | collective-permute-start | bytes 5308424 | tf_op jit(solution)/shard_map/ppermute | solution.py:353
  90.8 3.7 %collective-permute-done.2.b_ref = bf16[8,864,128]{2,1,0:T(8,128)(2,1)S(1)} collective-permute-done((bf16[8,864,128]{2,1,0:T(8,128)(2,1)}, bf16[8,864,128]{2,1,0:T(8,128)(2,1)S(1)}, u32[]{:S(2)}, u32[]{:S(2)}) %collective-permute-start.2) | collective-permute-done | bytes 1769504 | tf_op jit(solution)/shard_map/ppermute | solution.py:353
  94.5 1.2 copy-done.16
  95.7 4.1 %shard_map.164 = bf16[8,864,128]{2,1,0:T(8,128)(2,1)} custom-call(bf16[8,864,128]{2,1,0:T(8,128)(2,1)} %get-tuple-element.34.a_ref, bf16[8,864,128]{2,1,0:T(8,128)(2,1)} %copy-done.16), custom_call_target="tpu_custom_call" | custom-call | flops 1000000 | bytes 5000000 | tf_op jit(solution)/shard_map/pallas_call | solution.py:290
  99.8 0.0 all-to-all-done.2.wo_ref
  99.8 5.9 %all-to-all-start.3 = ((bf16[8,864,128]{2,1,0:T(8,128)(2,1)}), bf16[8,864,128]{2,1,0:T(8,128)(2,1)}, u32[]{:S(2)}, u32[]{:S(2)}) async-start(bf16[8,864,128]{2,1,0:T(8,128)(2,1)} %shard_map.164), calls=%async_computation.3 | async-start | bytes 3538944 | tf_op jit(solution)/shard_map/all_to_all | solution.py:345
  105.7 1.9 %collective-permute-start.1 = (bf16[8,864,128]{2,1,0:T(8,128)(2,1)S(1)}, bf16[8,864,128]{2,1,0:T(8,128)(2,1)}, u32[]{:S(2)}, u32[]{:S(2)}) collective-permute-start(bf16[8,864,128]{2,1,0:T(8,128)(2,1)S(1)} %all-to-all-done.2.wo_ref), channel_id=1, source_target_pairs={{0,16},{16,0},{1,17},{17,1},{2,18},{18,2},{3,19},{19,3},{4,20},{20... | collective-permute-start | bytes 5308424 | tf_op jit(solution)/shard_map/ppermute | solution.py:353
  107.6 0.0 copy-done.1
  107.6 0.0 copy-start.7
  107.6 0.9 copy-done.7
  108.5 1.0 copy-done.11
  109.5 1.4 copy-done.14
  110.9 6.1 %shard_map.165 = (bf16[257,768]{1,0:T(8,128)(2,1)}, bf16[74,768]{1,0:T(8,128)(2,1)S(1)}) custom-call(bf16[352,2304]{1,0:T(8,128)(2,1)S(1)} %copy-done.14, bf16[257,768]{1,0:T(8,128)(2,1)S(1)} %bitcast.46, bf16[74,768]{1,0:T(8,128)(2,1)S(1)} %copy-done.7, bf16[8,864,128]{2,1,0:T(8,128)(2,1)S(1)} %copy-done.1, ...), custom_call_target="tpu_custom_call" | custom-call | flops 3000000000 | bytes 6000000 | tf_op jit(solution)/shard_map/pallas_call | solution.py:251
  117.0 0.0 copy-start.8
  117.0 0.6 copy-done.8
  117.7 10.5 %all-to-all-done.3 = bf16[8,864,128]{2,1,0:T(8,128)(2,1)} async-done(((bf16[8,864,128]{2,1,0:T(8,128)(2,1)}), bf16[8,864,128]{2,1,0:T(8,128)(2,1)}, u32[]{:S(2)}, u32[]{:S(2)}) %all-to-all-start.3) | async-done | bytes 1769504 | tf_op jit(solution)/shard_map/all_to_all | solution.py:345
  128.2 1.8 %reduce_sum.42 = bf16[864,128]{1,0:T(8,128)(2,1)S(1)} reduce(bf16[8,864,128]{2,1,0:T(8,128)(2,1)} %all-to-all-done.3, bf16[]{:T(256)} %constant.110.clone.1), dimensions={0}, to_apply=%region_0.1 | reduce | flops 774144 | bytes 1990658 | tf_op jit(solution)/shard_map/reduce_sum | solution.py:390
  130.0 0.0 copy-start.19
  130.0 0.0 copy-start.12
  130.1 20.2 %all_to_all.31 = bf16[8,5,24,128]{3,2,1,0:T(8,128)(2,1)S(1)} all-to-all(bf16[8,5,24,128]{3,2,1,0:T(8,128)(2,1)S(1)} %copy.31), channel_id=1, replica_groups=mesh['zh'=2,'yh'=4,'yl'=2,'c'=2,'zl'=4,'x'=4] {'yh','zh'}, dimensions={0} | all-to-all | bytes 491520 | tf_op jit(solution)/shard_map/all_to_all | solution.py:345
  150.3 0.9 broadcast_in_dim.51
  151.2 3.8 %all-to-all-start.5 = ((bf16[16,5,24,128]{3,2,1,0:T(8,128)(2,1)}), bf16[16,5,24,128]{3,2,1,0:T(8,128)(2,1)S(1)}, u32[]{:S(2)}, u32[]{:S(2)}) async-start(bf16[16,5,24,128]{3,2,1,0:T(8,128)(2,1)} %broadcast_in_dim.51), calls=%async_computation.5 | async-start | bytes 983040 | tf_op jit(solution)/shard_map/all_to_all | solution.py:345
  155.0 0.0 copy-done.19
  155.0 0.8 reshape.279
  155.8 0.0 collective-permute-done.1.wx_ref
  155.8 0.0 copy-done.12
  155.8 8.8 %shard_map.163 = bf16[257,768]{1,0:T(8,128)(2,1)} custom-call(bf16[257,768]{1,0:T(8,128)(2,1)S(1)} %bitcast.47, s32[1,768]{1,0:T(1,128)S(1)} %fusion.order_ref, bf16[8,864,128]{2,1,0:T(8,128)(2,1)S(1)} %all-to-all-done.2.wo_ref, bf16[8,864,128]{2,1,0:T(8,128)(2,1)} %collective-permute-done.1.wx_ref), custom_call_target="tpu_custom_call" | custom-call | flops 3000000000 | bytes 5000000 | tf_op jit(solution)/shard_map/pallas_call | solution.py:251
  164.6 0.0 copy-start.3
  164.6 0.0 copy-start.5
  164.7 0.0 copy-start.17
  164.7 0.0 copy-start.18
  164.7 0.8 reshape.282
  165.4 5.3 %all-to-all-done.5 = bf16[16,5,24,128]{3,2,1,0:T(8,128)(2,1)S(1)} async-done(((bf16[16,5,24,128]{3,2,1,0:T(8,128)(2,1)}), bf16[16,5,24,128]{3,2,1,0:T(8,128)(2,1)S(1)}, u32[]{:S(2)}, u32[]{:S(2)}) %all-to-all-start.5) | async-done | bytes 491552 | tf_op jit(solution)/shard_map/all_to_all | solution.py:345
  170.8 0.1 convert_reduce_fusion
  170.9 0.1 multiply_multiply_fusion
  171.1 1.1 multiply_add_fusion
  (33 shorter events, 0.4 us)
Async XLA Ops:
  0.6 0.9 copy-start.2
  1.6 0.9 copy-start.4
  2.5 15.5 %copy-start.20 = (bf16[2,37,768]{2,0,1:T(2,128)(2,1)S(1)}, bf16[2,37,768]{2,0,1:T(2,128)(2,1)}, u32[]{:S(2)}) copy-start(bf16[2,37,768]{2,0,1:T(2,128)(2,1)} %param.10) | copy-start | bytes 340996
  2.5 15.7 %copy-start.21 = (bf16[2,37,768]{2,0,1:T(2,128)(2,1)S(1)}, bf16[2,37,768]{2,0,1:T(2,128)(2,1)}, u32[]{:S(2)}) copy-start(bf16[2,37,768]{2,0,1:T(2,128)(2,1)} %param.13) | copy-start | bytes 340996
  2.5 16.6 %copy-start.10 = (bf16[1,257,768]{2,1,0:T(8,128)(2,1)S(1)}, bf16[1,257,768]{2,1,0:T(8,128)(2,1)}, u32[]{:S(2)}) copy-start(bf16[1,257,768]{2,1,0:T(8,128)(2,1)} %param.9) | copy-start | bytes 1184260
  3.4 32.0 %all-to-all-start = ((bf16[8,2,5,24,128]{4,3,2,1,0:T(8,128)(2,1)}), bf16[8,2,5,24,128]{4,3,2,1,0:T(8,128)(2,1)S(1)}, u32[]{:S(2)}, u32[]{:S(2)}) async-start(bf16[8,2,5,24,128]{4,3,2,1,0:T(8,128)(2,1)} %shard_map.160), calls=%async_computation | async-start | bytes 983040 | tf_op jit(solution)/shard_map/all_to_all | solution.py:345
  18.2 1.9 %copy-start.6 = (bf16[74,768]{1,0:T(8,128)(2,1)}, bf16[74,768]{1,0:T(8,128)(2,1)S(1)}, u32[]{:S(2)}) copy-start(bf16[74,768]{1,0:T(8,128)(2,1)S(1)} %reshape.275.xl_ref.xl_hbm) | copy-start | bytes 340996
  20.1 15.7 %copy-start.13 = (bf16[768,352]{1,0:T(8,128)(2,1)}, bf16[768,352]{1,0:T(8,128)(2,1)S(1)}, u32[]{:S(2)}) copy-start(bf16[768,352]{1,0:T(8,128)(2,1)S(1)} %get-tuple-element.29.nt_hbm) | copy-start | bytes 1622020
  20.1 15.7 %copy-start.15 = (bf16[352,768]{1,0:T(8,128)(2,1)}, bf16[352,768]{1,0:T(8,128)(2,1)S(1)}, u32[]{:S(2)}) copy-start(bf16[352,768]{1,0:T(8,128)(2,1)S(1)} %get-tuple-element.28.n_hbm) | copy-start | bytes 1622020
  64.8 3.5 %copy-start = (bf16[8,864,128]{2,1,0:T(8,128)(2,1)}, bf16[8,864,128]{2,1,0:T(8,128)(2,1)S(1)}, u32[]{:S(2)}) copy-start(bf16[8,864,128]{2,1,0:T(8,128)(2,1)S(1)} %all_to_all.30.wo_hbm.wo_ref) | copy-start | bytes 5308420
  64.8 8.4 %collective-permute-start = (bf16[8,864,128]{2,1,0:T(8,128)(2,1)S(1)}, bf16[8,864,128]{2,1,0:T(8,128)(2,1)}, u32[]{:S(2)}, u32[]{:S(2)}) collective-permute-start(bf16[8,864,128]{2,1,0:T(8,128)(2,1)S(1)} %all_to_all.30.wo_hbm.wo_ref), channel_id=1, source_target_pairs={{0,16},{16,0},{1,17},{17,1},{2,18},{18,2},{3,19},{19,3},{4,20},{20... | collective-permute-start | bytes 5308424 | tf_op jit(solution)/shard_map/ppermute | solution.py:353
  68.3 31.6 %all-to-all-start.2 = ((bf16[8,864,128]{2,1,0:T(8,128)(2,1)}), bf16[8,864,128]{2,1,0:T(8,128)(2,1)S(1)}, u32[]{:S(2)}, u32[]{:S(2)}) async-start(bf16[8,864,128]{2,1,0:T(8,128)(2,1)} %broadcast_in_dim.47), calls=%async_computation.2 | async-start | bytes 3538944 | tf_op jit(solution)/shard_map/all_to_all | solution.py:345
  88.7 5.8 %collective-permute-start.2 = (bf16[8,864,128]{2,1,0:T(8,128)(2,1)}, bf16[8,864,128]{2,1,0:T(8,128)(2,1)S(1)}, u32[]{:S(2)}, u32[]{:S(2)}) collective-permute-start(bf16[8,864,128]{2,1,0:T(8,128)(2,1)} %get-tuple-element.35), channel_id=1, source_target_pairs={{0,16},{16,0},{1,17},{17,1},{2,18},{18,2},{3,19},{19,3},{4,20},{20... | collective-permute-start | bytes 5308424 | tf_op jit(solution)/shard_map/ppermute | solution.py:353
  94.5 1.2 copy-start.16
  99.8 7.8 %copy-start.1 = (bf16[8,864,128]{2,1,0:T(8,128)(2,1)S(1)}, bf16[8,864,128]{2,1,0:T(8,128)(2,1)}, u32[]{:S(2)}) copy-start(bf16[8,864,128]{2,1,0:T(8,128)(2,1)} %copy-done) | copy-start | bytes 5308420
  99.8 28.3 %all-to-all-start.3 = ((bf16[8,864,128]{2,1,0:T(8,128)(2,1)}), bf16[8,864,128]{2,1,0:T(8,128)(2,1)}, u32[]{:S(2)}, u32[]{:S(2)}) async-start(bf16[8,864,128]{2,1,0:T(8,128)(2,1)} %shard_map.164), calls=%async_computation.3 | async-start | bytes 3538944 | tf_op jit(solution)/shard_map/all_to_all | solution.py:345
  105.7 50.1 %collective-permute-start.1 = (bf16[8,864,128]{2,1,0:T(8,128)(2,1)S(1)}, bf16[8,864,128]{2,1,0:T(8,128)(2,1)}, u32[]{:S(2)}, u32[]{:S(2)}) collective-permute-start(bf16[8,864,128]{2,1,0:T(8,128)(2,1)S(1)} %all-to-all-done.2.wo_ref), channel_id=1, source_target_pairs={{0,16},{16,0},{1,17},{17,1},{2,18},{18,2},{3,19},{19,3},{4,20},{20... | collective-permute-start | bytes 5308424 | tf_op jit(solution)/shard_map/ppermute | solution.py:353
  107.6 0.9 copy-start.7
  108.5 1.0 copy-start.11
  109.5 1.4 copy-start.14
  117.0 0.7 copy-start.8
  130.0 25.0 %copy-start.19 = (bf16[74,768]{1,0:T(8,128)(2,1)S(1)}, bf16[74,768]{1,0:T(8,128)(2,1)}, u32[]{:S(2)}) copy-start(bf16[74,768]{1,0:T(8,128)(2,1)} %get-tuple-element.33) | copy-start | bytes 340996
  130.0 25.8 %copy-start.12 = (bf16[1,257,768]{2,1,0:T(8,128)(2,1)S(1)}, bf16[1,257,768]{2,1,0:T(8,128)(2,1)}, u32[]{:S(2)}) copy-start(bf16[1,257,768]{2,1,0:T(8,128)(2,1)} %param.11) | copy-start | bytes 1184260
  151.2 19.6 %all-to-all-start.5 = ((bf16[16,5,24,128]{3,2,1,0:T(8,128)(2,1)}), bf16[16,5,24,128]{3,2,1,0:T(8,128)(2,1)S(1)}, u32[]{:S(2)}, u32[]{:S(2)}) async-start(bf16[16,5,24,128]{3,2,1,0:T(8,128)(2,1)} %broadcast_in_dim.51), calls=%async_computation.5 | async-start | bytes 983040 | tf_op jit(solution)/shard_map/all_to_all | solution.py:345
  155.8 8.9 %copy-start.9 = (bf16[74,768]{1,0:T(8,128)(2,1)S(1)}, bf16[74,768]{1,0:T(8,128)(2,1)}, u32[]{:S(2)}) copy-start(bf16[74,768]{1,0:T(8,128)(2,1)} %copy-done.8) | copy-start | bytes 340996
  164.6 6.4 %copy-start.3 = (f32[24,2304]{1,0:T(8,128)S(1)}, f32[24,2304]{1,0:T(8,128)}, u32[]{:S(2)}) copy-start(f32[24,2304]{1,0:T(8,128)} %sw_ref.1) | copy-start | bytes 663556
  164.6 6.4 %copy-start.5 = (f32[24,2304]{1,0:T(8,128)S(1)}, f32[24,2304]{1,0:T(8,128)}, u32[]{:S(2)}) copy-start(f32[24,2304]{1,0:T(8,128)} %tw_ref.1) | copy-start | bytes 663556
  164.7 6.4 %copy-start.17 = (f32[24,2304]{1,0:T(8,128)S(1)}, f32[24,2304]{1,0:T(8,128)}, u32[]{:S(2)}) copy-start(f32[24,2304]{1,0:T(8,128)} %param.16) | copy-start | bytes 663556
  164.7 6.4 %copy-start.18 = (f32[24,2304]{1,0:T(8,128)S(1)}, f32[24,2304]{1,0:T(8,128)}, u32[]{:S(2)}) copy-start(f32[24,2304]{1,0:T(8,128)} %param.17) | copy-start | bytes 663556

commit v4 on v3

v4 whole, which is shorter than its diff:
```python
import jax
import jax.numpy as jnp
from jax import lax
from jax.experimental import pallas as pl
from jax.experimental.pallas import tpu as pltpu
from jax.sharding import Mesh, PartitionSpec as P

HEADS = 12
D = 768
G_TOK = 257
LOCAL_AT = 272
L_ALL = 74
ROWS_S = 352
ROWS_T = 272
KEYS = 384
PAIRS = 6
MAIN = 512
SPAN = 192
BLOCK = 4 * SPAN + SPAN // 2
HALF = 384
AT_N, AT_DO, AT_NT, AT_DP, AT_OL, SHELF = 0, 352, 704, 1472, 2528, 16384
NT = (((1,), (1,)), ((), ()))
NN = (((1,), (0,)), ((), ()))
TN = (((0,), (0,)), ((), ()))
norm_eps = 1e-06
BF = jnp.bfloat16
F32 = jnp.float32


def dot(a, b, dims):
    return lax.dot_general(a, b, dims, preferred_element_type=jnp.float32)


def normalize(x):
    x = x.astype(jnp.float32)
    centred = x - jnp.mean(x, axis=-1, keepdims=True)
    scale = lax.rsqrt(jnp.mean(centred * centred, axis=-1, keepdims=True) + norm_eps)
    return centred * scale, scale


def one_hot(order_ref):
    row = lax.broadcasted_iota(jnp.int32, (D, D), 0)
    return jnp.where(row == order_ref[...], 1.0, 0.0).astype(jnp.bfloat16)


def assemble(src, at, w_ref):
    for g in range(4):
        for low in range(2):
            block, top = 4 * low + g, at + low * SPAN
            for u in range(4):
                w_ref[top : top + SPAN, g * MAIN + u * 128 : g * MAIN + (u + 1) * 128] = src[
                    block, u * SPAN : (u + 1) * SPAN, :
                ]
            top, left = top + (g % 2) * (SPAN // 2), 4 * MAIN + (g // 2) * 128
            w_ref[top : top + SPAN // 2, left : left + 128] = src[block, 4 * SPAN :, :]


def project(n_ref, w_ref, p_ref):
    for part in range(3):
        at = slice(part * D, (part + 1) * D)
        p_ref[:, at] = dot(n_ref[...], w_ref[:, at], NN).astype(jnp.bfloat16)


def doubled(x, first):
    rows = x.shape[0]
    zero = jnp.zeros_like(x)
    pad = jnp.zeros((KEYS - rows, 128), x.dtype)
    return jnp.concatenate([jnp.where(first, x, zero), pad, jnp.where(first, zero, x), pad], axis=0)


def bias_of(shape, keys):
    q = lax.broadcasted_iota(jnp.int32, shape, 1 - keys)
    k = lax.broadcasted_iota(jnp.int32, shape, keys)
    in_global = (q < LOCAL_AT) & (k < G_TOK)
    in_local = (q >= LOCAL_AT) & (k >= LOCAL_AT) & (k < LOCAL_AT + L_ALL) & (q % 2 == k % 2)
    return jnp.where(in_global | in_local, 0.0, -1e30)


def softmax(scores, bias, keys):
    e = jnp.exp(scores + bias)
    return e * (1.0 / jnp.sum(e, axis=keys, keepdims=True))


def copies(pairs, sem):
    return [pltpu.make_async_copy(a, b, sem.at[i]) for i, (a, b) in enumerate(pairs)]


def start(moves):
    for move in moves:
        move.start()


def wait(moves):
    for move in moves:
        move.wait()


def cut_kernel(place_ref, sw_ref, tw_ref, out_ref):
    place = place_ref[0]
    main = pl.ds(pl.multiple_of(place * MAIN, MAIN), MAIN)
    tail = pl.ds(pl.multiple_of(4 * MAIN + place // 2 * 128, 128), 128)
    for i, ref in enumerate((sw_ref, tw_ref)):
        units = ref[:, main].astype(jnp.bfloat16)
        last = ref[:, tail].astype(jnp.bfloat16)
        for copy in range(8):
            for u in range(4):
                out_ref[copy, i, u] = units[:, u * 128 : (u + 1) * 128]
            out_ref[copy, i, 4] = last


def pre_kernel(xg_ref, xl_ref, gg_ref, gl_ref, order_ref, shelf, scr, n_ref, nt_ref, do_ref, sem):
    do_ref[...] = jnp.zeros_like(do_ref)
    do_ref[:G_TOK, :] = gg_ref[...]
    do_ref[LOCAL_AT : LOCAL_AT + L_ALL, :] = gl_ref[...]
    scr[...] = jnp.zeros_like(scr)
    scr[:G_TOK, :] = normalize(xg_ref[...])[0].astype(BF)
    scr[LOCAL_AT : LOCAL_AT + L_ALL, :] = normalize(xl_ref[...])[0].astype(BF)
    n = dot(scr[...], one_hot(order_ref), NN)
    n_ref[...] = n.astype(BF)
    nt_ref[...] = jnp.zeros_like(nt_ref)
    nt_ref[:, :ROWS_S] = n.T.astype(BF)
    moves = copies(
        [
            (n_ref, shelf.at[pl.ds(AT_N, ROWS_S), :]),
            (do_ref, shelf.at[pl.ds(AT_DO, ROWS_S), :]),
            (nt_ref, shelf.at[pl.ds(AT_NT, D), pl.ds(0, KEYS)]),
        ],
        sem,
    )
    start(moves)
    wait(moves)


def student_kernel(
    shelf_in, wo_ref, wx_ref,
    shelf, og_hbm, dwo_ref, dwx_ref,
    n_ref, do_scr, nt_ref, og_ref, ol_ref, dp_ref,
    p_scr, w_scr, bias_scr, sem,
):
    loads = copies(
        [
            (shelf_in.at[pl.ds(AT_N, ROWS_S), :], n_ref),
            (shelf_in.at[pl.ds(AT_DO, ROWS_S), :], do_scr),
            (shelf_in.at[pl.ds(AT_NT, D), pl.ds(0, KEYS)], nt_ref),
        ],
        sem,
    )
    start(loads)
    bias_scr[...] = bias_of((KEYS, ROWS_S), 0)
    ol_ref[...] = jnp.zeros_like(ol_ref)
    assemble(wo_ref, 0, w_scr)
    assemble(wx_ref, HALF, w_scr)
    wait(loads)
    project(n_ref, w_scr, p_scr)
    first = lax.broadcasted_iota(jnp.int32, (ROWS_S, 128), 1) < 64

    @pl.loop(0, PAIRS, unroll=PAIRS)
    def _(i):
        at = [pl.ds(pl.multiple_of(part * D + i * 128, 128), 128) for part in range(3)]
        q, k, v = (p_scr[:, a] for a in at)
        do = do_scr[:, at[0]]
        kd = doubled(k * jnp.bfloat16(0.125), first)
        vd = doubled(v, first)
        scores = dot(kd, q, NT)
        dprob = dot(vd, do, NT)
        bias = bias_scr[...]
        p, ds = [], []
        for h in range(2):
            at_h = slice(h * KEYS, (h + 1) * KEYS)
            prob = softmax(scores[at_h], bias, 0)
            both = prob * dprob[at_h]
            p.append(prob.astype(BF))
            ds.append((both - prob * jnp.sum(both, axis=0, keepdims=True)).astype(BF))
        p = jnp.concatenate(p, axis=0)
        ds = jnp.concatenate(ds, axis=0)
        dv = dot(p, do, NN)
        dk = dot(ds, q * jnp.bfloat16(0.125), NN)
        o = dot(p, vd, TN)
        dq = dot(ds, kd, TN)
        o = o.astype(jnp.bfloat16)
        og_ref[:, at[0]] = o[:G_TOK]
        ol_ref[:L_ALL, at[0]] = o[LOCAL_AT : LOCAL_AT + L_ALL]
        dp_ref[:, at[0]] = dq.astype(jnp.bfloat16)
        dp_ref[:, at[1]] = jnp.where(first, dk[:ROWS_S], dk[KEYS : KEYS + ROWS_S]).astype(jnp.bfloat16)
        dp_ref[:, at[2]] = jnp.where(first, dv[:ROWS_S], dv[KEYS : KEYS + ROWS_S]).astype(jnp.bfloat16)

    pairs = [(og_ref, og_hbm), (ol_ref, shelf.at[pl.ds(AT_OL, 80), :])]
    pairs += [
        (dp_ref.at[:, pl.ds(i * D, D)], shelf.at[pl.ds(AT_DP + i * ROWS_S, ROWS_S), :]) for i in range(3)
    ]
    stores = copies(pairs, sem)
    start(stores)
    for out_ref, rows in ((dwx_ref, slice(HALF, D)), (dwo_ref, slice(0, HALF))):
        nt = nt_ref[rows, :ROWS_S]
        for g in range(4):
            term = dot(nt, dp_ref[:, g * MAIN : (g + 1) * MAIN], NN).astype(jnp.bfloat16)
            for low in range(2):
                for u in range(4):
                    out_ref[4 * low + g, u * SPAN : (u + 1) * SPAN, :] = term[
                        low * SPAN : (low + 1) * SPAN, u * 128 : (u + 1) * 128
                    ]
        term = dot(nt, dp_ref[:, 4 * MAIN :], NN).astype(jnp.bfloat16)
        for g in range(4):
            for low in range(2):
                top, left = low * SPAN + (g % 2) * (SPAN // 2), (g // 2) * 128
                out_ref[4 * low + g, 4 * SPAN :, :] = term[top : top + SPAN // 2, left : left + 128]
    wait(stores)


def post_kernel(
    shelf, xg_hbm, xl_hbm, wo_ref, wx_ref, order_ref, bg_hbm, bl_hbm,
    dp_ref, xg_ref, xl_ref, bg_ref, bl_ref, w_scr, sem,
):
    pairs = [
        (shelf.at[pl.ds(AT_DP + i * ROWS_S, ROWS_S), :], dp_ref.at[:, pl.ds(i * D, D)]) for i in range(3)
    ]
    loads = copies(pairs + [(xg_hbm, xg_ref), (xl_hbm, xl_ref)], sem)
    start(loads)
    assemble(wo_ref, 0, w_scr)
    assemble(wx_ref, HALF, w_scr)
    wait(loads)
    dn = dot(dp_ref[...], w_scr[...], NT).astype(jnp.bfloat16)
    dn = dot(dn, one_hot(order_ref), NT)
    for x_ref, out_ref, at, count in ((xg_ref, bg_ref, 0, G_TOK), (xl_ref, bl_ref, LOCAL_AT, L_ALL)):
        hat, scale = normalize(x_ref[...])
        d = dn[at : at + count]
        mean = jnp.mean(d, axis=-1, keepdims=True)
        along = jnp.mean(d * hat, axis=-1, keepdims=True)
        out_ref[...] = (scale * (d - mean - hat * along)).astype(jnp.bfloat16)
    stores = copies([(bg_ref, bg_hbm), (bl_ref, bl_hbm)], sem)
    start(stores)
    wait(stores)


def teacher_kernel(x_hbm, order_ref, wo_ref, wx_ref, o_ref, x_ref, n_scr, scr, p_scr, w_scr, bias_scr, sem):
    loads = copies([(x_hbm, x_ref)], sem)
    start(loads)
    assemble(wo_ref, 0, w_scr)
    assemble(wx_ref, HALF, w_scr)
    bias_scr[...] = bias_of((ROWS_T, KEYS), 1)
    scr[...] = jnp.zeros_like(scr)
    wait(loads)
    scr[:G_TOK, :] = normalize(x_ref[...])[0].astype(jnp.bfloat16)
    n_scr[...] = dot(scr[...], one_hot(order_ref), NN).astype(jnp.bfloat16)
    project(n_scr, w_scr, p_scr)
    first = lax.broadcasted_iota(jnp.int32, (ROWS_T, 128), 1) < 64

    @pl.loop(0, PAIRS, unroll=PAIRS)
    def _(i):
        at = [pl.ds(pl.multiple_of(part * D + i * 128, 128), 128) for part in range(3)]
        q, k, v = (p_scr[:, a] for a in at)
        scores = dot(q, doubled(k * jnp.bfloat16(0.125), first), NT)
        bias = bias_scr[...]
        p = [softmax(scores[:, h * KEYS : (h + 1) * KEYS], bias, 1).astype(jnp.bfloat16) for h in range(2)]
        o = dot(jnp.concatenate(p, axis=1), doubled(v, first), NN)
        o_ref[:, at[0]] = o[:G_TOK].astype(jnp.bfloat16)


HBM = pl.BlockSpec(memory_space=pltpu.HBM)
HERE = pl.BlockSpec(memory_space=pltpu.VMEM)


def call(kernel, mib, ins, outs, scratch, sems, flops, nbytes, *args, aliases=None):
    scratch = [pltpu.VMEM(s, t) for s, t in scratch]
    return pl.pallas_call(
        kernel,
        in_specs=ins,
        out_specs=[spec for _, spec in outs],
        out_shape=[jax.ShapeDtypeStruct(s, BF) for s, _ in outs],
        scratch_shapes=scratch + [pltpu.SemaphoreType.DMA((n,)) for n in sems],
        input_output_aliases=aliases or {},
        compiler_params=pltpu.CompilerParams(vmem_limit_bytes=mib * 2**20),
        cost_estimate=pl.CostEstimate(flops=flops, bytes_accessed=nbytes, transcendentals=0),
    )(*args)


def cut(place, sw, tw):
    ins = [pl.BlockSpec(memory_space=pltpu.SMEM), HERE, HERE]
    return call(cut_kernel, 56, ins, [((8, 2, 5, 24, 128), HERE)], [], [], 10**6, 10**6, place, sw, tw)[0]


SHELF_SHAPE = (SHELF, D)


def pre(xg, xl, gg, gl, order):
    here = [((ROWS_S, D), BF), ((ROWS_S, D), BF), ((D, KEYS), BF), ((ROWS_S, D), BF)]
    return call(
        pre_kernel, 44, [HERE] * 5, [(SHELF_SHAPE, HBM)], here, [3],
        10**9, 10**6, xg, xl, gg, gl, order,
    )[0]


def student(shelf, wo, wx):
    block = (8, BLOCK, 128)
    outs = [(SHELF_SHAPE, HBM), ((G_TOK, D), HBM), (block, HERE), (block, HERE)]
    here = [(ROWS_S, D), (ROWS_S, D), (D, KEYS), (G_TOK, D), (80, D)]
    here += [(ROWS_S, 3 * D), (ROWS_S, 3 * D), (D, 3 * D)]
    return call(
        student_kernel, 42, [HBM, HERE, HERE], outs, [(s, BF) for s in here] + [((KEYS, ROWS_S), F32)], [5],
        8 * 10**9, 10**7, shelf, wo, wx, aliases={0: 0},
    )


def post(shelf, wo, wx, xg, xl, order):
    outs = [((G_TOK, D), HBM), ((L_ALL, D), HBM)]
    here = [((ROWS_S, 3 * D), BF)] + [((G_TOK, D), BF), ((L_ALL, D), BF)] * 2 + [((D, 3 * D), BF)]
    return call(
        post_kernel, 42, [HBM] * 3 + [HERE] * 3, outs, here, [5],
        3 * 10**9, 6 * 10**6, shelf, xg, xl, wo, wx, order,
    )


def teacher(x, order, wo, wx):
    here = [((G_TOK, D), BF), ((ROWS_T, D), BF), ((ROWS_T, D), BF), ((ROWS_T, 3 * D), BF)]
    here += [((D, 3 * D), BF), ((ROWS_T, KEYS), F32)]
    return call(
        teacher_kernel, 20, [HBM] + [HERE] * 3, [((G_TOK, D), HERE)], here, [1],
        3 * 10**9, 5 * 10**6, x, order, wo, wx,
    )[0]


ROWS = 24
AXES = ("zh", "yh", "yl", "c", "zlh", "zll", "x")
FSDP = ("zh", "yh", "yl", "c")
SWAP = [(0, 1), (1, 0)]
TOKENS = 169472

beta_one = 0.9
beta_two = 0.999
corr_one = 1.0 - 0.9**10
corr_two = 1.0 - 0.999**10
learn_rate = 0.002
decay_rate = 0.04
momentum = 0.994
adam_eps = 1e-08


def adam_update(weight, teacher_weight, first, second, gradient):
    first = beta_one * first + (1.0 - beta_one) * gradient
    second = beta_two * second + (1.0 - beta_two) * gradient * gradient
    update = first / corr_one / (jnp.sqrt(second / corr_two) + adam_eps)
    weight_new = weight - learn_rate * (update + decay_rate * weight)
    teacher_new = momentum * teacher_weight + (1.0 - momentum) * weight_new
    return (weight_new, teacher_new, first, second)


def exchange(x, axes):
    return lax.all_to_all(x, axes, 0, 0, tiled=True)


def exchange_near(x):
    groups = [[4 * y + 2 * z + (z ^ side) for y in range(4) for z in range(2)] for side in range(2)]
    return lax.all_to_all(x, ("yh", "zh", "zlh"), 0, 0, tiled=True, axis_index_groups=groups)


def spread(x, count):
    return jnp.broadcast_to(x[None], (count,) + x.shape)


def swap(x):
    return lax.ppermute(x, "c", SWAP)


def gather_block(column):
    main = column[:, :4].transpose(1, 0, 2, 3).reshape(4 * SPAN, 128)
    tail = lax.dynamic_slice_in_dim(column[:, 4], lax.axis_index("x") % 2 * 4, 4, axis=0)
    return jnp.concatenate([main, tail.reshape(SPAN // 2, 128)], axis=0)


def by_row(block):
    main = block[: 4 * SPAN].reshape(4, 8, ROWS, 128).transpose(1, 0, 2, 3)
    tail = block[4 * SPAN :].reshape(4, 1, ROWS, 128)
    zero = jnp.zeros_like(tail)
    low = lax.axis_index("x") % 2 == 0
    tail = jnp.concatenate([jnp.where(low, tail, zero), jnp.where(low, zero, tail)], axis=0)
    return jnp.concatenate([main, tail], axis=1)


def join_units(units):
    main = units[:, :4].reshape(16, ROWS, 128)
    tail = units[:, 4].reshape(2, 2, ROWS, 128).sum(axis=1)
    whole = jnp.concatenate([main, tail], axis=0)
    return whole.transpose(1, 0, 2).reshape(ROWS, 3 * D)


def row_order():
    place = jnp.arange(D, dtype=jnp.int32)
    core = lax.axis_index("c").astype(jnp.int32)
    core = jnp.where(place < HALF, core, 1 - core)
    inner = place % HALF
    low, y_high, z_high, row = inner // SPAN, inner % SPAN // 48, inner % 48 // ROWS, inner % ROWS
    return ((((z_high * 4 + y_high) * 2 + low) * 2 + core) * ROWS + row)[None]


def add_up(own, other, first, second):
    total = (own.astype(F32) + swap(other).astype(F32)).astype(BF)
    shares = exchange(total, ("yl", "x"))
    shares, first = lax.optimization_barrier((shares, first))
    total = jnp.sum(shares.astype(F32), axis=0).astype(BF)
    shares = exchange_near(by_row(total))
    shares, second = lax.optimization_barrier((shares, second))
    total = jnp.sum(shares.astype(F32), axis=0).astype(BF)
    shares = exchange(spread(total, 16), ("x", "zlh", "zll"))
    total = jnp.sum(shares.astype(F32).reshape(4, 4, 5, ROWS, 128), axis=1)
    return join_units(total), first, second


def tokens(x):
    return x.transpose(1, 0, 2).reshape(L_ALL, D)


def crops(x):
    return x.reshape(L_ALL // 2, 2, D).transpose(1, 0, 2)


def on_device(
    student_global,
    student_local,
    teacher_global,
    grad_global,
    grad_local,
    student_qkv,
    teacher_qkv,
    first_moment,
    second_moment,
):
    order = row_order()
    place = lax.axis_index("x").astype(jnp.int32)[None]
    columns = exchange_near(cut(place, student_qkv, teacher_qkv))
    local, grad_rows = tokens(student_local), tokens(grad_local)
    shelf = pre(student_global[0], local, grad_global[0], grad_rows, order)
    columns, shelf = lax.optimization_barrier((columns, shelf))
    student_own = exchange(spread(gather_block(columns[:, 0]), 8), ("yl", "x"))
    student_other = swap(student_own)
    shelf, out_g, own_term, other_term = student(shelf, student_own, student_other)
    out_l = shelf[AT_OL : AT_OL + L_ALL]
    teacher_own = exchange(spread(gather_block(columns[:, 1]), 8), ("yl", "x"))
    teacher_other = swap(teacher_own)
    teacher_rows = teacher(teacher_global[0], order, teacher_own, teacher_other)
    back_g, back_l = post(shelf, student_own, student_other, student_global[0], local, order)

    gradient, (back_g, back_l, out_l), teacher_rows = add_up(
        own_term, other_term, (back_g, crops(back_l), crops(out_l)), teacher_rows
    )
    gradient = gradient * (1.0 / jnp.sqrt(jnp.float32(TOKENS)))
    new_student, new_teacher, new_first, new_second = adam_update(
        student_qkv, teacher_qkv, first_moment, second_moment, gradient
    )
    return (
        out_g[None],
        out_l,
        teacher_rows[None],
        back_g[None],
        back_l,
        new_student,
        new_teacher,
        new_first,
        new_second,
    )


def solution(mesh):
    mesh = Mesh(mesh.devices.reshape(2, 4, 2, 2, 2, 2, 4), AXES)
    crop, rows = P(AXES, None, None), P(FSDP, None)
    return jax.shard_map(
        on_device,
        mesh=mesh,
        in_specs=(crop,) * 5 + (rows,) * 4,
        out_specs=(crop,) * 5 + (rows,) * 4,
        check_vma=False,
    )
```

time: 173 us -> 163 us (0.942)
  Pallas kernels: 36.3 us -> 27.7 us
  local copies, waits for them, and re-layouts: 12.5 us -> 10.5 us
  blocking collectives: 49.2 us -> 47.3 us
  other arithmetic: 3.17 us -> 4.99 us
    all_to_all x0 -> x2, starting transfers between devices: none -> 19.9 us  [exchange_near(): lax.all_to_all(x, ('yh', 'zh', 'zlh'), 0, 0, tiled=True, axis_index_group...]
    all_to_all x4 -> x2, waiting for transfers between devices: 31.1 us -> 12 us  [exchange(): return lax.all_to_all(x, axes, 0, 0, tiled=True)]
    all_to_all x4 -> x2, starting transfers between devices: 29.2 us -> 10.4 us  [exchange(): return lax.all_to_all(x, axes, 0, 0, tiled=True)]
    all_to_all x0 -> x2, waiting for transfers between devices: none -> 18.5 us  [exchange_near(): lax.all_to_all(x, ('yh', 'zh', 'zlh'), 0, 0, tiled=True, axis_index_group...]
    unnamed x45 -> x27, local copies, waits for them, and re-layouts: 7.17 us -> 2.64 us
    pallas_call x5, Pallas kernels: 32.2 us -> 27.7 us  [call(): pl.pallas_call(kernel, in_specs=ins, out_specs=[spec for _, spec in outs]...]
    pallas_call x1 -> x0, Pallas kernels: 4.11 us -> none  [add(): pl.pallas_call(add_kernel, grid=(4,), in_specs=[spec, spec], out_specs=sp...]
    all_to_all x2, blocking collectives: 49.2 us -> 47.3 us  [exchange(): return lax.all_to_all(x, axes, 0, 0, tiled=True)]
  transfers between devices with their start and end apart: 7 -> 7, of which waited for: 4 -> 5; matrix products, arithmetic and copies ran while one was open for 4% -> 7% of each run, Pallas kernels for 21% -> 16%
where the time goes in v4:
time: 163 us; the launch traced here: 162 us
  blocking collectives  47.3 us (29%)
  starting transfers between devices  36.4 us (22%)
  waiting for transfers between devices  34 us (21%)
  Pallas kernels  27.7 us (17%)
  local copies, waits for them, and re-layouts  10.5 us (6%)
  other arithmetic  4.99 us (3%)
    all_to_all x2, blocking collectives, exchange(): return lax.all_to_all(x, axes, 0, 0, tiled=True)  47.3 us
    pallas_call x5, Pallas kernels, call(): pl.pallas_call(kernel, in_specs=ins, out_specs=[spec for _, spec in outs]...  27.7 us
    all_to_all x2, starting transfers between devices, exchange_near(): lax.all_to_all(x, ('yh', 'zh', 'zlh'), 0, 0, tiled=True, axis_index_group...  19.9 us
    all_to_all x2, waiting for transfers between devices, exchange_near(): lax.all_to_all(x, ('yh', 'zh', 'zlh'), 0, 0, tiled=True, axis_index_group...  18.5 us
    all_to_all x2, waiting for transfers between devices, exchange(): return lax.all_to_all(x, axes, 0, 0, tiled=True)  12 us
    all_to_all x2, starting transfers between devices, exchange(): return lax.all_to_all(x, axes, 0, 0, tiled=True)  10.4 us
    ppermute x3, starting transfers between devices, swap(): return lax.ppermute(x, 'c', SWAP)  6.17 us
    ppermute x3, waiting for transfers between devices, swap(): return lax.ppermute(x, 'c', SWAP)  3.45 us
  transfers between devices with their start and end apart: 7, of which 5 were waited for; matrix products, arithmetic and copies ran while one was open for 7% of the time, Pallas kernels for 16%

profile of v4, /device:TPU:8, one launch (start us, length us, event | category | flops | bytes accessed | tf_op | source)
XLA Modules:
  0.0 162.1 jit_solution(3227945652061266527)
XLA Ops:
  0.6 0.0 copy-start.11
  0.7 0.0 copy-start.12
  0.7 0.0 copy-start
  0.7 0.0 copy-start.4
  0.7 2.0 %shard_map.160 = bf16[8,2,5,24,128]{4,3,2,1,0:T(8,128)(2,1)} custom-call(s32[1]{0:T(128)} %bitcast.place_ref, f32[24,2304]{1,0:T(8,128)} %sw_ref.1, f32[24,2304]{1,0:T(8,128)} %tw_ref.1), custom_call_target="tpu_custom_call" | custom-call | flops 1000000 | bytes 1000000 | tf_op jit(solution)/shard_map/pallas_call | solution.py:265
  2.7 14.7 %all-to-all-start = ((bf16[8,2,5,24,128]{4,3,2,1,0:T(8,128)(2,1)}), bf16[8,2,5,24,128]{4,3,2,1,0:T(8,128)(2,1)S(1)}, u32[]{:S(2)}, u32[]{:S(2)}) async-start(bf16[8,2,5,24,128]{4,3,2,1,0:T(8,128)(2,1)} %shard_map.160), calls=%async_computation | async-start | bytes 983040 | tf_op jit(solution)/shard_map/all_to_all | solution.py:353
  17.3 0.0 copy-done.11
  17.3 0.2 reshape.275.xl_ref.xl_hbm
  17.5 0.0 copy-start.2
  17.5 0.0 copy-done.12
  17.5 0.2 reshape.276.gl_ref
  17.7 0.1 fusion.order_ref
  17.9 0.0 copy-done
  17.9 0.0 copy-done.4
  17.9 2.2 %shard_map.161.shelf_in = bf16[16384,768]{1,0:T(8,128)(2,1)} custom-call(bf16[257,768]{1,0:T(8,128)(2,1)S(1)} %bitcast.45, bf16[74,768]{1,0:T(8,128)(2,1)S(1)} %reshape.275.xl_ref.xl_hbm, bf16[257,768]{1,0:T(8,128)(2,1)S(1)} %bitcast.47, bf16[74,768]{1,0:T(8,128)(2,1)S(1)} %reshape.276.gl_ref, s32[1,768]{1,0:T(1,128)S(1)} %fusion.order_ref), custom_call_target="tpu_custom_call" | custom-call | flops 1000000000 | bytes 1000000 | tf_op jit(solution)/shard_map/pallas_call | solution.py:265
  20.0 0.0 copy-done.2
  20.1 12.9 %all-to-all-done = bf16[8,2,5,24,128]{4,3,2,1,0:T(8,128)(2,1)S(1)} async-done(((bf16[8,2,5,24,128]{4,3,2,1,0:T(8,128)(2,1)}), bf16[8,2,5,24,128]{4,3,2,1,0:T(8,128)(2,1)S(1)}, u32[]{:S(2)}, u32[]{:S(2)}) %all-to-all-start) | async-done | bytes 491552 | tf_op jit(solution)/shard_map/all_to_all | solution.py:353
  32.9 0.1 slice_bitcast_fusion
  33.1 0.2 broadcast_in_dim.45
  33.4 29.0 %all_to_all.30.wo_ref = bf16[8,864,128]{2,1,0:T(8,128)(2,1)S(1)} all-to-all(bf16[8,864,128]{2,1,0:T(8,128)(2,1)S(1)} %broadcast_in_dim.45), channel_id=1, replica_groups=mesh['zh'=2,'yh'=4,'yl'=2,'c'=2,'zlh'=2,'zll'=2,'x'=4] {'yl','x'}, dimensions={0} | all-to-all | bytes 3538944 | tf_op jit(solution)/shard_map/all_to_all | solution.py:348
  62.3 1.9 %collective-permute-start = (bf16[8,864,128]{2,1,0:T(8,128)(2,1)S(1)}, bf16[8,864,128]{2,1,0:T(8,128)(2,1)S(1)}, u32[]{:S(2)}, u32[]{:S(2)}) collective-permute-start(bf16[8,864,128]{2,1,0:T(8,128)(2,1)S(1)} %all_to_all.30.wo_ref), channel_id=1, source_target_pairs={{0,16},{16,0},{1,17},{17,1},{2,18},{18,2},{3,19},{19,3},{4,20},{20... | collective-permute-start | bytes 5308424 | tf_op jit(solution)/shard_map/ppermute | solution.py:361
  64.3 1.4 broadcast_in_dim.48
  65.7 5.7 %all-to-all-start.4 = ((bf16[8,864,128]{2,1,0:T(8,128)(2,1)}), bf16[8,864,128]{2,1,0:T(8,128)(2,1)}, u32[]{:S(2)}, u32[]{:S(2)}) async-start(bf16[8,864,128]{2,1,0:T(8,128)(2,1)} %broadcast_in_dim.48), calls=%async_computation.4 | async-start | bytes 3538944 | tf_op jit(solution)/shard_map/all_to_all | solution.py:348
  71.4 0.0 collective-permute-done.wx_ref
  71.4 11.5 %shard_map.162 = (bf16[16384,768]{1,0:T(8,128)(2,1)}, bf16[257,768]{1,0:T(8,128)(2,1)}, bf16[8,864,128]{2,1,0:T(8,128)(2,1)S(1)}, bf16[8,864,128]{2,1,0:T(8,128)(2,1)S(1)}) custom-call(bf16[16384,768]{1,0:T(8,128)(2,1)} %shard_map.161.shelf_in, bf16[8,864,128]{2,1,0:T(8,128)(2,1)S(1)} %all_to_all.30.wo_ref, ...), custom_call_target="tpu_custom_call", output_to_operand_aliasing={{0}: (0, {})} | custom-call | flops 8000000000 | bytes 10000000 | tf_op jit(solution)/shard_map/pallas_call | solution.py:265
  82.9 2.1 %collective-permute-start.1 = (bf16[8,864,128]{2,1,0:T(8,128)(2,1)S(1)}, bf16[8,864,128]{2,1,0:T(8,128)(2,1)S(1)}, u32[]{:S(2)}, u32[]{:S(2)}) collective-permute-start(bf16[8,864,128]{2,1,0:T(8,128)(2,1)S(1)} %get-tuple-element.27), channel_id=1, source_target_pairs={{0,16},{16,0},{1,17},{17,1},{2,18},{18,2},{3,19},{19,3},{4,20},{20... | collective-permute-start | bytes 5308424 | tf_op jit(solution)/shard_map/ppermute | solution.py:361
  85.1 3.4 %collective-permute-done.1 = bf16[8,864,128]{2,1,0:T(8,128)(2,1)S(1)} collective-permute-done((bf16[8,864,128]{2,1,0:T(8,128)(2,1)S(1)}, bf16[8,864,128]{2,1,0:T(8,128)(2,1)S(1)}, u32[]{:S(2)}, u32[]{:S(2)}) %collective-permute-start.1) | collective-permute-done | bytes 1769504 | tf_op jit(solution)/shard_map/ppermute | solution.py:361
  88.5 1.8 %add_convert_fusion = bf16[8,864,128]{2,1,0:T(8,128)(2,1)} fusion(bf16[8,864,128]{2,1,0:T(8,128)(2,1)S(1)} %collective-permute-done.1, bf16[8,864,128]{2,1,0:T(8,128)(2,1)S(1)} %get-tuple-element.26), kind=kLoop, calls=%fused_computation | loop fusion | flops 3538944 | bytes 5308416 | tf_op jit(solution)/shard_map/convert_element_type | solution.py:396
  90.3 4.1 %all-to-all-done.4.wo_ref = bf16[8,864,128]{2,1,0:T(8,128)(2,1)} async-done(((bf16[8,864,128]{2,1,0:T(8,128)(2,1)}), bf16[8,864,128]{2,1,0:T(8,128)(2,1)}, u32[]{:S(2)}, u32[]{:S(2)}) %all-to-all-start.4) | async-done | bytes 1769504 | tf_op jit(solution)/shard_map/all_to_all | solution.py:348
  94.4 4.8 %all-to-all-start.2 = ((bf16[8,864,128]{2,1,0:T(8,128)(2,1)}), bf16[8,864,128]{2,1,0:T(8,128)(2,1)}, u32[]{:S(2)}, u32[]{:S(2)}) async-start(bf16[8,864,128]{2,1,0:T(8,128)(2,1)} %add_convert_fusion), calls=%async_computation.2 | async-start | bytes 3538944 | tf_op jit(solution)/shard_map/all_to_all | solution.py:348
  99.2 2.1 %collective-permute-start.2 = (bf16[8,864,128]{2,1,0:T(8,128)(2,1)}, bf16[8,864,128]{2,1,0:T(8,128)(2,1)}, u32[]{:S(2)}, u32[]{:S(2)}) collective-permute-start(bf16[8,864,128]{2,1,0:T(8,128)(2,1)} %all-to-all-done.4.wo_ref), channel_id=1, source_target_pairs={{0,16},{16,0},{1,17},{17,1},{2,18},{18,2},{3,19},{19,3},{4,20},{20... | collective-permute-start | bytes 5308424 | tf_op jit(solution)/shard_map/ppermute | solution.py:361
  101.3 1.6 slice.36
  102.9 0.0 copy-start.1
  102.9 1.0 copy-done.1
  103.9 0.0 copy-start.3
  103.9 0.9 copy-done.3
  104.8 4.9 %shard_map.163 = (bf16[257,768]{1,0:T(8,128)(2,1)}, bf16[74,768]{1,0:T(8,128)(2,1)S(1)}) custom-call(bf16[16384,768]{1,0:T(8,128)(2,1)} %get-tuple-element.28.shelf, bf16[257,768]{1,0:T(8,128)(2,1)S(1)} %bitcast.46, bf16[74,768]{1,0:T(8,128)(2,1)S(1)} %copy-done.3, bf16[8,864,128]{2,1,0:T(8,128)(2,1)S(1)} %all_to_all.30.wo_ref, ...), custom_call_target="tpu_custom_call" | custom-call | flops 3000000000 | bytes 6000000 | tf_op jit(solution)/shard_map/pallas_call | solution.py:265
  109.7 0.0 copy-start.5
  109.7 0.6 copy-done.5
  110.3 1.7 %reshape.279 = bf16[37,2,768]{2,1,0:T(2,128)(2,1)} reshape(bf16[74,768]{1,0:T(8,128)(2,1)} %copy-done.5) | data formatting | bytes 227328 | tf_op jit(solution)/shard_map/reshape | solution.py:413
  112.0 1.7 %reshape.280 = bf16[37,2,768]{2,1,0:T(2,128)(2,1)} reshape(bf16[74,768]{1,0:T(8,128)(2,1)} %slice.36) | data formatting | bytes 227328 | tf_op jit(solution)/shard_map/reshape | solution.py:413
  113.6 7.9 %all-to-all-done.2 = bf16[8,864,128]{2,1,0:T(8,128)(2,1)} async-done(((bf16[8,864,128]{2,1,0:T(8,128)(2,1)}), bf16[8,864,128]{2,1,0:T(8,128)(2,1)}, u32[]{:S(2)}, u32[]{:S(2)}) %all-to-all-start.2) | async-done | bytes 1769504 | tf_op jit(solution)/shard_map/all_to_all | solution.py:348
  121.5 0.0 copy-start.6
  121.5 1.8 %reduce_sum.42 = bf16[864,128]{1,0:T(8,128)(2,1)S(1)} reduce(bf16[8,864,128]{2,1,0:T(8,128)(2,1)} %all-to-all-done.2, bf16[]{:T(256)} %constant.109.clone.1), dimensions={0}, to_apply=%region_0.1 | reduce | flops 774144 | bytes 1990658 | tf_op jit(solution)/shard_map/reduce_sum | solution.py:399
  123.4 0.7 copy.31
  124.1 5.2 %all-to-all-start.3 = ((bf16[8,5,24,128]{3,2,1,0:T(8,128)(2,1)}), bf16[8,5,24,128]{3,2,1,0:T(8,128)(2,1)S(1)}, u32[]{:S(2)}, u32[]{:S(2)}) async-start(bf16[8,5,24,128]{3,2,1,0:T(8,128)(2,1)} %copy.31), calls=%async_computation.3 | async-start | bytes 491520 | tf_op jit(solution)/shard_map/all_to_all | solution.py:353
  129.3 0.0 collective-permute-done.2.wx_ref
  129.3 0.0 copy-done.6
  129.4 7.2 %shard_map.164 = bf16[257,768]{1,0:T(8,128)(2,1)} custom-call(bf16[257,768]{1,0:T(8,128)(2,1)S(1)} %bitcast.48, s32[1,768]{1,0:T(1,128)S(1)} %fusion.order_ref, bf16[8,864,128]{2,1,0:T(8,128)(2,1)} %all-to-all-done.4.wo_ref, bf16[8,864,128]{2,1,0:T(8,128)(2,1)} %collective-permute-done.2.wx_ref), custom_call_target="tpu_custom_call" | custom-call | flops 3000000000 | bytes 5000000 | tf_op jit(solution)/shard_map/pallas_call | solution.py:265
  136.6 5.7 %all-to-all-done.3 = bf16[8,5,24,128]{3,2,1,0:T(8,128)(2,1)S(1)} async-done(((bf16[8,5,24,128]{3,2,1,0:T(8,128)(2,1)}), bf16[8,5,24,128]{3,2,1,0:T(8,128)(2,1)S(1)}, u32[]{:S(2)}, u32[]{:S(2)}) %all-to-all-start.3) | async-done | bytes 245792 | tf_op jit(solution)/shard_map/all_to_all | solution.py:353
  142.3 0.1 broadcast_in_dim.51
  142.3 0.0 copy-start.7
  142.4 0.0 copy-start.8
  142.4 0.0 copy-start.9
  142.4 0.0 copy-start.10
  142.4 18.4 %all_to_all.31 = bf16[16,5,24,128]{3,2,1,0:T(8,128)(2,1)S(1)} all-to-all(bf16[16,5,24,128]{3,2,1,0:T(8,128)(2,1)S(1)} %broadcast_in_dim.51), channel_id=1, replica_groups=mesh['zh'=2,'yh'=4,'yl'=2,'c'=2,'zlh'=2,'zll'=2,'x'=4] {'x','zlh','zll'}, dimensions={0} | all-to-all | bytes 983040 | tf_op jit(solution)/shard_map/all_to_all | solution.py:348
  160.7 0.1 convert_reduce_fusion
  160.9 0.1 multiply_multiply_fusion
  161.0 0.0 copy-done.7
  161.0 0.0 copy-done.8
  161.0 0.0 copy-done.9
  161.0 0.0 copy-done.10
  161.0 1.1 multiply_add_fusion
  (17 shorter events, 0.3 us)
Async XLA Ops:
  0.6 16.7 %copy-start.11 = (bf16[2,37,768]{2,0,1:T(2,128)(2,1)S(1)}, bf16[2,37,768]{2,0,1:T(2,128)(2,1)}, u32[]{:S(2)}) copy-start(bf16[2,37,768]{2,0,1:T(2,128)(2,1)} %param.10) | copy-start | bytes 340996
  0.7 16.9 %copy-start.12 = (bf16[2,37,768]{2,0,1:T(2,128)(2,1)S(1)}, bf16[2,37,768]{2,0,1:T(2,128)(2,1)}, u32[]{:S(2)}) copy-start(bf16[2,37,768]{2,0,1:T(2,128)(2,1)} %param.13) | copy-start | bytes 340996
  0.7 17.2 %copy-start = (bf16[1,257,768]{2,1,0:T(8,128)(2,1)S(1)}, bf16[1,257,768]{2,1,0:T(8,128)(2,1)}, u32[]{:S(2)}) copy-start(bf16[1,257,768]{2,1,0:T(8,128)(2,1)} %param.9) | copy-start | bytes 1184260
  0.7 17.2 %copy-start.4 = (bf16[1,257,768]{2,1,0:T(8,128)(2,1)S(1)}, bf16[1,257,768]{2,1,0:T(8,128)(2,1)}, u32[]{:S(2)}) copy-start(bf16[1,257,768]{2,1,0:T(8,128)(2,1)} %param.12) | copy-start | bytes 1184260
  2.7 30.2 %all-to-all-start = ((bf16[8,2,5,24,128]{4,3,2,1,0:T(8,128)(2,1)}), bf16[8,2,5,24,128]{4,3,2,1,0:T(8,128)(2,1)S(1)}, u32[]{:S(2)}, u32[]{:S(2)}) async-start(bf16[8,2,5,24,128]{4,3,2,1,0:T(8,128)(2,1)} %shard_map.160), calls=%async_computation | async-start | bytes 983040 | tf_op jit(solution)/shard_map/all_to_all | solution.py:353
  17.5 2.5 %copy-start.2 = (bf16[74,768]{1,0:T(8,128)(2,1)}, bf16[74,768]{1,0:T(8,128)(2,1)S(1)}, u32[]{:S(2)}) copy-start(bf16[74,768]{1,0:T(8,128)(2,1)S(1)} %reshape.275.xl_ref.xl_hbm) | copy-start | bytes 340996
  62.3 9.1 %collective-permute-start = (bf16[8,864,128]{2,1,0:T(8,128)(2,1)S(1)}, bf16[8,864,128]{2,1,0:T(8,128)(2,1)S(1)}, u32[]{:S(2)}, u32[]{:S(2)}) collective-permute-start(bf16[8,864,128]{2,1,0:T(8,128)(2,1)S(1)} %all_to_all.30.wo_ref), channel_id=1, source_target_pairs={{0,16},{16,0},{1,17},{17,1},{2,18},{18,2},{3,19},{19,3},{4,20},{20... | collective-permute-start | bytes 5308424 | tf_op jit(solution)/shard_map/ppermute | solution.py:361
  65.7 28.7 %all-to-all-start.4 = ((bf16[8,864,128]{2,1,0:T(8,128)(2,1)}), bf16[8,864,128]{2,1,0:T(8,128)(2,1)}, u32[]{:S(2)}, u32[]{:S(2)}) async-start(bf16[8,864,128]{2,1,0:T(8,128)(2,1)} %broadcast_in_dim.48), calls=%async_computation.4 | async-start | bytes 3538944 | tf_op jit(solution)/shard_map/all_to_all | solution.py:348
  82.9 5.6 %collective-permute-start.1 = (bf16[8,864,128]{2,1,0:T(8,128)(2,1)S(1)}, bf16[8,864,128]{2,1,0:T(8,128)(2,1)S(1)}, u32[]{:S(2)}, u32[]{:S(2)}) collective-permute-start(bf16[8,864,128]{2,1,0:T(8,128)(2,1)S(1)} %get-tuple-element.27), channel_id=1, source_target_pairs={{0,16},{16,0},{1,17},{17,1},{2,18},{18,2},{3,19},{19,3},{4,20},{20... | collective-permute-start | bytes 5308424 | tf_op jit(solution)/shard_map/ppermute | solution.py:361
  94.4 27.1 %all-to-all-start.2 = ((bf16[8,864,128]{2,1,0:T(8,128)(2,1)}), bf16[8,864,128]{2,1,0:T(8,128)(2,1)}, u32[]{:S(2)}, u32[]{:S(2)}) async-start(bf16[8,864,128]{2,1,0:T(8,128)(2,1)} %add_convert_fusion), calls=%async_computation.2 | async-start | bytes 3538944 | tf_op jit(solution)/shard_map/all_to_all | solution.py:348
  99.2 30.2 %collective-permute-start.2 = (bf16[8,864,128]{2,1,0:T(8,128)(2,1)}, bf16[8,864,128]{2,1,0:T(8,128)(2,1)}, u32[]{:S(2)}, u32[]{:S(2)}) collective-permute-start(bf16[8,864,128]{2,1,0:T(8,128)(2,1)} %all-to-all-done.4.wo_ref), channel_id=1, source_target_pairs={{0,16},{16,0},{1,17},{17,1},{2,18},{18,2},{3,19},{19,3},{4,20},{20... | collective-permute-start | bytes 5308424 | tf_op jit(solution)/shard_map/ppermute | solution.py:361
  102.9 1.0 copy-start.1
  103.9 0.9 copy-start.3
  109.7 0.7 copy-start.5
  121.5 7.8 %copy-start.6 = (bf16[1,257,768]{2,1,0:T(8,128)(2,1)S(1)}, bf16[1,257,768]{2,1,0:T(8,128)(2,1)}, u32[]{:S(2)}) copy-start(bf16[1,257,768]{2,1,0:T(8,128)(2,1)} %param.11) | copy-start | bytes 1184260
  124.1 18.1 %all-to-all-start.3 = ((bf16[8,5,24,128]{3,2,1,0:T(8,128)(2,1)}), bf16[8,5,24,128]{3,2,1,0:T(8,128)(2,1)S(1)}, u32[]{:S(2)}, u32[]{:S(2)}) async-start(bf16[8,5,24,128]{3,2,1,0:T(8,128)(2,1)} %copy.31), calls=%async_computation.3 | async-start | bytes 491520 | tf_op jit(solution)/shard_map/all_to_all | solution.py:353
  142.3 18.7 %copy-start.7 = (f32[24,2304]{1,0:T(8,128)S(1)}, f32[24,2304]{1,0:T(8,128)}, u32[]{:S(2)}) copy-start(f32[24,2304]{1,0:T(8,128)} %sw_ref.1) | copy-start | bytes 663556
  142.4 18.7 %copy-start.8 = (f32[24,2304]{1,0:T(8,128)S(1)}, f32[24,2304]{1,0:T(8,128)}, u32[]{:S(2)}) copy-start(f32[24,2304]{1,0:T(8,128)} %tw_ref.1) | copy-start | bytes 663556
  142.4 18.7 %copy-start.9 = (f32[24,2304]{1,0:T(8,128)S(1)}, f32[24,2304]{1,0:T(8,128)}, u32[]{:S(2)}) copy-start(f32[24,2304]{1,0:T(8,128)} %param.16) | copy-start | bytes 663556
  142.4 18.7 %copy-start.10 = (f32[24,2304]{1,0:T(8,128)S(1)}, f32[24,2304]{1,0:T(8,128)}, u32[]{:S(2)}) copy-start(f32[24,2304]{1,0:T(8,128)} %param.17) | copy-start | bytes 663556

commit v5 on v4

--- a/solution.py
+++ b/solution.py
@@ -133,8 +133,8 @@
 
 def student_kernel(
     shelf_in, wo_ref, wx_ref,
-    shelf, og_hbm, dwo_ref, dwx_ref,
-    n_ref, do_scr, nt_ref, og_ref, ol_ref, dp_ref,
+    shelf, og_ref, dwo_ref, dwx_ref,
+    n_ref, do_scr, nt_ref, ol_ref, dp_ref,
     p_scr, w_scr, bias_scr, sem,
 ):
     loads = copies(
@@ -184,7 +184,7 @@
         dp_ref[:, at[1]] = jnp.where(first, dk[:ROWS_S], dk[KEYS : KEYS + ROWS_S]).astype(jnp.bfloat16)
         dp_ref[:, at[2]] = jnp.where(first, dv[:ROWS_S], dv[KEYS : KEYS + ROWS_S]).astype(jnp.bfloat16)
 
-    pairs = [(og_ref, og_hbm), (ol_ref, shelf.at[pl.ds(AT_OL, 80), :])]
+    pairs = [(ol_ref, shelf.at[pl.ds(AT_OL, 80), :])]
     pairs += [
         (dp_ref.at[:, pl.ds(i * D, D)], shelf.at[pl.ds(AT_DP + i * ROWS_S, ROWS_S), :]) for i in range(3)
     ]
@@ -208,13 +208,13 @@
 
 
 def post_kernel(
-    shelf, xg_hbm, xl_hbm, wo_ref, wx_ref, order_ref, bg_hbm, bl_hbm,
-    dp_ref, xg_ref, xl_ref, bg_ref, bl_ref, w_scr, sem,
+    shelf, xg_ref, xl_ref, wo_ref, wx_ref, order_ref, bg_ref, bl_ref,
+    dp_ref, w_scr, sem,
 ):
     pairs = [
         (shelf.at[pl.ds(AT_DP + i * ROWS_S, ROWS_S), :], dp_ref.at[:, pl.ds(i * D, D)]) for i in range(3)
     ]
-    loads = copies(pairs + [(xg_hbm, xg_ref), (xl_hbm, xl_ref)], sem)
+    loads = copies(pairs, sem)
     start(loads)
     assemble(wo_ref, 0, w_scr)
     assemble(wx_ref, HALF, w_scr)
@@ -227,19 +227,13 @@
         mean = jnp.mean(d, axis=-1, keepdims=True)
         along = jnp.mean(d * hat, axis=-1, keepdims=True)
         out_ref[...] = (scale * (d - mean - hat * along)).astype(jnp.bfloat16)
-    stores = copies([(bg_ref, bg_hbm), (bl_ref, bl_hbm)], sem)
-    start(stores)
-    wait(stores)
-
-
-def teacher_kernel(x_hbm, order_ref, wo_ref, wx_ref, o_ref, x_ref, n_scr, scr, p_scr, w_scr, bias_scr, sem):
-    loads = copies([(x_hbm, x_ref)], sem)
-    start(loads)
+
+
+def teacher_kernel(x_ref, order_ref, wo_ref, wx_ref, o_ref, n_scr, scr, p_scr, w_scr, bias_scr):
     assemble(wo_ref, 0, w_scr)
     assemble(wx_ref, HALF, w_scr)
     bias_scr[...] = bias_of((ROWS_T, KEYS), 1)
     scr[...] = jnp.zeros_like(scr)
-    wait(loads)
     scr[:G_TOK, :] = normalize(x_ref[...])[0].astype(jnp.bfloat16)
     n_scr[...] = dot(scr[...], one_hot(order_ref), NN).astype(jnp.bfloat16)
     project(n_scr, w_scr, p_scr)
@@ -292,8 +286,8 @@
 
 def student(shelf, wo, wx):
     block = (8, BLOCK, 128)
-    outs = [(SHELF_SHAPE, HBM), ((G_TOK, D), HBM), (block, HERE), (block, HERE)]
-    here = [(ROWS_S, D), (ROWS_S, D), (D, KEYS), (G_TOK, D), (80, D)]
+    outs = [(SHELF_SHAPE, HBM), ((G_TOK, D), HERE), (block, HERE), (block, HERE)]
+    here = [(ROWS_S, D), (ROWS_S, D), (D, KEYS), (80, D)]
     here += [(ROWS_S, 3 * D), (ROWS_S, 3 * D), (D, 3 * D)]
     return call(
         student_kernel, 42, [HBM, HERE, HERE], outs, [(s, BF) for s in here] + [((KEYS, ROWS_S), F32)], [5],
@@ -302,19 +296,19 @@
 
 
 def post(shelf, wo, wx, xg, xl, order):
-    outs = [((G_TOK, D), HBM), ((L_ALL, D), HBM)]
-    here = [((ROWS_S, 3 * D), BF)] + [((G_TOK, D), BF), ((L_ALL, D), BF)] * 2 + [((D, 3 * D), BF)]
+    outs = [((G_TOK, D), HERE), ((L_ALL, D), HERE)]
+    here = [((ROWS_S, 3 * D), BF), ((D, 3 * D), BF)]
     return call(
-        post_kernel, 42, [HBM] * 3 + [HERE] * 3, outs, here, [5],
+        post_kernel, 42, [HBM] + [HERE] * 5, outs, here, [5],
         3 * 10**9, 6 * 10**6, shelf, xg, xl, wo, wx, order,
     )
 
 
 def teacher(x, order, wo, wx):
-    here = [((G_TOK, D), BF), ((ROWS_T, D), BF), ((ROWS_T, D), BF), ((ROWS_T, 3 * D), BF)]
+    here = [((ROWS_T, D), BF), ((ROWS_T, D), BF), ((ROWS_T, 3 * D), BF)]
     here += [((D, 3 * D), BF), ((ROWS_T, KEYS), F32)]
     return call(
-        teacher_kernel, 20, [HBM] + [HERE] * 3, [((G_TOK, D), HERE)], here, [1],
+        teacher_kernel, 20, [HERE] * 4, [((G_TOK, D), HERE)], here, [],
         3 * 10**9, 5 * 10**6, x, order, wo, wx,
     )[0]
 

time: 163 us -> 163 us (level)
  no operation moved by 1% of the time
where the time goes in v5:
time: 163 us; the launch traced here: 162 us
  blocking collectives  47.3 us (29%)
  starting transfers between devices  36.4 us (22%)
  waiting for transfers between devices  34.1 us (21%)
  Pallas kernels  27.7 us (17%)
  local copies, waits for them, and re-layouts  10.5 us (6%)
  other arithmetic  4.99 us (3%)
    all_to_all x2, blocking collectives, exchange(): return lax.all_to_all(x, axes, 0, 0, tiled=True)  47.3 us
    pallas_call x5, Pallas kernels, call(): pl.pallas_call(kernel, in_specs=ins, out_specs=[spec for _, spec in outs]...  27.7 us
    all_to_all x2, starting transfers between devices, exchange_near(): lax.all_to_all(x, ('yh', 'zh', 'zlh'), 0, 0, tiled=True, axis_index_group...  19.9 us
    all_to_all x2, waiting for transfers between devices, exchange_near(): lax.all_to_all(x, ('yh', 'zh', 'zlh'), 0, 0, tiled=True, axis_index_group...  19.4 us
    all_to_all x2, waiting for transfers between devices, exchange(): return lax.all_to_all(x, axes, 0, 0, tiled=True)  11.3 us
    all_to_all x2, starting transfers between devices, exchange(): return lax.all_to_all(x, axes, 0, 0, tiled=True)  10.4 us
    ppermute x3, starting transfers between devices, swap(): return lax.ppermute(x, 'c', SWAP)  6.17 us
    ppermute x3, waiting for transfers between devices, swap(): return lax.ppermute(x, 'c', SWAP)  3.45 us
  transfers between devices with their start and end apart: 7, of which 5 were waited for; matrix products, arithmetic and copies ran while one was open for 7% of the time, Pallas kernels for 16%

profile of v5, /device:TPU:8, one launch (start us, length us, event | category | flops | bytes accessed | tf_op | source)
XLA Modules:
  0.0 162.1 jit_solution(16813148266372436408)
XLA Ops:
  0.6 0.0 copy-start.11
  0.7 0.0 copy-start.12
  0.7 0.0 copy-start
  0.7 0.0 copy-start.4
  0.7 2.0 %shard_map.160 = bf16[8,2,5,24,128]{4,3,2,1,0:T(8,128)(2,1)} custom-call(s32[1]{0:T(128)} %bitcast.place_ref, f32[24,2304]{1,0:T(8,128)} %sw_ref.1, f32[24,2304]{1,0:T(8,128)} %tw_ref.1), custom_call_target="tpu_custom_call" | custom-call | flops 1000000 | bytes 1000000 | tf_op jit(solution)/shard_map/pallas_call | solution.py:259
  2.7 14.7 %all-to-all-start = ((bf16[8,2,5,24,128]{4,3,2,1,0:T(8,128)(2,1)}), bf16[8,2,5,24,128]{4,3,2,1,0:T(8,128)(2,1)S(1)}, u32[]{:S(2)}, u32[]{:S(2)}) async-start(bf16[8,2,5,24,128]{4,3,2,1,0:T(8,128)(2,1)} %shard_map.160), calls=%async_computation | async-start | bytes 983040 | tf_op jit(solution)/shard_map/all_to_all | solution.py:347
  17.3 0.0 copy-done.11
  17.3 0.2 reshape.275.xl_ref
  17.5 0.0 copy-start.2
  17.5 0.0 copy-done.12
  17.5 0.2 reshape.276.gl_ref
  17.7 0.1 fusion.order_ref
  17.9 0.0 copy-done
  17.9 0.0 copy-done.4
  17.9 2.2 %shard_map.161.shelf_in = bf16[16384,768]{1,0:T(8,128)(2,1)} custom-call(bf16[257,768]{1,0:T(8,128)(2,1)S(1)} %bitcast.45, bf16[74,768]{1,0:T(8,128)(2,1)S(1)} %reshape.275.xl_ref, bf16[257,768]{1,0:T(8,128)(2,1)S(1)} %bitcast.47, bf16[74,768]{1,0:T(8,128)(2,1)S(1)} %reshape.276.gl_ref, s32[1,768]{1,0:T(1,128)S(1)} %fusion.order_ref), custom_call_target="tpu_custom_call" | custom-call | flops 1000000000 | bytes 1000000 | tf_op jit(solution)/shard_map/pallas_call | solution.py:259
  20.0 0.0 copy-done.2
  20.1 12.9 %all-to-all-done = bf16[8,2,5,24,128]{4,3,2,1,0:T(8,128)(2,1)S(1)} async-done(((bf16[8,2,5,24,128]{4,3,2,1,0:T(8,128)(2,1)}), bf16[8,2,5,24,128]{4,3,2,1,0:T(8,128)(2,1)S(1)}, u32[]{:S(2)}, u32[]{:S(2)}) %all-to-all-start) | async-done | bytes 491552 | tf_op jit(solution)/shard_map/all_to_all | solution.py:347
  32.9 0.1 slice_bitcast_fusion
  33.1 0.2 broadcast_in_dim.45
  33.4 29.0 %all_to_all.30.wo_ref = bf16[8,864,128]{2,1,0:T(8,128)(2,1)S(1)} all-to-all(bf16[8,864,128]{2,1,0:T(8,128)(2,1)S(1)} %broadcast_in_dim.45), channel_id=1, replica_groups=mesh['zh'=2,'yh'=4,'yl'=2,'c'=2,'zlh'=2,'zll'=2,'x'=4] {'yl','x'}, dimensions={0} | all-to-all | bytes 3538944 | tf_op jit(solution)/shard_map/all_to_all | solution.py:342
  62.3 1.9 %collective-permute-start = (bf16[8,864,128]{2,1,0:T(8,128)(2,1)S(1)}, bf16[8,864,128]{2,1,0:T(8,128)(2,1)S(1)}, u32[]{:S(2)}, u32[]{:S(2)}) collective-permute-start(bf16[8,864,128]{2,1,0:T(8,128)(2,1)S(1)} %all_to_all.30.wo_ref), channel_id=1, source_target_pairs={{0,16},{16,0},{1,17},{17,1},{2,18},{18,2},{3,19},{19,3},{4,20},{20... | collective-permute-start | bytes 5308424 | tf_op jit(solution)/shard_map/ppermute | solution.py:355
  64.3 1.4 broadcast_in_dim.48
  65.7 5.7 %all-to-all-start.4 = ((bf16[8,864,128]{2,1,0:T(8,128)(2,1)}), bf16[8,864,128]{2,1,0:T(8,128)(2,1)}, u32[]{:S(2)}, u32[]{:S(2)}) async-start(bf16[8,864,128]{2,1,0:T(8,128)(2,1)} %broadcast_in_dim.48), calls=%async_computation.4 | async-start | bytes 3538944 | tf_op jit(solution)/shard_map/all_to_all | solution.py:342
  71.4 0.0 collective-permute-done.wx_ref
  71.4 12.3 %shard_map.162 = (bf16[16384,768]{1,0:T(8,128)(2,1)}, bf16[257,768]{1,0:T(8,128)(2,1)}, bf16[8,864,128]{2,1,0:T(8,128)(2,1)S(1)}, bf16[8,864,128]{2,1,0:T(8,128)(2,1)S(1)}) custom-call(bf16[16384,768]{1,0:T(8,128)(2,1)} %shard_map.161.shelf_in, bf16[8,864,128]{2,1,0:T(8,128)(2,1)S(1)} %all_to_all.30.wo_ref, ...), custom_call_target="tpu_custom_call", output_to_operand_aliasing={{0}: (0, {})} | custom-call | flops 8000000000 | bytes 10000000 | tf_op jit(solution)/shard_map/pallas_call | solution.py:259
  83.7 2.1 %collective-permute-start.1 = (bf16[8,864,128]{2,1,0:T(8,128)(2,1)S(1)}, bf16[8,864,128]{2,1,0:T(8,128)(2,1)S(1)}, u32[]{:S(2)}, u32[]{:S(2)}) collective-permute-start(bf16[8,864,128]{2,1,0:T(8,128)(2,1)S(1)} %get-tuple-element.27), channel_id=1, source_target_pairs={{0,16},{16,0},{1,17},{17,1},{2,18},{18,2},{3,19},{19,3},{4,20},{20... | collective-permute-start | bytes 5308424 | tf_op jit(solution)/shard_map/ppermute | solution.py:355
  85.8 3.4 %collective-permute-done.1 = bf16[8,864,128]{2,1,0:T(8,128)(2,1)S(1)} collective-permute-done((bf16[8,864,128]{2,1,0:T(8,128)(2,1)S(1)}, bf16[8,864,128]{2,1,0:T(8,128)(2,1)S(1)}, u32[]{:S(2)}, u32[]{:S(2)}) %collective-permute-start.1) | collective-permute-done | bytes 1769504 | tf_op jit(solution)/shard_map/ppermute | solution.py:355
  89.2 1.8 %add_convert_fusion = bf16[8,864,128]{2,1,0:T(8,128)(2,1)} fusion(bf16[8,864,128]{2,1,0:T(8,128)(2,1)S(1)} %collective-permute-done.1, bf16[8,864,128]{2,1,0:T(8,128)(2,1)S(1)} %get-tuple-element.26), kind=kLoop, calls=%fused_computation | loop fusion | flops 3538944 | bytes 5308416 | tf_op jit(solution)/shard_map/convert_element_type | solution.py:390
  91.0 3.4 %all-to-all-done.4.wo_ref = bf16[8,864,128]{2,1,0:T(8,128)(2,1)} async-done(((bf16[8,864,128]{2,1,0:T(8,128)(2,1)}), bf16[8,864,128]{2,1,0:T(8,128)(2,1)}, u32[]{:S(2)}, u32[]{:S(2)}) %all-to-all-start.4) | async-done | bytes 1769504 | tf_op jit(solution)/shard_map/all_to_all | solution.py:342
  94.4 4.8 %all-to-all-start.2 = ((bf16[8,864,128]{2,1,0:T(8,128)(2,1)}), bf16[8,864,128]{2,1,0:T(8,128)(2,1)}, u32[]{:S(2)}, u32[]{:S(2)}) async-start(bf16[8,864,128]{2,1,0:T(8,128)(2,1)} %add_convert_fusion), calls=%async_computation.2 | async-start | bytes 3538944 | tf_op jit(solution)/shard_map/all_to_all | solution.py:342
  99.2 2.1 %collective-permute-start.2 = (bf16[8,864,128]{2,1,0:T(8,128)(2,1)}, bf16[8,864,128]{2,1,0:T(8,128)(2,1)}, u32[]{:S(2)}, u32[]{:S(2)}) collective-permute-start(bf16[8,864,128]{2,1,0:T(8,128)(2,1)} %all-to-all-done.4.wo_ref), channel_id=1, source_target_pairs={{0,16},{16,0},{1,17},{17,1},{2,18},{18,2},{3,19},{19,3},{4,20},{20... | collective-permute-start | bytes 5308424 | tf_op jit(solution)/shard_map/ppermute | solution.py:355
  101.3 1.6 slice.36
  102.9 0.0 copy-start.1
  102.9 1.0 copy-done.1
  103.9 0.0 copy-start.3
  103.9 0.9 copy-done.3
  104.8 4.9 %shard_map.163 = (bf16[257,768]{1,0:T(8,128)(2,1)}, bf16[74,768]{1,0:T(8,128)(2,1)S(1)}) custom-call(bf16[16384,768]{1,0:T(8,128)(2,1)} %get-tuple-element.28.shelf, bf16[257,768]{1,0:T(8,128)(2,1)S(1)} %bitcast.46, bf16[74,768]{1,0:T(8,128)(2,1)S(1)} %copy-done.3, bf16[8,864,128]{2,1,0:T(8,128)(2,1)S(1)} %all_to_all.30.wo_ref, ...), custom_call_target="tpu_custom_call" | custom-call | flops 3000000000 | bytes 6000000 | tf_op jit(solution)/shard_map/pallas_call | solution.py:259
  109.7 0.0 copy-start.5
  109.7 0.6 copy-done.5
  110.3 1.7 %reshape.279 = bf16[37,2,768]{2,1,0:T(2,128)(2,1)} reshape(bf16[74,768]{1,0:T(8,128)(2,1)} %copy-done.5) | data formatting | bytes 227328 | tf_op jit(solution)/shard_map/reshape | solution.py:407
  112.0 1.7 %reshape.280 = bf16[37,2,768]{2,1,0:T(2,128)(2,1)} reshape(bf16[74,768]{1,0:T(8,128)(2,1)} %slice.36) | data formatting | bytes 227328 | tf_op jit(solution)/shard_map/reshape | solution.py:407
  113.7 7.9 %all-to-all-done.2 = bf16[8,864,128]{2,1,0:T(8,128)(2,1)} async-done(((bf16[8,864,128]{2,1,0:T(8,128)(2,1)}), bf16[8,864,128]{2,1,0:T(8,128)(2,1)}, u32[]{:S(2)}, u32[]{:S(2)}) %all-to-all-start.2) | async-done | bytes 1769504 | tf_op jit(solution)/shard_map/all_to_all | solution.py:342
  121.5 0.0 copy-start.6
  121.5 1.8 %reduce_sum.42 = bf16[864,128]{1,0:T(8,128)(2,1)S(1)} reduce(bf16[8,864,128]{2,1,0:T(8,128)(2,1)} %all-to-all-done.2, bf16[]{:T(256)} %constant.109.clone.1), dimensions={0}, to_apply=%region_0.1 | reduce | flops 774144 | bytes 1990658 | tf_op jit(solution)/shard_map/reduce_sum | solution.py:393
  123.4 0.7 copy.31
  124.1 5.2 %all-to-all-start.3 = ((bf16[8,5,24,128]{3,2,1,0:T(8,128)(2,1)}), bf16[8,5,24,128]{3,2,1,0:T(8,128)(2,1)S(1)}, u32[]{:S(2)}, u32[]{:S(2)}) async-start(bf16[8,5,24,128]{3,2,1,0:T(8,128)(2,1)} %copy.31), calls=%async_computation.3 | async-start | bytes 491520 | tf_op jit(solution)/shard_map/all_to_all | solution.py:347
  129.3 0.0 collective-permute-done.2.wx_ref
  129.3 0.0 copy-done.6
  129.4 6.4 %shard_map.164 = bf16[257,768]{1,0:T(8,128)(2,1)} custom-call(bf16[257,768]{1,0:T(8,128)(2,1)S(1)} %bitcast.48, s32[1,768]{1,0:T(1,128)S(1)} %fusion.order_ref, bf16[8,864,128]{2,1,0:T(8,128)(2,1)} %all-to-all-done.4.wo_ref, bf16[8,864,128]{2,1,0:T(8,128)(2,1)} %collective-permute-done.2.wx_ref), custom_call_target="tpu_custom_call" | custom-call | flops 3000000000 | bytes 5000000 | tf_op jit(solution)/shard_map/pallas_call | solution.py:259
  135.7 6.5 %all-to-all-done.3 = bf16[8,5,24,128]{3,2,1,0:T(8,128)(2,1)S(1)} async-done(((bf16[8,5,24,128]{3,2,1,0:T(8,128)(2,1)}), bf16[8,5,24,128]{3,2,1,0:T(8,128)(2,1)S(1)}, u32[]{:S(2)}, u32[]{:S(2)}) %all-to-all-start.3) | async-done | bytes 245792 | tf_op jit(solution)/shard_map/all_to_all | solution.py:347
  142.3 0.1 broadcast_in_dim.51
  142.3 0.0 copy-start.7
  142.4 0.0 copy-start.8
  142.4 0.0 copy-start.9
  142.4 0.0 copy-start.10
  142.4 18.4 %all_to_all.31 = bf16[16,5,24,128]{3,2,1,0:T(8,128)(2,1)S(1)} all-to-all(bf16[16,5,24,128]{3,2,1,0:T(8,128)(2,1)S(1)} %broadcast_in_dim.51), channel_id=1, replica_groups=mesh['zh'=2,'yh'=4,'yl'=2,'c'=2,'zlh'=2,'zll'=2,'x'=4] {'x','zlh','zll'}, dimensions={0} | all-to-all | bytes 983040 | tf_op jit(solution)/shard_map/all_to_all | solution.py:342
  160.7 0.1 convert_reduce_fusion
  160.9 0.1 multiply_multiply_fusion
  161.0 0.0 copy-done.7
  161.0 0.0 copy-done.8
  161.0 0.0 copy-done.9
  161.0 0.0 copy-done.10
  161.0 1.1 multiply_add_fusion
  (17 shorter events, 0.3 us)
Async XLA Ops:
  0.6 16.7 %copy-start.11 = (bf16[2,37,768]{2,0,1:T(2,128)(2,1)S(1)}, bf16[2,37,768]{2,0,1:T(2,128)(2,1)}, u32[]{:S(2)}) copy-start(bf16[2,37,768]{2,0,1:T(2,128)(2,1)} %param.10) | copy-start | bytes 340996
  0.7 16.9 %copy-start.12 = (bf16[2,37,768]{2,0,1:T(2,128)(2,1)S(1)}, bf16[2,37,768]{2,0,1:T(2,128)(2,1)}, u32[]{:S(2)}) copy-start(bf16[2,37,768]{2,0,1:T(2,128)(2,1)} %param.13) | copy-start | bytes 340996
  0.7 17.2 %copy-start = (bf16[1,257,768]{2,1,0:T(8,128)(2,1)S(1)}, bf16[1,257,768]{2,1,0:T(8,128)(2,1)}, u32[]{:S(2)}) copy-start(bf16[1,257,768]{2,1,0:T(8,128)(2,1)} %param.9) | copy-start | bytes 1184260
  0.7 17.2 %copy-start.4 = (bf16[1,257,768]{2,1,0:T(8,128)(2,1)S(1)}, bf16[1,257,768]{2,1,0:T(8,128)(2,1)}, u32[]{:S(2)}) copy-start(bf16[1,257,768]{2,1,0:T(8,128)(2,1)} %param.12) | copy-start | bytes 1184260
  2.7 30.2 %all-to-all-start = ((bf16[8,2,5,24,128]{4,3,2,1,0:T(8,128)(2,1)}), bf16[8,2,5,24,128]{4,3,2,1,0:T(8,128)(2,1)S(1)}, u32[]{:S(2)}, u32[]{:S(2)}) async-start(bf16[8,2,5,24,128]{4,3,2,1,0:T(8,128)(2,1)} %shard_map.160), calls=%async_computation | async-start | bytes 983040 | tf_op jit(solution)/shard_map/all_to_all | solution.py:347
  17.5 2.5 %copy-start.2 = (bf16[74,768]{1,0:T(8,128)(2,1)}, bf16[74,768]{1,0:T(8,128)(2,1)S(1)}, u32[]{:S(2)}) copy-start(bf16[74,768]{1,0:T(8,128)(2,1)S(1)} %reshape.275.xl_ref) | copy-start | bytes 340996
  62.3 9.1 %collective-permute-start = (bf16[8,864,128]{2,1,0:T(8,128)(2,1)S(1)}, bf16[8,864,128]{2,1,0:T(8,128)(2,1)S(1)}, u32[]{:S(2)}, u32[]{:S(2)}) collective-permute-start(bf16[8,864,128]{2,1,0:T(8,128)(2,1)S(1)} %all_to_all.30.wo_ref), channel_id=1, source_target_pairs={{0,16},{16,0},{1,17},{17,1},{2,18},{18,2},{3,19},{19,3},{4,20},{20... | collective-permute-start | bytes 5308424 | tf_op jit(solution)/shard_map/ppermute | solution.py:355
  65.7 28.7 %all-to-all-start.4 = ((bf16[8,864,128]{2,1,0:T(8,128)(2,1)}), bf16[8,864,128]{2,1,0:T(8,128)(2,1)}, u32[]{:S(2)}, u32[]{:S(2)}) async-start(bf16[8,864,128]{2,1,0:T(8,128)(2,1)} %broadcast_in_dim.48), calls=%async_computation.4 | async-start | bytes 3538944 | tf_op jit(solution)/shard_map/all_to_all | solution.py:342
  83.7 5.6 %collective-permute-start.1 = (bf16[8,864,128]{2,1,0:T(8,128)(2,1)S(1)}, bf16[8,864,128]{2,1,0:T(8,128)(2,1)S(1)}, u32[]{:S(2)}, u32[]{:S(2)}) collective-permute-start(bf16[8,864,128]{2,1,0:T(8,128)(2,1)S(1)} %get-tuple-element.27), channel_id=1, source_target_pairs={{0,16},{16,0},{1,17},{17,1},{2,18},{18,2},{3,19},{19,3},{4,20},{20... | collective-permute-start | bytes 5308424 | tf_op jit(solution)/shard_map/ppermute | solution.py:355
  94.4 27.1 %all-to-all-start.2 = ((bf16[8,864,128]{2,1,0:T(8,128)(2,1)}), bf16[8,864,128]{2,1,0:T(8,128)(2,1)}, u32[]{:S(2)}, u32[]{:S(2)}) async-start(bf16[8,864,128]{2,1,0:T(8,128)(2,1)} %add_convert_fusion), calls=%async_computation.2 | async-start | bytes 3538944 | tf_op jit(solution)/shard_map/all_to_all | solution.py:342
  99.2 30.2 %collective-permute-start.2 = (bf16[8,864,128]{2,1,0:T(8,128)(2,1)}, bf16[8,864,128]{2,1,0:T(8,128)(2,1)}, u32[]{:S(2)}, u32[]{:S(2)}) collective-permute-start(bf16[8,864,128]{2,1,0:T(8,128)(2,1)} %all-to-all-done.4.wo_ref), channel_id=1, source_target_pairs={{0,16},{16,0},{1,17},{17,1},{2,18},{18,2},{3,19},{19,3},{4,20},{20... | collective-permute-start | bytes 5308424 | tf_op jit(solution)/shard_map/ppermute | solution.py:355
  102.9 1.0 copy-start.1
  103.9 0.9 copy-start.3
  109.7 0.7 copy-start.5
  121.5 7.8 %copy-start.6 = (bf16[1,257,768]{2,1,0:T(8,128)(2,1)S(1)}, bf16[1,257,768]{2,1,0:T(8,128)(2,1)}, u32[]{:S(2)}) copy-start(bf16[1,257,768]{2,1,0:T(8,128)(2,1)} %param.11) | copy-start | bytes 1184260
  124.1 18.1 %all-to-all-start.3 = ((bf16[8,5,24,128]{3,2,1,0:T(8,128)(2,1)}), bf16[8,5,24,128]{3,2,1,0:T(8,128)(2,1)S(1)}, u32[]{:S(2)}, u32[]{:S(2)}) async-start(bf16[8,5,24,128]{3,2,1,0:T(8,128)(2,1)} %copy.31), calls=%async_computation.3 | async-start | bytes 491520 | tf_op jit(solution)/shard_map/all_to_all | solution.py:347
  142.3 18.7 %copy-start.7 = (f32[24,2304]{1,0:T(8,128)S(1)}, f32[24,2304]{1,0:T(8,128)}, u32[]{:S(2)}) copy-start(f32[24,2304]{1,0:T(8,128)} %sw_ref.1) | copy-start | bytes 663556
  142.4 18.7 %copy-start.8 = (f32[24,2304]{1,0:T(8,128)S(1)}, f32[24,2304]{1,0:T(8,128)}, u32[]{:S(2)}) copy-start(f32[24,2304]{1,0:T(8,128)} %tw_ref.1) | copy-start | bytes 663556
  142.4 18.7 %copy-start.9 = (f32[24,2304]{1,0:T(8,128)S(1)}, f32[24,2304]{1,0:T(8,128)}, u32[]{:S(2)}) copy-start(f32[24,2304]{1,0:T(8,128)} %param.16) | copy-start | bytes 663556
  142.4 18.7 %copy-start.10 = (f32[24,2304]{1,0:T(8,128)S(1)}, f32[24,2304]{1,0:T(8,128)}, u32[]{:S(2)}) copy-start(f32[24,2304]{1,0:T(8,128)} %param.17) | copy-start | bytes 663556
